TPU v7x, 32 devices: a whole 2x2x4 slice. The times are simulated.
32 devices in a mesh: seq: 4 (over z), head: 2 (over core), batch: 4 (over y, x).
Axes of the slice: x: 2, y: 2, z: 4, core: 2. Of those that a mesh axis runs over, the one named last changes fastest.
Arguments:
- tokens: bfloat16 [4, 2048, 1024], P('batch', 'seq'), may hold values from -6 to 6
- seg_ids: int32 [4, 2048], P('batch'), may hold values from 0 to 66, as said below
- mixer_gain: float32 [1024], replicated, may hold values from 0.5 to 1.5
- mamba_gate: bfloat16 [1024, 1536], P(None, 'head'), may hold values from -0.1875 to 0.1875
- mamba_input: bfloat16 [1024, 1536], P(None, 'head'), may hold values from -0.1875 to 0.1875
- mamba_maps: bfloat16 [1024, 256], replicated, may hold values from -0.1875 to 0.1875
- mamba_step: bfloat16 [1024, 24], P(None, 'head'), may hold values from -0.1875 to 0.1875
- conv_inner: float32 [4, 1536], P(None, 'head'), may hold values from -3 to 3
- conv_maps: float32 [4, 256], replicated, may hold values from -3 to 3
- log_rate: float32 [24], P('head'), may hold values from -11 to -1
- step_bias: float32 [24], P('head'), may hold values from -3 to 1
- skip_gain: float32 [24], P('head'), may hold values from 0.5 to 1.5
- mamba_gain: float32 [1536], P('head'), may hold values from 0.5 to 1.5
- mamba_output: bfloat16 [1024, 1536], P(None, 'head'), may hold values from -0.15625 to 0.15625
- query_weight: bfloat16 [1024, 512], P(None, 'head'), may hold values from -0.4375 to 0.4375
- memory_weight: bfloat16 [1024, 256], P(None, 'head'), may hold values from -0.1875 to 0.1875
- attention_out: bfloat16 [1024, 512], P(None, 'head'), may hold values from -1.5 to 1.5
- feed_gain: float32 [1024], replicated, may hold values from 0.5 to 1.5
- gate_weight: bfloat16 [1024, 2048], P(None, 'head'), may hold values from -0.1875 to 0.1875
- lift_weight: bfloat16 [1024, 2048], P(None, 'head'), may hold values from -0.1875 to 0.1875
- down_weight: bfloat16 [1024, 2048], P(None, 'head'), may hold values from -0.125 to 0.125
- cotangent: bfloat16 [4, 2048, 1024], P('batch', 'seq'), may hold values from -6 to 6
Outputs:
- layer_out: bfloat16 [4, 2048, 1024], P('batch', 'seq')
- grad_tokens: float32 [4, 2048, 1024], P('batch', 'seq')
- grad_mixer_gain: float32 [1024], P('seq')
- grad_mamba_gate: float32 [1024, 1536], P('seq', 'head')
- grad_mamba_input: float32 [1024, 1536], P('seq', 'head')
- grad_mamba_maps: float32 [1024, 256], P('seq')
- grad_mamba_step: float32 [1024, 24], P('seq', 'head')
- grad_conv_inner: float32 [4, 1536], P(None, 'head')
- grad_conv_maps: float32 [4, 256], replicated
- grad_log_rate: float32 [24], P('head')
- grad_step_bias: float32 [24], P('head')
- grad_skip_gain: float32 [24], P('head')
- grad_mamba_gain: float32 [1536], P('head')
- grad_mamba_output: float32 [1024, 1536], P('seq', 'head')
- grad_query_weight: float32 [1024, 512], P('seq', 'head')
- grad_memory_weight: float32 [1024, 256], P('seq', 'head')
- grad_attention_out: float32 [1024, 512], P('seq', 'head')
- grad_feed_gain: float32 [1024], P('seq')
- grad_gate_weight: float32 [1024, 2048], P('seq', 'head')
- grad_lift_weight: float32 [1024, 2048], P('seq', 'head')
- grad_down_weight: float32 [1024, 2048], P('seq', 'head')
Inputs may be any that keep to these rules, and one draw needn't show every extreme that they name: In each sequence seg_ids begin at 0, never fall and rise by at most one from a position to the next; one document begins within the first 512 positions and ends within the last 512; every sequence holds exactly 3 + 2 * max(1, 32) documents.
All inputs are finite; a program needn't handle non-finite values.
Results may differ from a plain program's by a relative error of at most 0.024.
Values may be sent and summed in bfloat16 or wider, within the bound.
A program may use at most 192 MiB of HBM per device.

v0:
```python
import jax
import jax.numpy as jnp
from jax import lax
from jax.sharding import PartitionSpec as P

HD = 64


eps_norm = 1e-05
rope_base = 10000.0
neg_large = -1e30
highest = lax.Precision.HIGHEST


def shifted(value, axis, steps):
    count = lax.axis_size(axis)
    first, last = (max(0, -steps), min(count, count - steps))
    return lax.ppermute(value, axis, [(source, source + steps) for source in range(first, last)])


def entering(shard, axis, combine, identity):
    count, mine = (lax.axis_size(axis), lax.axis_index(axis))
    everything = jax.tree.map(
        lambda part, kind: lax.all_gather(part.astype(kind), axis),
        shard,
        (jnp.bfloat16, jnp.bfloat16),
    )
    start = jax.tree.map(
        lambda part, zero: jnp.broadcast_to(jnp.asarray(zero, part.dtype), part.shape),
        shard,
        identity,
    )

    def lap(k, before):
        reached = k < mine
        new = combine(
            before, jax.tree.map(lambda part, own: part[k].astype(own.dtype), everything, shard)
        )
        return jax.tree.map(lambda a, b: jnp.where(reached, a, b), new, before)

    return lax.fori_loop(0, count, lap, start)


def carried_in(shard, axis, join, neutral):
    count = lax.axis_size(axis)
    place = lax.axis_index(axis)
    ahead = count - 1 - place
    gathered = jax.tree.map(
        lambda a, kind: lax.all_gather(a.astype(kind), axis),
        shard,
        jax.tree.map(lambda a: jnp.bfloat16 if a.dtype == jnp.float32 else a.dtype, shard),
    )
    state = jax.tree.map(lambda a, e: jnp.zeros_like(a) + jnp.asarray(e, a.dtype), shard, neutral)

    def one(lap, state):
        source = count - 1 - lap
        return join(
            state,
            jax.tree.map(
                lambda a, own: lax.dynamic_index_in_dim(a, source, 0, False).astype(own.dtype),
                gathered,
                shard,
            ),
        )

    return lax.fori_loop(0, ahead, one, state)


def matmul(former, latter):
    return jnp.dot(former, latter, preferred_element_type=jnp.float32)


def matmul_last(former, latter):
    return lax.dot_general(
        former, latter, (((1,), (1,)), ((), ())), preferred_element_type=jnp.float32
    )


def matmul_first(former, latter):
    return lax.dot_general(
        former, latter, (((0,), (0,)), ((), ())), preferred_element_type=jnp.float32
    )


def rms_scale(hidden, gain):
    inverse = lax.rsqrt(jnp.mean(hidden * hidden, axis=-1, keepdims=True) + eps_norm)
    return hidden * inverse * gain


def rotate(values, position, factor):
    half_dim = values.shape[-1] // 2
    inverse_freq = rope_base ** (-jnp.arange(half_dim, dtype=jnp.float32) / half_dim)
    angles = position.astype(jnp.float32)[:, None] * inverse_freq[None, :]
    cosine = jnp.cos(angles)[:, None, :]
    sine_part = factor * jnp.sin(angles)[:, None, :]
    former = values[..., :half_dim]
    latter = values[..., half_dim:]
    return jnp.concatenate(
        [former * cosine - latter * sine_part, latter * cosine + former * sine_part], axis=-1
    )


def conv_mix(extended, kernel, window_seg):
    tap_count = kernel.shape[0]
    row_count = extended.shape[0] - tap_count + 1
    own_seg = window_seg[tap_count - 1 :]
    summed = jnp.zeros((row_count, extended.shape[1]), extended.dtype)
    for tap_index in range(tap_count):
        same_doc = (window_seg[tap_index : tap_index + row_count] == own_seg).astype(extended.dtype)
        summed = (
            summed
            + kernel[tap_index][None, :]
            * extended[tap_index : tap_index + row_count]
            * same_doc[:, None]
        )
    return jax.nn.silu(summed)


def state_part(scan_input, input_map, step_size, log_rate, local_seg, prev_seg):
    cumulative = jnp.cumsum(-jnp.exp(log_rate)[None, :] * step_size, axis=0)
    final_log = cumulative[-1]
    in_tail = local_seg == local_seg[-1]
    spread = jnp.where(in_tail[:, None], final_log[None, :] - cumulative, 0.0)
    weights = jnp.exp(spread) * in_tail[:, None].astype(step_size.dtype) * step_size
    local_state = jnp.einsum("sh,sn,shp->hnp", weights, input_map, scan_input, precision=highest)
    unbroken = (local_seg[-1] == prev_seg).astype(step_size.dtype)
    return (local_state, jnp.exp(final_log) * unbroken)


def output_part(
    scan_input, input_map, output_map, step_size, log_rate, skip_gain, state_in, local_seg, prev_seg
):
    cumulative = jnp.cumsum(-jnp.exp(log_rate)[None, :] * step_size, axis=0)
    row_index = jnp.arange(local_seg.shape[0])
    causal = (row_index[:, None] >= row_index[None, :]) & (local_seg[:, None] == local_seg[None, :])
    gaps = jnp.where(causal[:, :, None], cumulative[:, None, :] - cumulative[None, :, :], 0.0)
    decays = jnp.exp(gaps) * causal[:, :, None].astype(step_size.dtype)
    intersection = jnp.dot(output_map, input_map.T, precision=highest)
    mixing = intersection[:, :, None] * decays * step_size[None, :, :]
    inside = jnp.einsum("tsh,shp->thp", mixing, scan_input, precision=highest)
    carried = (local_seg == prev_seg).astype(step_size.dtype)[:, None] * jnp.exp(cumulative)
    across = (
        jnp.einsum("tn,hnp->thp", output_map, state_in, precision=highest) * carried[:, :, None]
    )
    return inside + across + skip_gain[None, :, None] * scan_input


def link_states(earlier, latter):
    return (earlier[0] * latter[0], latter[0][:, None, None] * earlier[1] + latter[1])


def head_total(partial_sum):
    return lax.psum(partial_sum.astype(jnp.bfloat16), "head").astype(jnp.float32)


def group_total(partial_sum):
    return lax.psum(partial_sum, "head")


def fold_rows(gradient, seq_count):
    return gradient.reshape((seq_count, gradient.shape[0] // seq_count) + gradient.shape[1:])


def score_block(queries, key_rows, key_start, position, local_seg, segments):
    span_rows = key_rows.shape[0]
    key_pos = key_start + jnp.arange(span_rows, dtype=jnp.int32)
    key_seg = lax.dynamic_slice_in_dim(segments, key_start, span_rows)
    allowed = (key_pos[None, :] <= position[:, None]) & (key_seg[None, :] == local_seg[:, None])
    scores = jnp.einsum(
        "kgrd,nkd->kgrn", queries, key_rows, preferred_element_type=jnp.float32
    ) * queries.shape[-1] ** (-0.5)
    return (jnp.where(allowed, scores, neg_large), allowed)


def body(
    tokens,
    seg_ids,
    mixer_gain,
    mamba_gate,
    mamba_input,
    mamba_maps,
    mamba_step,
    conv_inner,
    conv_maps,
    log_rate,
    step_bias,
    skip_gain,
    mamba_gain,
    mamba_output,
    query_weight,
    memory_weight,
    attention_out,
    feed_gain,
    gate_weight,
    lift_weight,
    down_weight,
    cotangent,
):
    row_count = tokens.shape[1]
    tap_count = conv_inner.shape[0]
    head_count = log_rate.shape[0]
    inner_width = conv_inner.shape[1]
    head_size = inner_width // head_count
    state_width = conv_maps.shape[1] // 2
    query_heads = query_weight.shape[1] // HD
    memory_heads = memory_weight.shape[1] // (2 * HD)
    group_size = query_heads // memory_heads
    all_width = inner_width * lax.axis_size("head")
    hidden = tokens[0].astype(jnp.float32)
    segments = seg_ids[0]
    offset = lax.axis_index("seq") * row_count
    last_row = offset + row_count - 1
    padded_seg = jnp.concatenate([jnp.full((tap_count - 1,), -1, jnp.int32), segments])
    window_seg = lax.dynamic_slice_in_dim(padded_seg, offset, row_count + tap_count - 1)
    local_seg = window_seg[tap_count - 1 :]
    prev_seg = window_seg[tap_count - 2]
    position = offset + jnp.arange(row_count, dtype=jnp.int32)
    normed, norm1_back = jax.vjp(rms_scale, hidden, mixer_gain)
    normed_low = normed.astype(jnp.bfloat16)
    gate_z = matmul(normed_low, mamba_gate)
    inner_x = matmul(normed_low, mamba_input)
    maps = matmul(normed_low, mamba_maps)
    raw_step = matmul(normed_low, mamba_step)
    query = matmul(normed_low, query_weight)
    memory = matmul(normed_low, memory_weight)
    before = jnp.concatenate([inner_x, maps], axis=1)
    edge_rows = shifted(before[row_count - tap_count + 1 :], "seq", 1)
    extended = jnp.concatenate([edge_rows, before], axis=0)
    kernel = jnp.concatenate([conv_inner, conv_maps], axis=1)

    def conv_apply(extended_rows, kernel_taps):
        return conv_mix(extended_rows, kernel_taps, window_seg)

    activated, conv_back = jax.vjp(conv_apply, extended, kernel)
    scan_input = activated[:, :inner_width].reshape(row_count, head_count, head_size)
    input_map = activated[:, inner_width : inner_width + state_width]
    output_map = activated[:, inner_width + state_width :]

    def step_apply(raw_rows, bias_now):
        return jax.nn.softplus(raw_rows + bias_now)

    step_size, step_back = jax.vjp(step_apply, raw_step, step_bias)

    def state_apply(input_now, in_map_now, step_now, rate_now):
        return state_part(input_now, in_map_now, step_now, rate_now, local_seg, prev_seg)

    (local_state, decays), state_back = jax.vjp(
        state_apply, scan_input, input_map, step_size, log_rate
    )
    identity = (jnp.ones_like(decays), jnp.zeros_like(local_state))
    prefix = entering((decays, local_state), "seq", link_states, identity)
    state_in = prefix[1]

    def output_apply(input_now, in_map_now, out_map_now, step_now, rate_now, skip_now, state_now):
        return output_part(
            input_now,
            in_map_now,
            out_map_now,
            step_now,
            rate_now,
            skip_now,
            state_now,
            local_seg,
            prev_seg,
        )

    mamba_y, output_back = jax.vjp(
        output_apply, scan_input, input_map, output_map, step_size, log_rate, skip_gain, state_in
    )
    gate_silu, silu_back = jax.vjp(jax.nn.silu, gate_z)
    flat_y = mamba_y.reshape(row_count, inner_width)
    g_six = flat_y * gate_silu
    square_total = group_total(jnp.sum(g_six * g_six, axis=1))
    inverse_six = lax.rsqrt(square_total / all_width + eps_norm)[:, None]
    gated = g_six * inverse_six * mamba_gain
    gated_low = gated.astype(jnp.bfloat16)
    mamba_out = matmul_last(gated_low, mamba_output)
    query_rot = rotate(query.reshape(row_count, query_heads, HD), position, 1.0)
    queries = (
        query_rot.astype(jnp.bfloat16)
        .reshape(row_count, memory_heads, group_size, HD)
        .transpose(1, 2, 0, 3)
    )
    memory_split = memory.reshape(row_count, memory_heads, 2, HD)
    key_low = rotate(memory_split[:, :, 0], position, 1.0).astype(jnp.bfloat16)
    value_low = memory_split[:, :, 1].astype(jnp.bfloat16)
    all_keys, all_values = (
        lax.all_gather(key_low, "seq", axis=0, tiled=True),
        lax.all_gather(value_low, "seq", axis=0, tiled=True),
    )
    total_rows = all_keys.shape[0]
    block_rows = min(512, total_rows)
    block_count = total_rows // block_rows
    key_blocks = all_keys.reshape((block_count, block_rows) + all_keys.shape[1:])
    value_blocks = all_values.reshape((block_count, block_rows) + all_values.shape[1:])
    block_starts = jnp.arange(block_count, dtype=jnp.int32) * block_rows

    def fold_step(running, pieces):
        key_rows, value_rows, key_start = pieces

        def live_fold(carried):
            running_max, running_sum, running_acc = carried
            scores, allowed = score_block(
                queries, key_rows, key_start, position, local_seg, segments
            )
            new_max = jnp.maximum(running_max, jnp.max(scores, axis=-1))
            weights = jnp.where(allowed, jnp.exp(scores - new_max[..., None]), 0.0)
            factor = jnp.exp(running_max - new_max)
            new_sum = running_sum * factor + jnp.sum(weights, axis=-1)
            new_acc = running_acc * factor[..., None] + jnp.einsum(
                "kgrn,nkd->kgrd",
                weights.astype(jnp.bfloat16),
                value_rows,
                preferred_element_type=jnp.float32,
            )
            return (new_max, new_sum, new_acc)

        def keep_fold(carried):
            return carried

        return (lax.cond(key_start <= last_row, live_fold, keep_fold, running), None)

    start_state = (
        jnp.full(queries.shape[:3], neg_large, jnp.float32),
        jnp.zeros(queries.shape[:3], jnp.float32),
        jnp.zeros(queries.shape, jnp.float32),
    )
    (final_max, final_sum, numer), _ = lax.scan(
        fold_step, start_state, (key_blocks, value_blocks, block_starts)
    )
    attention = numer / final_sum[..., None]
    attention_low = (
        attention.transpose(2, 0, 1, 3).reshape(row_count, query_heads * HD).astype(jnp.bfloat16)
    )
    attention_part = matmul_last(attention_low, attention_out)
    second = hidden + head_total(mamba_out + attention_part)
    normed2, norm2_back = jax.vjp(rms_scale, second, feed_gain)
    normed2_low = normed2.astype(jnp.bfloat16)
    gate_value = matmul(normed2_low, gate_weight)
    lift_value = matmul(normed2_low, lift_weight)

    def active_apply(gate_now, lift_now):
        return jax.nn.silu(gate_now) * lift_now

    active, active_back = jax.vjp(active_apply, gate_value, lift_value)
    active_low = active.astype(jnp.bfloat16)
    layer_out = (second + head_total(matmul_last(active_low, down_weight))).astype(jnp.bfloat16)
    grad_out = cotangent[0]
    d_active = matmul(grad_out, down_weight)
    g_down = matmul_first(grad_out, active_low)
    d_gate_f, d_lift_f = active_back(d_active)
    d_gate_low = d_gate_f.astype(jnp.bfloat16)
    d_lift_low = d_lift_f.astype(jnp.bfloat16)
    g_gate = matmul_first(normed2_low, d_gate_low)
    g_lift = matmul_first(normed2_low, d_lift_low)
    d_normed2 = head_total(
        matmul_last(d_gate_low, gate_weight) + matmul_last(d_lift_low, lift_weight)
    )
    d_second_norm, g_feed_gain = norm2_back(d_normed2)
    d_second = grad_out.astype(jnp.float32) + d_second_norm
    d_mix = d_second.astype(jnp.bfloat16)
    g_attn_out = matmul_first(d_mix, attention_low)
    g_mamba_out = matmul_first(d_mix, gated_low)
    d_attention = (
        matmul(d_mix, attention_out)
        .reshape(row_count, memory_heads, group_size, HD)
        .transpose(1, 2, 0, 3)
    )
    d_gated = matmul(d_mix, mamba_output)
    delta = jnp.sum(d_attention * attention, axis=-1)
    num_grad = (d_attention / final_sum[..., None]).astype(jnp.bfloat16)
    scale_now = HD ** (-0.5)

    def back_step(query_grad, pieces):
        key_rows, value_rows, key_start = pieces

        def live_back(grad_now):
            scores, allowed = score_block(
                queries, key_rows, key_start, position, local_seg, segments
            )
            weights = jnp.where(allowed, jnp.exp(scores - final_max[..., None]), 0.0)
            value_inner = jnp.einsum(
                "kgrd,nkd->kgrn", num_grad, value_rows, preferred_element_type=jnp.float32
            )
            score_grad = (weights * (value_inner - (delta / final_sum)[..., None])).astype(
                jnp.bfloat16
            )
            grad_next = (
                grad_now
                + jnp.einsum(
                    "kgrn,nkd->kgrd", score_grad, key_rows, preferred_element_type=jnp.float32
                )
                * scale_now
            )
            key_grad = (
                jnp.einsum(
                    "kgrn,kgrd->nkd", score_grad, queries, preferred_element_type=jnp.float32
                )
                * scale_now
            )
            value_grad = jnp.einsum(
                "kgrn,kgrd->nkd",
                weights.astype(jnp.bfloat16),
                num_grad,
                preferred_element_type=jnp.float32,
            )
            return (grad_next, jnp.stack([key_grad, value_grad], axis=2))

        def skip_back(grad_now):
            return (grad_now, jnp.zeros((key_rows.shape[0], memory_heads, 2, HD), jnp.float32))

        return lax.cond(key_start <= last_row, live_back, skip_back, query_grad)

    query_grad, pair_blocks = lax.scan(
        back_step, jnp.zeros(queries.shape, jnp.float32), (key_blocks, value_blocks, block_starts)
    )
    pair_grads = lax.psum_scatter(
        pair_blocks.reshape(total_rows, memory_heads * 2 * HD).astype(jnp.bfloat16),
        "seq",
        scatter_dimension=0,
        tiled=True,
    ).astype(jnp.float32)
    pair_local = pair_grads.reshape(row_count, memory_heads, 2, HD)
    key_back = rotate(pair_local[:, :, 0], position, -1.0)
    d_memory_low = (
        jnp.stack([key_back, pair_local[:, :, 1]], axis=2)
        .reshape(row_count, memory_heads * 2 * HD)
        .astype(jnp.bfloat16)
    )
    query_back = rotate(
        query_grad.transpose(2, 0, 1, 3).reshape(row_count, query_heads, HD), position, -1.0
    )
    d_query_low = query_back.reshape(row_count, query_heads * HD).astype(jnp.bfloat16)
    e_six = d_gated * mamba_gain
    cross_mean = group_total(jnp.sum(e_six * g_six, axis=1))[:, None] / all_width
    d_g_six = inverse_six * e_six - g_six * inverse_six * inverse_six * inverse_six * cross_mean
    d_mamba_y = (d_g_six * gate_silu).reshape(row_count, head_count, head_size)
    d_gate_z = silu_back(d_g_six * flat_y)[0]
    g_mamba_gain = jnp.sum(d_gated * g_six * inverse_six, axis=0)
    d_gate_z_low = d_gate_z.astype(jnp.bfloat16)
    d_input1, d_in_map1, d_out_map, d_step1, d_rate1, g_skip, d_state_in = output_back(d_mamba_y)
    later_grad = carried_in((decays, d_state_in), "seq", link_states, identity)[1]
    d_decays = jnp.sum(state_in * later_grad, axis=(1, 2))
    d_input2, d_in_map2, d_step2, d_rate2 = state_back((later_grad, d_decays))
    map_grads = lax.psum(
        jnp.concatenate([d_in_map1 + d_in_map2, d_out_map], axis=1).astype(jnp.bfloat16), "head"
    ).astype(jnp.float32)
    d_activated = jnp.concatenate(
        [(d_input1 + d_input2).reshape(row_count, inner_width), map_grads], axis=1
    )
    d_extended, g_kernel = conv_back(d_activated)
    back_edge = shifted(d_extended[: tap_count - 1], "seq", -1)
    d_before = d_extended[tap_count - 1 :] + jnp.concatenate(
        [jnp.zeros((row_count - tap_count + 1, d_extended.shape[1]), jnp.float32), back_edge],
        axis=0,
    )
    d_inner_low = d_before[:, :inner_width].astype(jnp.bfloat16)
    d_maps_low = d_before[:, inner_width:].astype(jnp.bfloat16)
    d_raw, g_step_bias = step_back(d_step1 + d_step2)
    d_raw_low = d_raw.astype(jnp.bfloat16)
    g_log_rate = d_rate1 + d_rate2
    d_normed = (
        matmul_last(d_gate_z_low, mamba_gate)
        + matmul_last(d_inner_low, mamba_input)
        + matmul_last(d_maps_low, mamba_maps) / lax.axis_size("head")
        + matmul_last(d_raw_low, mamba_step)
        + matmul_last(d_query_low, query_weight)
        + matmul_last(d_memory_low, memory_weight)
    )
    d_normed = head_total(d_normed)
    d_hidden_norm, g_mixer_gain = norm1_back(d_normed)
    grad_tokens = d_second + d_hidden_norm
    g_gate_z = matmul_first(normed_low, d_gate_z_low)
    g_inner = matmul_first(normed_low, d_inner_low)
    g_maps = matmul_first(normed_low, d_maps_low)
    g_step_weight = matmul_first(normed_low, d_raw_low)
    g_query = matmul_first(normed_low, d_query_low)
    g_memory = matmul_first(normed_low, d_memory_low)
    seq_count = lax.axis_size("seq")
    folded = (
        lax.psum_scatter(
            fold_rows(g_mixer_gain, seq_count).astype(jnp.bfloat16),
            "batch",
            scatter_dimension=1,
            tiled=True,
        ).astype(jnp.float32),
        lax.psum_scatter(
            fold_rows(g_gate_z, seq_count).astype(jnp.bfloat16),
            "batch",
            scatter_dimension=1,
            tiled=True,
        ).astype(jnp.float32),
        lax.psum_scatter(
            fold_rows(g_inner, seq_count).astype(jnp.bfloat16),
            "batch",
            scatter_dimension=1,
            tiled=True,
        ).astype(jnp.float32),
        lax.psum_scatter(
            fold_rows(g_maps, seq_count).astype(jnp.bfloat16),
            "batch",
            scatter_dimension=1,
            tiled=True,
        ).astype(jnp.float32),
        lax.psum_scatter(
            fold_rows(g_step_weight, seq_count).astype(jnp.bfloat16),
            "batch",
            scatter_dimension=1,
            tiled=True,
        ).astype(jnp.float32),
        lax.psum_scatter(
            fold_rows(g_mamba_out, seq_count).astype(jnp.bfloat16),
            "batch",
            scatter_dimension=1,
            tiled=True,
        ).astype(jnp.float32),
        lax.psum_scatter(
            fold_rows(g_query, seq_count).astype(jnp.bfloat16),
            "batch",
            scatter_dimension=1,
            tiled=True,
        ).astype(jnp.float32),
        lax.psum_scatter(
            fold_rows(g_memory, seq_count).astype(jnp.bfloat16),
            "batch",
            scatter_dimension=1,
            tiled=True,
        ).astype(jnp.float32),
        lax.psum_scatter(
            fold_rows(g_attn_out, seq_count).astype(jnp.bfloat16),
            "batch",
            scatter_dimension=1,
            tiled=True,
        ).astype(jnp.float32),
        lax.psum_scatter(
            fold_rows(g_feed_gain, seq_count).astype(jnp.bfloat16),
            "batch",
            scatter_dimension=1,
            tiled=True,
        ).astype(jnp.float32),
        lax.psum_scatter(
            fold_rows(g_gate, seq_count).astype(jnp.bfloat16),
            "batch",
            scatter_dimension=1,
            tiled=True,
        ).astype(jnp.float32),
        lax.psum_scatter(
            fold_rows(g_lift, seq_count).astype(jnp.bfloat16),
            "batch",
            scatter_dimension=1,
            tiled=True,
        ).astype(jnp.float32),
        lax.psum_scatter(
            fold_rows(g_down, seq_count).astype(jnp.bfloat16),
            "batch",
            scatter_dimension=1,
            tiled=True,
        ).astype(jnp.float32),
    )
    summed = (
        lax.psum_scatter(
            folded[0].astype(jnp.bfloat16), "seq", scatter_dimension=0, tiled=True
        ).astype(jnp.float32),
        lax.psum_scatter(
            folded[1].astype(jnp.bfloat16), "seq", scatter_dimension=0, tiled=True
        ).astype(jnp.float32),
        lax.psum_scatter(
            folded[2].astype(jnp.bfloat16), "seq", scatter_dimension=0, tiled=True
        ).astype(jnp.float32),
        lax.psum_scatter(
            folded[3].astype(jnp.bfloat16), "seq", scatter_dimension=0, tiled=True
        ).astype(jnp.float32),
        lax.psum_scatter(
            folded[4].astype(jnp.bfloat16), "seq", scatter_dimension=0, tiled=True
        ).astype(jnp.float32),
        lax.psum_scatter(
            folded[5].astype(jnp.bfloat16), "seq", scatter_dimension=0, tiled=True
        ).astype(jnp.float32),
        lax.psum_scatter(
            folded[6].astype(jnp.bfloat16), "seq", scatter_dimension=0, tiled=True
        ).astype(jnp.float32),
        lax.psum_scatter(
            folded[7].astype(jnp.bfloat16), "seq", scatter_dimension=0, tiled=True
        ).astype(jnp.float32),
        lax.psum_scatter(
            folded[8].astype(jnp.bfloat16), "seq", scatter_dimension=0, tiled=True
        ).astype(jnp.float32),
        lax.psum_scatter(
            folded[9].astype(jnp.bfloat16), "seq", scatter_dimension=0, tiled=True
        ).astype(jnp.float32),
        lax.psum_scatter(
            folded[10].astype(jnp.bfloat16), "seq", scatter_dimension=0, tiled=True
        ).astype(jnp.float32),
        lax.psum_scatter(
            folded[11].astype(jnp.bfloat16), "seq", scatter_dimension=0, tiled=True
        ).astype(jnp.float32),
        lax.psum_scatter(
            folded[12].astype(jnp.bfloat16), "seq", scatter_dimension=0, tiled=True
        ).astype(jnp.float32),
    )
    joined = (
        lax.all_gather(summed[0].astype(jnp.bfloat16), "batch", axis=1, tiled=True).astype(
            jnp.float32
        ),
        lax.all_gather(summed[1].astype(jnp.bfloat16), "batch", axis=1, tiled=True).astype(
            jnp.float32
        ),
        lax.all_gather(summed[2].astype(jnp.bfloat16), "batch", axis=1, tiled=True).astype(
            jnp.float32
        ),
        lax.all_gather(summed[3].astype(jnp.bfloat16), "batch", axis=1, tiled=True).astype(
            jnp.float32
        ),
        lax.all_gather(summed[4].astype(jnp.bfloat16), "batch", axis=1, tiled=True).astype(
            jnp.float32
        ),
        lax.all_gather(summed[5].astype(jnp.bfloat16), "batch", axis=1, tiled=True).astype(
            jnp.float32
        ),
        lax.all_gather(summed[6].astype(jnp.bfloat16), "batch", axis=1, tiled=True).astype(
            jnp.float32
        ),
        lax.all_gather(summed[7].astype(jnp.bfloat16), "batch", axis=1, tiled=True).astype(
            jnp.float32
        ),
        lax.all_gather(summed[8].astype(jnp.bfloat16), "batch", axis=1, tiled=True).astype(
            jnp.float32
        ),
        lax.all_gather(summed[9].astype(jnp.bfloat16), "batch", axis=1, tiled=True).astype(
            jnp.float32
        ),
        lax.all_gather(summed[10].astype(jnp.bfloat16), "batch", axis=1, tiled=True).astype(
            jnp.float32
        ),
        lax.all_gather(summed[11].astype(jnp.bfloat16), "batch", axis=1, tiled=True).astype(
            jnp.float32
        ),
        lax.all_gather(summed[12].astype(jnp.bfloat16), "batch", axis=1, tiled=True).astype(
            jnp.float32
        ),
    )
    shards = tuple((member[0] for member in joined))
    small = lax.psum(
        (
            g_kernel[:, :inner_width],
            g_kernel[:, inner_width:],
            g_log_rate,
            g_step_bias,
            g_skip,
            g_mamba_gain,
        ),
        ("seq", "batch"),
    )
    return (
        layer_out[None],
        grad_tokens[None],
        shards[0],
        shards[1],
        shards[2],
        shards[3],
        shards[4],
        small[0],
        small[1],
        small[2],
        small[3],
        small[4],
        small[5],
        shards[5],
        shards[6],
        shards[7],
        shards[8],
        shards[9],
        shards[10],
        shards[11],
        shards[12],
    )


def solution(mesh):
    return jax.shard_map(
        body,
        mesh=mesh,
        in_specs=(
            P("batch", "seq", None),
            P("batch", None),
            P(),
            P(None, "head"),
            P(None, "head"),
            P(),
            P(None, "head"),
            P(None, "head"),
            P(),
            P("head"),
            P("head"),
            P("head"),
            P("head"),
            P(None, "head"),
            P(None, "head"),
            P(None, "head"),
            P(None, "head"),
            P(),
            P(None, "head"),
            P(None, "head"),
            P(None, "head"),
            P("batch", "seq", None),
        ),
        out_specs=(
            P("batch", "seq", None),
            P("batch", "seq", None),
            P("seq"),
            P("seq", "head"),
            P("seq", "head"),
            P("seq", None),
            P("seq", "head"),
            P(None, "head"),
            P(),
            P("head"),
            P("head"),
            P("head"),
            P("head"),
            P("seq", "head"),
            P("seq", "head"),
            P("seq", "head"),
            P("seq", "head"),
            P("seq"),
            P("seq", "head"),
            P("seq", "head"),
            P("seq", "head"),
        ),
        check_vma=False,
    )
```

profile of v0, /device:TPU:0, one launch (start us, length us, event | category | flops | bytes accessed | tf_op | source)
XLA Modules:
  0.0 1158.1 jit_solution(14734689518548616131)
XLA Ops:
  73.6 17.2 %while.60 = (s32[]{:T(128)}, f32[1,4,512]{2,1,0:T(4,128)S(1)}, f32[1,4,512]{2,1,0:T(4,128)S(1)}, f32[1,4,512,64]{2,3,1,0:T(8,128)}, s32[4]{0:T(128)}, /*index=5*...) while((s32[]{:T(128)}, f32[1,4,512]{2,1,0:T(4,128)S(1)}, ...), condition=%wide.region_12.13_spmd.clone, body=%wide.region_7.12_spmd.clone.sunk | while | flops 283122688 | bytes 15226205 | solution.py:328
  94.2 37.3 %all-gather.3 = bf16[4,1,12]{2,1,0:T(2,128)(2,1)S(1)} all-gather(bf16[1,1,12]{2,1,0:T(2,128)(2,1)S(1)} %bitcast.640), channel_id=1, replica_groups=mesh['seq'=4,'head'=2,'batch'=4] {'seq'}, dimensions={0}, use_global_device_ids=true | all-gather | bytes 120 | tf_op jit(solution)/shard_map/all_gather | solution.py:24
  146.5 16.9 %all-gather = bf16[48,128,64]{1,2,0:T(8,128)(2,1)} all-gather(bf16[12,128,64]{1,2,0:T(8,128)(2,1)S(1)} %fusion.148), channel_id=2, replica_groups=mesh['seq'=4,'head'=2,'batch'=4] {'seq'}, dimensions={0}, use_global_device_ids=true | all-gather | bytes 983040 | tf_op jit(solution)/shard_map/all_gather | solution.py:24
  163.4 22.8 %while.62 = (s32[]{:T(128)}, f32[12,128,64]{2,1,0:T(8,128)}, s32[]{:T(128)}, bf16[4,12]{1,0:T(4,128)(2,1)S(1)}, bf16[4,12,128,64]{2,3,1,0:T(8,128)(2,1)}, /*index=5*/s32[]{:T(128)}, s32[]{:T(128)}) while((s32[]{:T(128)}, f32[12,128,64]{2,1,0:T(8,128)}, s32[]{:T(128)}, bf16[4,12]{1,0:T(4,128)(2,1)S(1)}, ...), condition=%wide.region_4.5_spmd.clone, body=%wide.region_3.4_spmd.clone.sunk | while | flops 491536 | bytes 1769697 | solution.py:41
  191.0 17.5 %fusion.117 = f32[512,12,64]{0,2,1:T(8,128)} fusion(f32[512,12,64]{0,2,1:T(8,128)S(1)} %bitcast.551, f32[512,12,64]{0,2,1:T(8,128)S(1)} %bitcast.567, f32[512,12]{0,1:T(8,128)S(1)} %copy-done.88, f32[512,512]{1,0:T(8,128)} %get-tuple-element.993, f32[512,12]{0,1:T(8,128)S(1)} %bitcast.596, f32[512,512]{1,0:T(8,128)} %fusion.183, ...), kind=kOutput, calls=%fused_computation.178 | convolution fusion | flops 2433220608 | bytes 7151664 | tf_op jit(solution)/shard_map/jvp(tsh,shp->thp)/dot_general | solution.py:140
  258.4 17.4 %all-reduce.26.cloned.1.call-done = bf16[512,1024]{1,0:T(8,128)(2,1)} async-done(((bf16[512,1024]{1,0:T(8,128)(2,1)}), bf16[512,1024]{1,0:T(8,128)(2,1)}) %all-reduce.26.cloned.1.call-update) | async-done | bytes 1048592 | tf_op jit(solution)/shard_map/psum | solution.py:153
  298.2 20.2 %all-gather.2 = bf16[48,128,64]{1,2,0:T(8,128)(2,1)} all-gather(bf16[12,128,64]{1,2,0:T(8,128)(2,1)S(1)} %fusion.145), channel_id=4, replica_groups=mesh['seq'=4,'head'=2,'batch'=4] {'seq'}, dimensions={0}, use_global_device_ids=true | all-gather | bytes 983040 | tf_op jit(solution)/shard_map/all_gather | solution.py:49
  340.1 20.8 %fusion.70 = (f32[512,12]{0,1:T(8,128)}, f32[512,12]{0,1:T(8,128)}, f32[512,12]{0,1:T(8,128)}, f32[512,512]{1,0:T(8,128)S(1)}) fusion(f32[512,12]{0,1:T(8,128)S(1)} %copy-done.89, f32[512,512]{1,0:T(8,128)S(1)} %copy-done.42, f32[512,12]{0,1:T(8,128)S(1)} %bitcast.597, f32[512,512]{1,0:T(8,128)S(1)} %copy-done.45, pred[512,512]{1,0:T(8,128)(4,1)S(1)} %copy-done.62, ...), kind=kOutput, calls=%fused_computation.87 | convolution fusion | flops 2462824448 | bytes 6676480 | tf_op jit(solution)/shard_map/transpose(jvp(tsh,shp->thp))/dot_general | solution.py:140
  400.8 19.9 %while.61 = (s32[]{:T(128)}, f32[1,4,512,64]{2,3,1,0:T(8,128)S(1)}, bf16[4,512,1,2,64]{1,4,3,2,0:T(8,128)(2,1)}, s32[4]{0:T(128)}, s32[]{:T(128)}, /*index=5*/s3...) while((s32[]{:T(128)}, f32[1,4,512,64]{2,3,1,0:T(8,128)S(1)}, ...), condition=%wide.region_38.39_spmd.clone, body=%wide.region_35.38_spmd.clone.sunk | while | flops 684854272 | bytes 22680932 | solution.py:414
  448.5 24.3 %reduce-scatter.32.cloned.1.call-done = bf16[512,128]{0,1:T(8,128)(2,1)} async-done(((bf16[2048,128]{0,1:T(8,128)(2,1)}), bf16[512,128]{0,1:T(8,128)(2,1)}) %reduce-scatter.32.cloned.1.call-update) | async-done | bytes 131088 | tf_op jit(solution)/shard_map/reduce_scatter | solution.py:417
  533.4 22.6 %reduce-scatter.78.cloned.1.call-done = bf16[64,48]{1,0:T(8,128)(2,1)} async-done(((bf16[256,48]{1,0:T(8,128)(2,1)}), bf16[64,48]{1,0:T(8,128)(2,1)}) %reduce-scatter.78.cloned.1.call-update) | async-done | bytes 6160
  557.6 25.9 %reduce-scatter.56.cloned.1.call-done = bf16[4,64,128]{2,1,0:T(8,128)(2,1)} async-done(((bf16[4,256,128]{2,1,0:T(8,128)(2,1)}), bf16[4,64,128]{2,1,0:T(8,128)(2,1)}) %reduce-scatter.56.cloned.1.call-update) | async-done | bytes 65552 | tf_op jit(solution)/shard_map/reduce_scatter | solution.py:523
  583.5 34.2 %reduce-scatter.48.cloned.1.call-done = bf16[4,64,768]{2,1,0:T(8,128)(2,1)} async-done(((bf16[4,256,768]{2,1,0:T(8,128)(2,1)}), bf16[4,64,768]{2,1,0:T(8,128)(2,1)}) %reduce-scatter.48.cloned.1.call-update) | async-done | bytes 393232 | tf_op jit(solution)/shard_map/reduce_scatter | solution.py:511
  617.8 38.2 %reduce-scatter.68.cloned.1.call-done = bf16[4,64,1024]{2,1,0:T(8,128)(2,1)} async-done(((bf16[4,256,1024]{2,1,0:T(8,128)(2,1)}), bf16[4,64,1024]{2,1,0:T(8,128)(2,1)}) %reduce-scatter.68.cloned.1.call-update) | async-done | bytes 524304 | tf_op jit(solution)/shard_map/reduce_scatter | solution.py:547
  656.1 38.1 %reduce-scatter.64.cloned.1.call-done = bf16[4,64,1024]{2,1,0:T(8,128)(2,1)} async-done(((bf16[4,256,1024]{2,1,0:T(8,128)(2,1)}), bf16[4,64,1024]{2,1,0:T(8,128)(2,1)}) %reduce-scatter.64.cloned.1.call-update) | async-done | bytes 524304 | tf_op jit(solution)/shard_map/reduce_scatter | solution.py:541
  694.2 38.3 %reduce-scatter.72.cloned.1.call-done = bf16[4,64,1024]{2,1,0:T(8,128)(2,1)} async-done(((bf16[4,256,1024]{2,1,0:T(8,128)(2,1)}), bf16[4,64,1024]{2,1,0:T(8,128)(2,1)}) %reduce-scatter.72.cloned.1.call-update) | async-done | bytes 524304 | tf_op jit(solution)/shard_map/reduce_scatter | solution.py:553
  734.8 25.9 %reduce-scatter.52.cloned.1.call-done = bf16[4,64,256]{2,1,0:T(8,128)(2,1)} async-done(((bf16[4,256,256]{2,1,0:T(8,128)(2,1)}), bf16[4,64,256]{2,1,0:T(8,128)(2,1)}) %reduce-scatter.52.cloned.1.call-update) | async-done | bytes 131088 | tf_op jit(solution)/shard_map/reduce_scatter | solution.py:517
  760.7 28.2 %reduce-scatter.42.cloned.1.call-done = bf16[4,64,256]{2,1,0:T(8,128)(2,1)} async-done(((bf16[4,256,256]{2,1,0:T(8,128)(2,1)}), bf16[4,64,256]{2,1,0:T(8,128)(2,1)}) %reduce-scatter.42.cloned.1.call-update) | async-done | bytes 131088 | tf_op jit(solution)/shard_map/reduce_scatter | solution.py:499
  793.5 22.3 %reduce-scatter.80.cloned.1.call-done = bf16[64,4]{1,0:T(8,128)(2,1)} async-done(((bf16[256,4]{1,0:T(8,128)(2,1)}), bf16[64,4]{1,0:T(8,128)(2,1)}) %reduce-scatter.80.cloned.1.call-update) | async-done | bytes 528
  816.7 75.9 %all-reduce.15 = (f32[4,768]{1,0:T(4,128)}, f32[4,256]{1,0:T(4,128)}, f32[12]{0:T(128)}, f32[12]{0:T(128)}, f32[12]{0:T(128)}, /*index=5*/f32[768]{0:T(1024)}) all-reduce(f32[4,768]{1,0:T(4,128)S(1)} %slice.206, f32[4,256]{1,0:T(4,128)S(1)} %pad_add_fusion.3, ...), channel_id=1, replica_groups=mesh['seq'=4,'head'=2,'batch'=4] {'seq','batch'}, use_global_device_ids=true, to_apply=%region_57.58 | all-reduce | flops 4900 | bytes 39200 | tf_op jit(solution)/shard_map/psum | solution.py:643
  1004.5 18.5 %reduce-scatter.38.cloned.1.call-done = bf16[4,64,768]{2,1,0:T(8,128)(2,1)} async-done(((bf16[4,256,768]{2,1,0:T(8,128)(2,1)}), bf16[4,64,768]{2,1,0:T(8,128)(2,1)}) %reduce-scatter.38.cloned.1.call-update) | async-done | bytes 393232 | tf_op jit(solution)/shard_map/reduce_scatter | solution.py:493
  1026.4 18.1 %reduce-scatter.54.cloned.1.call-done = bf16[1,64,256]{2,1,0:T(8,128)(2,1)} async-done(((bf16[4,64,256]{2,1,0:T(8,128)(2,1)}), bf16[1,64,256]{2,1,0:T(8,128)(2,1)}) %reduce-scatter.54.cloned.1.call-update) | async-done | bytes 32784 | tf_op jit(solution)/shard_map/reduce_scatter | solution.py:579
  1072.6 23.4 %reduce-scatter.34.cloned.1.call-done = bf16[4,64,768]{2,1,0:T(8,128)(2,1)} async-done(((bf16[4,256,768]{2,1,0:T(8,128)(2,1)}), bf16[4,64,768]{2,1,0:T(8,128)(2,1)}) %reduce-scatter.34.cloned.1.call-update) | async-done | bytes 393232 | tf_op jit(solution)/shard_map/reduce_scatter | solution.py:487
  1097.4 21.4 %reduce-scatter.40.cloned.1.call-done = bf16[1,64,768]{2,1,0:T(8,128)(2,1)} async-done(((bf16[4,64,768]{2,1,0:T(8,128)(2,1)}), bf16[1,64,768]{2,1,0:T(8,128)(2,1)}) %reduce-scatter.40.cloned.1.call-update) | async-done | bytes 98320 | tf_op jit(solution)/shard_map/reduce_scatter | solution.py:567
  (670 shorter events, 568.8 us)
Async XLA Ops:
  7.2 234.4 %all-reduce.24.cloned.1.call-start = ((), (), s32[]{:S(2)}) async-start(), calls=%async_computation.25 | async-start | bytes 2097152 | tf_op jit(solution)/shard_map/psum | solution.py:153
  13.7 118.4 %collective-permute-start = (f32[3,1024]{1,0:T(4,128)}, f32[3,1024]{1,0:T(4,128)}, u32[]{:S(2)}, u32[]{:S(2)}) collective-permute-start(f32[3,1024]{1,0:T(4,128)} %fusion.222), channel_id=1, source_target_pairs={{0,8},{8,16},{16,24},{1,9},{9,17},{17,25},{2,10},{10,18},{18,26},{... | collective-permute-start | bytes 36872 | tf_op jit(solution)/shard_map/ppermute | solution.py:18
  254.9 171.9 %all-reduce.28.cloned.1.call-start = ((), (), s32[]{:S(2)}) async-start(), calls=%async_computation.27 | async-start | bytes 524288 | tf_op jit(solution)/shard_map/psum | solution.py:445
  511.6 106.1 %reduce-scatter.48.cloned.1.call-start = ((), (), s32[]{:S(2)}) async-start(), calls=%async_computation.36 | async-start | bytes 1966080 | tf_op jit(solution)/shard_map/reduce_scatter | solution.py:511
  515.5 140.5 %reduce-scatter.68.cloned.1.call-start = ((), (), s32[]{:S(2)}) async-start(), calls=%async_computation.46 | async-start | bytes 2621440 | tf_op jit(solution)/shard_map/reduce_scatter | solution.py:547
  519.4 174.7 %reduce-scatter.64.cloned.1.call-start = ((), (), s32[]{:S(2)}) async-start(), calls=%async_computation.44 | async-start | bytes 2621440 | tf_op jit(solution)/shard_map/reduce_scatter | solution.py:541
  523.3 209.2 %reduce-scatter.72.cloned.1.call-start = ((), (), s32[]{:S(2)}) async-start(), calls=%async_computation.48 | async-start | bytes 2621440 | tf_op jit(solution)/shard_map/reduce_scatter | solution.py:553
  527.5 233.1 %reduce-scatter.52.cloned.1.call-start = ((), (), s32[]{:S(2)}) async-start(), calls=%async_computation.38 | async-start | bytes 655360 | tf_op jit(solution)/shard_map/reduce_scatter | solution.py:517
  529.8 259.2 %reduce-scatter.42.cloned.1.call-start = ((), (), s32[]{:S(2)}) async-start(), calls=%async_computation.33 | async-start | bytes 655360 | tf_op jit(solution)/shard_map/reduce_scatter | solution.py:499
  531.1 284.7 %reduce-scatter.80.cloned.1.call-start = ((), (), s32[]{:S(2)}) async-start(), calls=%async_computation.52 | async-start | bytes 81920
  531.9 360.6 %reduce-scatter.62.cloned.1.call-start = ((), (), s32[]{:S(2)}) async-start(), calls=%async_computation.43 | async-start | bytes 163840 | tf_op jit(solution)/shard_map/reduce_scatter | solution.py:585
  532.5 368.5 %reduce-scatter.76.cloned.1.call-start = ((), (), s32[]{:S(2)}) async-start(), calls=%async_computation.50 | async-start | bytes 81920
  533.4 387.9 %reduce-scatter.46.cloned.1.call-start = ((), (), s32[]{:S(2)}) async-start(), calls=%async_computation.35 | async-start | bytes 20480 | tf_op jit(solution)/shard_map/reduce_scatter | solution.py:573
  557.6 373.9 %reduce-scatter.58.cloned.1.call-start = ((), (), s32[]{:S(2)}) async-start(), calls=%async_computation.41 | async-start | bytes 81920 | tf_op jit(solution)/shard_map/reduce_scatter | solution.py:582
  583.5 356.1 %reduce-scatter.50.cloned.1.call-start = ((), (), s32[]{:S(2)}) async-start(), calls=%async_computation.37 | async-start | bytes 491520 | tf_op jit(solution)/shard_map/reduce_scatter | solution.py:576
  617.7 332.1 %reduce-scatter.70.cloned.1.call-start = ((), (), s32[]{:S(2)}) async-start(), calls=%async_computation.47 | async-start | bytes 655360 | tf_op jit(solution)/shard_map/reduce_scatter | solution.py:594
  656.0 312.8 %reduce-scatter.66.cloned.1.call-start = ((), (), s32[]{:S(2)}) async-start(), calls=%async_computation.45 | async-start | bytes 655360 | tf_op jit(solution)/shard_map/reduce_scatter | solution.py:591
  694.2 296.8 %reduce-scatter.74.cloned.1.call-start = ((), (), s32[]{:S(2)}) async-start(), calls=%async_computation.49 | async-start | bytes 655360 | tf_op jit(solution)/shard_map/reduce_scatter | solution.py:597
  732.5 290.5 %reduce-scatter.38.cloned.1.call-start = ((), (), s32[]{:S(2)}) async-start(), calls=%async_computation.31 | async-start | bytes 1966080 | tf_op jit(solution)/shard_map/reduce_scatter | solution.py:493
  734.7 309.8 %reduce-scatter.54.cloned.1.call-start = ((), (), s32[]{:S(2)}) async-start(), calls=%async_computation.39 | async-start | bytes 163840 | tf_op jit(solution)/shard_map/reduce_scatter | solution.py:579
  760.7 303.4 %reduce-scatter.44.cloned.1.call-start = ((), (), s32[]{:S(2)}) async-start(), calls=%async_computation.34 | async-start | bytes 163840 | tf_op jit(solution)/shard_map/reduce_scatter | solution.py:570
  789.1 306.8 %reduce-scatter.34.cloned.1.call-start = ((), (), s32[]{:S(2)}) async-start(), calls=%async_computation.29 | async-start | bytes 1966080 | tf_op jit(solution)/shard_map/reduce_scatter | solution.py:487
  791.4 327.5 %reduce-scatter.40.cloned.1.call-start = ((), (), s32[]{:S(2)}) async-start(), calls=%async_computation.32 | async-start | bytes 491520 | tf_op jit(solution)/shard_map/reduce_scatter | solution.py:567
  1023.1 117.1 %reduce-scatter.36.cloned.1.call-start = ((), (), s32[]{:S(2)}) async-start(), calls=%async_computation.30 | async-start | bytes 491520 | tf_op jit(solution)/shard_map/reduce_scatter | solution.py:564
  (156 other events, 2296.4 us)
Sparse Core Ops, SparseCore 0:
  255.0 20.7 all-reduce.25
  426.8 45.9 reduce-scatter.31
  480.5 19.5 all-reduce.29
  502.8 25.9 reduce-scatter.59
  532.3 23.6 reduce-scatter.77
  559.3 24.0 reduce-scatter.55
  586.7 30.9 reduce-scatter.47
  620.8 35.1 reduce-scatter.67
  659.0 35.1 reduce-scatter.63
  697.3 35.1 reduce-scatter.71
  735.9 24.7 reduce-scatter.51
  764.1 24.7 reduce-scatter.41
  792.1 23.6 reduce-scatter.79
  818.0 19.1 reduce-scatter.61
  840.3 21.9 reduce-scatter.75
  865.0 18.8 reduce-scatter.45
  926.7 19.8 reduce-scatter.69
  948.9 19.9 reduce-scatter.65
  971.1 19.8 reduce-scatter.73
  993.8 29.1 reduce-scatter.37
  1025.3 19.1 reduce-scatter.53
  1066.9 29.0 reduce-scatter.33
  1098.2 20.5 reduce-scatter.39
  1121.2 18.8 reduce-scatter.35
  (5 shorter events, 87.6 us)
where the time goes:
time: 1170 us; the launch traced here: 1160 us
  waiting for transfers between devices  472 us (40%)
  blocking collectives  305 us (26%)
  matrix products  164 us (14%)
  other arithmetic  85.6 us (7%)
  local copies, waits for them, and re-layouts  85 us (7%)
  starting transfers between devices  18.7 us (2%)
  between operations  18.2 us (2%)
    psum x1, blocking collectives, body(): lax.psum((g_kernel[:, :inner_width], g_kernel[:, inner_width:], g_log_rat...  75.9 us
    all_gather x2, blocking collectives, entering(): lax.all_gather(part.astype(kind), axis)  54.1 us
    dot_general x3, matrix products, output_part(): inside = jnp.einsum('tsh,shp->thp', mixing, scan_input, precision=highest)  50.9 us
    unnamed x32, waiting for transfers between devices  45.9 us
    psum x3, waiting for transfers between devices, head_total(): lax.psum(partial_sum.astype(jnp.bfloat16), 'head').astype(jnp.float32)  39.9 us
    reduce_scatter x1, waiting for transfers between devices, body(): lax.psum_scatter(fold_rows(g_down, seq_count).astype(jnp.bfloat16), 'batc...  38.3 us
    reduce_scatter x1, waiting for transfers between devices, body(): lax.psum_scatter(fold_rows(g_lift, seq_count).astype(jnp.bfloat16), 'batc...  38.2 us
    reduce_scatter x1, waiting for transfers between devices, body(): lax.psum_scatter(fold_rows(g_gate, seq_count).astype(jnp.bfloat16), 'batc...  38.1 us
  transfers between devices with their start and end apart: 31, of which 22 were waited for; matrix products, arithmetic and copies ran while one was open for 13% of the time, Pallas kernels for 0%

commit v1 on v0

--- a/solution.py
+++ b/solution.py
@@ -1,6 +1,10 @@
+import functools
+
 import jax
 import jax.numpy as jnp
 from jax import lax
+from jax.experimental import pallas as pl
+from jax.experimental.pallas import tpu as pltpu
 from jax.sharding import PartitionSpec as P
 
 HD = 64
@@ -10,6 +14,246 @@
 rope_base = 10000.0
 neg_large = -1e30
 highest = lax.Precision.HIGHEST
+
+
+LANES = 128
+MESH = pl.DeviceIdType.MESH
+
+
+def exchange(source, target, send_sem, recv_sem, device):
+    return pltpu.make_async_remote_copy(
+        src_ref=source,
+        dst_ref=target,
+        send_sem=send_sem,
+        recv_sem=recv_sem,
+        device_id=device,
+        device_id_type=MESH,
+    )
+
+
+def column_chunks(widths, most):
+    chunks = []
+    for group, width in enumerate(widths):
+        count = -(-width // most)
+        tiles = width // LANES
+        start = 0
+        for k in range(count):
+            size = (tiles // count + (1 if k < tiles % count else 0)) * LANES
+            chunks.append((group, start, size))
+            start += size
+    return chunks
+
+
+def reduce_kernel(seq_count, batch_count, chunks, *refs):
+    count = 1 + max(c[0] for c in chunks)
+    groups, refs = refs[:count], refs[count:]
+    small_in, refs = refs[0], refs[1:]
+    outs, refs = refs[:count], refs[count:]
+    small_out, refs = refs[0], refs[1:]
+    first_buf, refs = refs[:count], refs[count:]
+    second_buf, refs = refs[:count], refs[count:]
+    third_buf, refs = refs[:count], refs[count:]
+    small_buf, sem_one, sem_two, sem_seq, sem_back, sem_small = refs
+    seq, head, batch = lax.axis_index("seq"), lax.axis_index("head"), lax.axis_index("batch")
+    low_bit = lax.rem(batch, 2)
+    high_bit = batch // 2
+    low_peer = (seq, head, batch + 1 - 2 * low_bit)
+    high_peer = (seq, head, batch + 2 - 4 * high_bit)
+    world = seq_count * batch_count
+    mine = seq * batch_count + batch
+
+    def other(step):
+        place = lax.rem(mine + step, world)
+        return (place // batch_count, head, lax.rem(place, batch_count))
+
+    barrier = pltpu.get_barrier_semaphore()
+
+    def greet(step, carry):
+        pl.semaphore_signal(barrier, inc=1, device_id=other(step), device_id_type=MESH)
+        return carry
+
+    lax.fori_loop(1, world, greet, 0)
+    pl.semaphore_wait(barrier, world - 1)
+
+    def small_copy(step):
+        return exchange(
+            small_in,
+            small_buf.at[mine],
+            sem_small.at[0, step],
+            sem_small.at[1, step],
+            other(step),
+        )
+
+    def first_copy(k):
+        group, start, size = chunks[k]
+        columns = pl.ds(start, size)
+        source, target = groups[group], first_buf[group]
+        if k % 2 == 0:
+            part = source.at[:, :, 1 - low_bit, :, columns]
+            peer = low_peer
+        else:
+            part = source.at[:, 1 - high_bit, :, :, columns]
+            peer = high_peer
+        return exchange(part, target.at[:, :, :, columns], sem_one.at[0, k], sem_one.at[1, k], peer)
+
+    def second_copy(k):
+        group, start, size = chunks[k]
+        columns = pl.ds(start, size)
+        if k % 2 == 0:
+            away, peer = 1 - high_bit, high_peer
+        else:
+            away, peer = 1 - low_bit, low_peer
+        return exchange(
+            first_buf[group].at[:, away, :, columns],
+            second_buf[group].at[:, :, columns],
+            sem_two.at[0, k],
+            sem_two.at[1, k],
+            peer,
+        )
+
+    def seq_copy(k, step):
+        group, start, size = chunks[k]
+        columns = pl.ds(start, size)
+        place = lax.rem(seq + step, seq_count)
+        return exchange(
+            second_buf[group].at[place, :, columns],
+            third_buf[group].at[step - 1, :, columns],
+            sem_seq.at[0, k, step - 1],
+            sem_seq.at[1, k, step - 1],
+            (place, head, batch),
+        )
+
+    def back_copy(k, turn):
+        group, start, size = chunks[k]
+        columns = pl.ds(start, size)
+        out = outs[group]
+        if (k + turn) % 2 == 0:
+            peer = high_peer
+        else:
+            peer = low_peer
+        if turn == 0:
+            part = out.at[high_bit, low_bit, :, columns]
+        elif k % 2 == 0:
+            part = out.at[:, low_bit, :, columns]
+        else:
+            part = out.at[high_bit, :, :, columns]
+        return exchange(part, part, sem_back.at[0, k, turn], sem_back.at[1, k, turn], peer)
+
+    def each_seq(action):
+        lax.fori_loop(1, seq_count, lambda step, carry: (action(step), carry)[1], 0)
+
+    def add_first(k):
+        group, start, size = chunks[k]
+        columns = pl.ds(start, size)
+
+        def one(place, carry):
+            if k % 2 == 0:
+                own = groups[group][place, :, low_bit, :, columns]
+            else:
+                own = groups[group][place, high_bit, :, :, columns]
+            came = first_buf[group][place, :, :, columns]
+            first_buf[group][place, :, :, columns] = (
+                own.astype(jnp.float32) + came.astype(jnp.float32)
+            ).astype(jnp.bfloat16)
+            return carry
+
+        lax.fori_loop(0, seq_count, one, 0)
+
+    def add_second(k):
+        group, start, size = chunks[k]
+        columns = pl.ds(start, size)
+        keep = high_bit if k % 2 == 0 else low_bit
+
+        def one(place, carry):
+            own = first_buf[group][place, keep, :, columns]
+            came = second_buf[group][place, :, columns]
+            second_buf[group][place, :, columns] = (
+                own.astype(jnp.float32) + came.astype(jnp.float32)
+            ).astype(jnp.bfloat16)
+            return carry
+
+        lax.fori_loop(0, seq_count, one, 0)
+
+    def add_third(k):
+        group, start, size = chunks[k]
+        columns = pl.ds(start, size)
+
+        def one(slot, total):
+            return total + third_buf[group][slot, :, columns].astype(jnp.float32)
+
+        total = second_buf[group][seq, :, columns].astype(jnp.float32)
+        total = lax.fori_loop(0, seq_count - 1, one, total)
+        outs[group][high_bit, low_bit, :, columns] = total.astype(jnp.bfloat16)
+
+    total_chunks = len(chunks)
+    ahead = 3
+    for k in range(min(ahead, total_chunks)):
+        first_copy(k).start()
+    lax.fori_loop(1, world, lambda step, carry: (small_copy(step).start(), carry)[1], 0)
+    for turn in range(total_chunks + 4):
+        k = turn
+        if k < total_chunks:
+            first_copy(k).wait()
+            if k + ahead < total_chunks:
+                first_copy(k + ahead).start()
+            add_first(k)
+            second_copy(k).start()
+        k = turn - 1
+        if 0 <= k < total_chunks:
+            second_copy(k).wait()
+            add_second(k)
+            each_seq(lambda step: seq_copy(k, step).start())
+        k = turn - 2
+        if 0 <= k < total_chunks:
+            each_seq(lambda step: seq_copy(k, step).wait())
+            add_third(k)
+            back_copy(k, 0).start()
+        k = turn - 3
+        if 0 <= k < total_chunks:
+            back_copy(k, 0).wait()
+            back_copy(k, 1).start()
+        k = turn - 4
+        if 0 <= k < total_chunks:
+            back_copy(k, 1).wait()
+    lax.fori_loop(1, world, lambda step, carry: (small_copy(step).wait(), carry)[1], 0)
+    small_buf[mine] = small_in[...]
+    small_out[...] = lax.fori_loop(
+        1, world, lambda place, total: total + small_buf[place], small_buf[0]
+    )
+
+
+def reduce_gradients(groups, small):
+    seq_count, batch_count = lax.axis_size("seq"), lax.axis_size("batch")
+    world = seq_count * batch_count
+    rows = groups[0].shape[0] // world
+    widths = [g.shape[1] for g in groups]
+    chunks = column_chunks(widths, 512)
+    blocks = [g.reshape(seq_count, 2, 2, rows, g.shape[1]) for g in groups]
+    vmem = pl.BlockSpec(memory_space=pltpu.VMEM)
+    count, parts = len(groups), len(chunks)
+    result = pl.pallas_call(
+        functools.partial(reduce_kernel, seq_count, batch_count, chunks),
+        out_shape=[jax.ShapeDtypeStruct((2, 2, rows, w), jnp.bfloat16) for w in widths]
+        + [jax.ShapeDtypeStruct(small.shape, jnp.float32)],
+        in_specs=[vmem] * (count + 1),
+        out_specs=[vmem] * (count + 1),
+        scratch_shapes=[pltpu.VMEM((seq_count, 2, rows, w), jnp.bfloat16) for w in widths]
+        + [pltpu.VMEM((seq_count, rows, w), jnp.bfloat16) for w in widths]
+        + [pltpu.VMEM((seq_count - 1, rows, w), jnp.bfloat16) for w in widths]
+        + [
+            pltpu.VMEM((world,) + small.shape, jnp.float32),
+            pltpu.SemaphoreType.DMA((2, parts)),
+            pltpu.SemaphoreType.DMA((2, parts)),
+            pltpu.SemaphoreType.DMA((2, parts, seq_count - 1)),
+            pltpu.SemaphoreType.DMA((2, parts, 2)),
+            pltpu.SemaphoreType.DMA((2, world)),
+        ],
+        compiler_params=pltpu.CompilerParams(
+            collective_id=0, has_side_effects=True, vmem_limit_bytes=56 << 20
+        ),
+        name="reduce_gradients",
+    )(*blocks, small)
+    return [r.reshape(4 * rows, w) for r, w in zip(result[:-1], widths)], result[-1]
 
 
 def shifted(value, axis, steps):
@@ -470,209 +714,67 @@
     d_normed = head_total(d_normed)
     d_hidden_norm, g_mixer_gain = norm1_back(d_normed)
     grad_tokens = d_second + d_hidden_norm
-    g_gate_z = matmul_first(normed_low, d_gate_z_low)
-    g_inner = matmul_first(normed_low, d_inner_low)
-    g_maps = matmul_first(normed_low, d_maps_low)
-    g_step_weight = matmul_first(normed_low, d_raw_low)
-    g_query = matmul_first(normed_low, d_query_low)
-    g_memory = matmul_first(normed_low, d_memory_low)
-    seq_count = lax.axis_size("seq")
-    folded = (
-        lax.psum_scatter(
-            fold_rows(g_mixer_gain, seq_count).astype(jnp.bfloat16),
-            "batch",
-            scatter_dimension=1,
-            tiled=True,
-        ).astype(jnp.float32),
-        lax.psum_scatter(
-            fold_rows(g_gate_z, seq_count).astype(jnp.bfloat16),
-            "batch",
-            scatter_dimension=1,
-            tiled=True,
-        ).astype(jnp.float32),
-        lax.psum_scatter(
-            fold_rows(g_inner, seq_count).astype(jnp.bfloat16),
-            "batch",
-            scatter_dimension=1,
-            tiled=True,
-        ).astype(jnp.float32),
-        lax.psum_scatter(
-            fold_rows(g_maps, seq_count).astype(jnp.bfloat16),
-            "batch",
-            scatter_dimension=1,
-            tiled=True,
-        ).astype(jnp.float32),
-        lax.psum_scatter(
-            fold_rows(g_step_weight, seq_count).astype(jnp.bfloat16),
-            "batch",
-            scatter_dimension=1,
-            tiled=True,
-        ).astype(jnp.float32),
-        lax.psum_scatter(
-            fold_rows(g_mamba_out, seq_count).astype(jnp.bfloat16),
-            "batch",
-            scatter_dimension=1,
-            tiled=True,
-        ).astype(jnp.float32),
-        lax.psum_scatter(
-            fold_rows(g_query, seq_count).astype(jnp.bfloat16),
-            "batch",
-            scatter_dimension=1,
-            tiled=True,
-        ).astype(jnp.float32),
-        lax.psum_scatter(
-            fold_rows(g_memory, seq_count).astype(jnp.bfloat16),
-            "batch",
-            scatter_dimension=1,
-            tiled=True,
-        ).astype(jnp.float32),
-        lax.psum_scatter(
-            fold_rows(g_attn_out, seq_count).astype(jnp.bfloat16),
-            "batch",
-            scatter_dimension=1,
-            tiled=True,
-        ).astype(jnp.float32),
-        lax.psum_scatter(
-            fold_rows(g_feed_gain, seq_count).astype(jnp.bfloat16),
-            "batch",
-            scatter_dimension=1,
-            tiled=True,
-        ).astype(jnp.float32),
-        lax.psum_scatter(
-            fold_rows(g_gate, seq_count).astype(jnp.bfloat16),
-            "batch",
-            scatter_dimension=1,
-            tiled=True,
-        ).astype(jnp.float32),
-        lax.psum_scatter(
-            fold_rows(g_lift, seq_count).astype(jnp.bfloat16),
-            "batch",
-            scatter_dimension=1,
-            tiled=True,
-        ).astype(jnp.float32),
-        lax.psum_scatter(
-            fold_rows(g_down, seq_count).astype(jnp.bfloat16),
-            "batch",
-            scatter_dimension=1,
-            tiled=True,
-        ).astype(jnp.float32),
-    )
-    summed = (
-        lax.psum_scatter(
-            folded[0].astype(jnp.bfloat16), "seq", scatter_dimension=0, tiled=True
-        ).astype(jnp.float32),
-        lax.psum_scatter(
-            folded[1].astype(jnp.bfloat16), "seq", scatter_dimension=0, tiled=True
-        ).astype(jnp.float32),
-        lax.psum_scatter(
-            folded[2].astype(jnp.bfloat16), "seq", scatter_dimension=0, tiled=True
-        ).astype(jnp.float32),
-        lax.psum_scatter(
-            folded[3].astype(jnp.bfloat16), "seq", scatter_dimension=0, tiled=True
-        ).astype(jnp.float32),
-        lax.psum_scatter(
-            folded[4].astype(jnp.bfloat16), "seq", scatter_dimension=0, tiled=True
-        ).astype(jnp.float32),
-        lax.psum_scatter(
-            folded[5].astype(jnp.bfloat16), "seq", scatter_dimension=0, tiled=True
-        ).astype(jnp.float32),
-        lax.psum_scatter(
-            folded[6].astype(jnp.bfloat16), "seq", scatter_dimension=0, tiled=True
-        ).astype(jnp.float32),
-        lax.psum_scatter(
-            folded[7].astype(jnp.bfloat16), "seq", scatter_dimension=0, tiled=True
-        ).astype(jnp.float32),
-        lax.psum_scatter(
-            folded[8].astype(jnp.bfloat16), "seq", scatter_dimension=0, tiled=True
-        ).astype(jnp.float32),
-        lax.psum_scatter(
-            folded[9].astype(jnp.bfloat16), "seq", scatter_dimension=0, tiled=True
-        ).astype(jnp.float32),
-        lax.psum_scatter(
-            folded[10].astype(jnp.bfloat16), "seq", scatter_dimension=0, tiled=True
-        ).astype(jnp.float32),
-        lax.psum_scatter(
-            folded[11].astype(jnp.bfloat16), "seq", scatter_dimension=0, tiled=True
-        ).astype(jnp.float32),
-        lax.psum_scatter(
-            folded[12].astype(jnp.bfloat16), "seq", scatter_dimension=0, tiled=True
-        ).astype(jnp.float32),
-    )
-    joined = (
-        lax.all_gather(summed[0].astype(jnp.bfloat16), "batch", axis=1, tiled=True).astype(
-            jnp.float32
-        ),
-        lax.all_gather(summed[1].astype(jnp.bfloat16), "batch", axis=1, tiled=True).astype(
-            jnp.float32
-        ),
-        lax.all_gather(summed[2].astype(jnp.bfloat16), "batch", axis=1, tiled=True).astype(
-            jnp.float32
-        ),
-        lax.all_gather(summed[3].astype(jnp.bfloat16), "batch", axis=1, tiled=True).astype(
-            jnp.float32
-        ),
-        lax.all_gather(summed[4].astype(jnp.bfloat16), "batch", axis=1, tiled=True).astype(
-            jnp.float32
-        ),
-        lax.all_gather(summed[5].astype(jnp.bfloat16), "batch", axis=1, tiled=True).astype(
-            jnp.float32
-        ),
-        lax.all_gather(summed[6].astype(jnp.bfloat16), "batch", axis=1, tiled=True).astype(
-            jnp.float32
-        ),
-        lax.all_gather(summed[7].astype(jnp.bfloat16), "batch", axis=1, tiled=True).astype(
-            jnp.float32
-        ),
-        lax.all_gather(summed[8].astype(jnp.bfloat16), "batch", axis=1, tiled=True).astype(
-            jnp.float32
-        ),
-        lax.all_gather(summed[9].astype(jnp.bfloat16), "batch", axis=1, tiled=True).astype(
-            jnp.float32
-        ),
-        lax.all_gather(summed[10].astype(jnp.bfloat16), "batch", axis=1, tiled=True).astype(
-            jnp.float32
-        ),
-        lax.all_gather(summed[11].astype(jnp.bfloat16), "batch", axis=1, tiled=True).astype(
-            jnp.float32
-        ),
-        lax.all_gather(summed[12].astype(jnp.bfloat16), "batch", axis=1, tiled=True).astype(
-            jnp.float32
-        ),
-    )
-    shards = tuple((member[0] for member in joined))
-    small = lax.psum(
-        (
-            g_kernel[:, :inner_width],
-            g_kernel[:, inner_width:],
-            g_log_rate,
-            g_step_bias,
-            g_skip,
-            g_mamba_gain,
-        ),
-        ("seq", "batch"),
-    )
+    d_raw_wide = jnp.pad(d_raw_low, ((0, 0), (0, LANES - head_count)))
+    mixer_side = jnp.concatenate(
+        [d_gate_z_low, d_inner_low, d_maps_low, d_raw_wide, d_query_low, d_memory_low], axis=1
+    )
+    feed_side = jnp.concatenate([d_gate_low, d_lift_low], axis=1)
+    mixed_side = jnp.concatenate([gated_low, attention_low], axis=1)
+    groups = [
+        matmul_first(normed_low, mixer_side).astype(jnp.bfloat16),
+        matmul_first(normed2_low, feed_side).astype(jnp.bfloat16),
+        matmul_first(d_mix, mixed_side).astype(jnp.bfloat16),
+        matmul_first(grad_out, active_low).astype(jnp.bfloat16),
+    ]
+    wide = hidden.shape[1]
+    scalars = jnp.concatenate([g_log_rate, g_step_bias, g_skip])
+    small = jnp.concatenate(
+        [
+            g_kernel,
+            jnp.stack(
+                [
+                    jnp.pad(g_mamba_gain, (0, wide - inner_width)),
+                    g_mixer_gain,
+                    g_feed_gain,
+                    jnp.pad(scalars, (0, wide - scalars.shape[0])),
+                ]
+            ),
+        ],
+        axis=0,
+    )
+    (mixer_sum, feed_sum, mixed_sum, down_sum), small = reduce_gradients(groups, small)
+    maps_width = conv_maps.shape[1]
+    query_width = query_weight.shape[1]
+    memory_width = memory_weight.shape[1]
+    edges = [0]
+    for width in (inner_width, inner_width, maps_width, LANES, query_width, memory_width):
+        edges.append(edges[-1] + width)
+    pieces = [mixer_sum[:, a:b].astype(jnp.float32) for a, b in zip(edges[:-1], edges[1:])]
+    own_rows = wide // lax.axis_size("seq")
+    own_at = lax.axis_index("seq") * own_rows
+    ff_width = gate_weight.shape[1]
     return (
         layer_out[None],
         grad_tokens[None],
-        shards[0],
-        shards[1],
-        shards[2],
-        shards[3],
-        shards[4],
-        small[0],
-        small[1],
-        small[2],
-        small[3],
-        small[4],
-        small[5],
-        shards[5],
-        shards[6],
-        shards[7],
-        shards[8],
-        shards[9],
-        shards[10],
-        shards[11],
-        shards[12],
+        lax.dynamic_slice_in_dim(small[5], own_at, own_rows),
+        pieces[0],
+        pieces[1],
+        pieces[2],
+        pieces[3][:, :head_count],
+        small[:4, :inner_width],
+        small[:4, inner_width:],
+        small[7, :head_count],
+        small[7, head_count : 2 * head_count],
+        small[7, 2 * head_count : 3 * head_count],
+        small[4, :inner_width],
+        mixed_sum[:, :inner_width].astype(jnp.float32),
+        pieces[4],
+        pieces[5],
+        mixed_sum[:, inner_width:].astype(jnp.float32),
+        lax.dynamic_slice_in_dim(small[6], own_at, own_rows),
+        feed_sum[:, :ff_width].astype(jnp.float32),
+        feed_sum[:, ff_width:].astype(jnp.float32),
+        down_sum.astype(jnp.float32),
     )
 
 

time: 1170 us -> 707 us (0.60)
  waiting for transfers between devices: 472 us -> 58.7 us
  blocking collectives: 305 us -> 105 us
  Pallas kernels: 0 us -> 161 us
    reduce_scatter x21 -> x0, waiting for transfers between devices: 352 us -> none  [the longest x1 38.3 us: body(): lax.psum_scatter(fold_rows(g_down, seq_count).astype(jnp.bfloat16), 'batc...]
    pallas_call x0 -> x1, Pallas kernels: none -> 161 us  [reduce_gradients(): pl.pallas_call(functools.partial(reduce_kernel, seq_count, batch_count, c...]
    all_gather x11 -> x0, blocking collectives: 104 us -> none  [the longest x1 13.5 us: body(): lax.all_gather(summed[12].astype(jnp.bfloat16), 'batch', axis=1, tiled=True)]
    psum x1 -> x0, blocking collectives: 75.9 us -> none  [body(): lax.psum((g_kernel[:, :inner_width], g_kernel[:, inner_width:], g_log_rat...]
    unnamed x32 -> x5, waiting for transfers between devices: 45.9 us -> 0.08 us
    unnamed x2 -> x0, blocking collectives: 17.3 us -> none
    unnamed x326 -> x282, local copies, waits for them, and re-layouts: 26.4 us -> 17.8 us
    dot_general x11 -> x4, matrix products: 23.8 us -> 21 us  [matmul_first(): lax.dot_general(former, latter, (((0,), (0,)), ((), ())), preferred_eleme...]
  transfers between devices with their start and end apart: 31 -> 7, of which waited for: 22 -> 4; matrix products, arithmetic and copies ran while one was open for 13% -> 15% of each run, Pallas kernels for 0% -> 0%
where the time goes in v1:
time: 707 us; the launch traced here: 697 us
  matrix products  162 us (23%)
  Pallas kernels  161 us (23%)
  blocking collectives  105 us (15%)
  other arithmetic  93.9 us (13%)
  local copies, waits for them, and re-layouts  81.3 us (11%)
  waiting for transfers between devices  58.7 us (8%)
  between operations  17 us (2%)
  loops' own time  10.1 us (1%)
  starting transfers between devices  8 us (1%)
    pallas_call x1, Pallas kernels, reduce_gradients(): pl.pallas_call(functools.partial(reduce_kernel, seq_count, batch_count, c...  161 us
    dot_general x3, matrix products, output_part(): inside = jnp.einsum('tsh,shp->thp', mixing, scan_input, precision=highest)  53.6 us
    all_gather x2, blocking collectives, entering(): lax.all_gather(part.astype(kind), axis)  52 us
    psum x3, waiting for transfers between devices, head_total(): lax.psum(partial_sum.astype(jnp.bfloat16), 'head').astype(jnp.float32)  30.3 us
    dot_general x11, matrix products, matmul_last(): lax.dot_general(former, latter, (((1,), (1,)), ((), ())), preferred_eleme...  23.5 us
    dot_general x11, matrix products, matmul(): return jnp.dot(former, latter, preferred_element_type=jnp.float32)  22.4 us
    dot_general x4, matrix products, matmul_first(): lax.dot_general(former, latter, (((0,), (0,)), ((), ())), preferred_eleme...  21 us
    reduce_scatter x1, waiting for transfers between devices, body(): lax.psum_scatter(pair_blocks.reshape(total_rows, memory_heads * 2 * HD).a...  20.7 us
  transfers between devices with their start and end apart: 7, of which 4 were waited for; matrix products, arithmetic and copies ran while one was open for 15% of the time, Pallas kernels for 0%

profile of v1, /device:TPU:0, one launch (start us, length us, event | category | flops | bytes accessed | tf_op | source)
XLA Modules:
  0.0 697.3 jit_solution(8004203190595865828)
XLA Ops:
  38.0 14.5 %all_gather.27 = bf16[2048,1,64]{0,2,1:T(8,128)(2,1)S(1)} all-gather(bf16[512,1,64]{0,2,1:T(8,128)(2,1)S(1)} %pad_maximum_fusion.5), channel_id=1, replica_groups=mesh['seq'=4,'head'=2,'batch'=4] {'seq'}, dimensions={0}, use_global_device_ids=true | all-gather | bytes 327680 | tf_op jit(solution)/shard_map/all_gather | solution.py:532
  53.2 13.9 %all-gather.1 = bf16[2048,1,1,64]{0,3,2,1:T(8,128)(2,1)S(1)} all-gather(bf16[512,1,1,64]{0,3,2,1:T(8,128)(2,1)S(1)} %copy-done.64), channel_id=3, replica_groups=mesh['seq'=4,'head'=2,'batch'=4] {'seq'}, dimensions={0}, use_global_device_ids=true | all-gather | bytes 327680 | tf_op jit(solution)/shard_map/all_gather | solution.py:533
  71.8 14.1 %while.60 = (s32[]{:T(128)}, f32[1,4,512]{2,1,0:T(4,128)S(1)}, f32[1,4,512]{2,1,0:T(4,128)S(1)}, f32[1,4,512,64]{2,3,1,0:T(8,128)}, s32[4]{0:T(128)S(1)}, /*inde...) while((s32[]{:T(128)}, f32[1,4,512]{2,1,0:T(4,128)S(1)}, ...), condition=%wide.region_12.13_spmd.clone, body=%wide.region_7.12_spmd.clone.sunk | while | flops 283122688 | bytes 15226205 | solution.py:572
  73.0 9.0 %conditional.6 = ((f32[1,4,512]{2,1,0:T(4,128)S(1)}, f32[1,4,512]{2,1,0:T(4,128)S(1)}, f32[1,4,512,64]{2,3,1,0:T(8,128)})) conditional(s32[]{:T(128)} %convert_element_type.583, (f32[1,4,512]{2,1,0:T(4,128)S(1)}, f32[1,4,512]{2,1,0:T(4,128)S(1)}, f32[1,4,512,64]{2,3,1,0:T(8,128)}) %tuple.226, (s32[]{:T(128)}, s32[]{:T(128)}, s32[2048]{0:T(1024)S(1)}, ...), branch_computations={%region_8.8_spmd, %region_9.11_spmd} | conditional | flops 283122688 | bytes 15223886 | solution.py:565
  89.2 35.1 %all-gather.3 = bf16[4,1,12]{2,1,0:T(2,128)(2,1)S(1)} all-gather(bf16[1,1,12]{2,1,0:T(2,128)(2,1)S(1)} %bitcast.564), channel_id=1, replica_groups=mesh['seq'=4,'head'=2,'batch'=4] {'seq'}, dimensions={0}, use_global_device_ids=true | all-gather | bytes 120 | tf_op jit(solution)/shard_map/all_gather | solution.py:268
  139.5 16.9 %all-gather = bf16[48,128,64]{1,2,0:T(8,128)(2,1)} all-gather(bf16[12,128,64]{1,2,0:T(8,128)(2,1)S(1)} %fusion.151), channel_id=2, replica_groups=mesh['seq'=4,'head'=2,'batch'=4] {'seq'}, dimensions={0}, use_global_device_ids=true | all-gather | bytes 983040 | tf_op jit(solution)/shard_map/all_gather | solution.py:268
  156.3 22.8 %while.62 = (s32[]{:T(128)}, f32[12,128,64]{2,1,0:T(8,128)}, s32[]{:T(128)}, bf16[4,12]{1,0:T(4,128)(2,1)S(1)}, bf16[4,12,128,64]{2,3,1,0:T(8,128)(2,1)}, /*index=5*/s32[]{:T(128)}, s32[]{:T(128)}) while((s32[]{:T(128)}, f32[12,128,64]{2,1,0:T(8,128)}, s32[]{:T(128)}, bf16[4,12]{1,0:T(4,128)(2,1)S(1)}, ...), condition=%wide.region_4.5_spmd.clone, body=%wide.region_3.4_spmd.clone.sunk | while | flops 491536 | bytes 1769697 | solution.py:285
  183.9 17.5 %fusion.120 = f32[512,12,64]{0,2,1:T(8,128)} fusion(f32[512,12,64]{0,2,1:T(8,128)S(1)} %bitcast.480, f32[512,12,64]{0,2,1:T(8,128)S(1)} %bitcast.490, f32[512,12]{0,1:T(8,128)S(1)} %copy-done.85, f32[512,512]{1,0:T(8,128)} %get-tuple-element.1166, f32[512,12]{0,1:T(8,128)S(1)} %bitcast.522, f32[512,512]{1,0:T(8,128)} %fusion.184, ...), kind=kOutput, calls=%fused_computation.179 | convolution fusion | flops 2433220608 | bytes 7151664 | tf_op jit(solution)/shard_map/jvp(tsh,shp->thp)/dot_general | solution.py:384
  216.8 17.9 %all-reduce.20.cloned.1.call-done = bf16[512,1024]{1,0:T(8,128)(2,1)} async-done(((bf16[512,1024]{1,0:T(8,128)(2,1)}), bf16[512,1024]{1,0:T(8,128)(2,1)}) %all-reduce.20.cloned.1.call-update) | async-done | bytes 1048592 | tf_op jit(solution)/shard_map/psum | solution.py:397
  256.6 12.4 %all-reduce.22.cloned.1.call-done = bf16[512,1024]{1,0:T(8,128)(2,1)} async-done(((bf16[512,1024]{1,0:T(8,128)(2,1)}), bf16[512,1024]{1,0:T(8,128)(2,1)}) %all-reduce.22.cloned.1.call-update) | async-done | bytes 1048592 | tf_op jit(solution)/shard_map/psum | solution.py:397
  290.5 20.2 %all-gather.2 = bf16[48,128,64]{1,2,0:T(8,128)(2,1)} all-gather(bf16[12,128,64]{1,2,0:T(8,128)(2,1)S(1)} %fusion.148), channel_id=4, replica_groups=mesh['seq'=4,'head'=2,'batch'=4] {'seq'}, dimensions={0}, use_global_device_ids=true | all-gather | bytes 983040 | tf_op jit(solution)/shard_map/all_gather | solution.py:293
  310.8 9.4 %while.59 = (s32[]{:T(128)}, f32[12,128,64]{2,1,0:T(8,128)S(1)}, s32[]{:T(128)}, bf16[4,12]{1,0:T(4,128)(2,1)S(1)}, bf16[4,12,128,64]{2,3,1,0:T(8,128)(2,1)}, /*index=5*/s32[]{:T(128)}, s32[]{:T(128)}, s32[]{:T(128)}, s32[]{:T(128)}) while((s32[]{:T(128)}, f32[12,128,64]{2,1,0:T(8,128)S(1)}, s32[]{:T(128)}, bf16[4,12]{1,0:T(4,128)(2,1)S(1)}, ...), condition=%wide.region_21.22_spmd, body=%wide.region_20.21_spmd.sunk | while | flops 294930 | bytes 1769739 | solution.py:310
  326.3 5.8 fusion.140
  332.1 5.8 fusion.143
  345.7 6.2 reduce-window.26
  354.3 21.1 %fusion.70 = (f32[512,12]{0,1:T(8,128)S(1)}, f32[512,12]{0,1:T(8,128)S(1)}, f32[512,12]{0,1:T(8,128)}, f32[512,512]{1,0:T(8,128)}) fusion(f32[512,12]{0,1:T(8,128)} %get-tuple-element.1149, f32[512,512]{1,0:T(8,128)} %get-tuple-element.1166, f32[512,12]{0,1:T(8,128)S(1)} %bitcast.525, f32[512,512]{1,0:T(8,128)} %fusion.184, ...), kind=kOutput, calls=%fused_computation.87 | convolution fusion | flops 2462824448 | bytes 6676480 | tf_op jit(solution)/shard_map/transpose(jvp(tsh,shp->thp))/dot_general | solution.py:384
  381.3 15.0 %fusion.119 = f32[512,12,64]{0,2,1:T(8,128)} fusion(f32[512,12,64]{0,2,1:T(8,128)} %get-tuple-element.1172, f32[512,12,64]{0,2,1:T(8,128)} %bitcast.486, f32[12,64,512]{2,1,0:T(8,128)} %bitcast.487, f32[512,12]{0,1:T(8,128)} %get-tuple-element.1149, f32[512,512]{1,0:T(8,128)} %get-tuple-element.1166, f32[512,12]{0,1:T(8,128)S(1)} %bitcast.527, ...), kind=kOutput, calls=%fused_computation.177 | convolution fusion | flops 2433220608 | bytes 8724528 | tf_op jit(solution)/shard_map/transpose(jvp(tsh,shp->thp))/dot_general | solution.py:384
  411.1 17.8 %while.61 = (s32[]{:T(128)}, f32[1,4,512,64]{2,3,1,0:T(8,128)S(1)}, bf16[4,512,1,2,64]{1,4,3,2,0:T(8,128)(2,1)}, s32[4]{0:T(128)S(1)}, s32[]{:T(128)}, /*index=5...) while((s32[]{:T(128)}, f32[1,4,512,64]{2,3,1,0:T(8,128)S(1)}, ...), condition=%wide.region_38.39_spmd.clone, body=%wide.region_35.38_spmd.clone.sunk | while | flops 684854272 | bytes 23729536 | solution.py:658
  412.6 9.9 %conditional.7 = (f32[1,4,512,64]{2,3,1,0:T(8,128)S(1)}, bf16[1,512,1,2,64]{1,4,3,2,0:T(8,128)(2,1)S(1)}) conditional(s32[]{:T(128)} %convert_element_type.584, f32[1,4,512,64]{2,3,1,0:T(8,128)S(1)} %get-tuple-element.1505, (s32[]{:T(128)}, s32[]{:T(128)}, s32[2048]{0:T(1024)}, s32[512]{0:T(512)S(1)}, bf16[4,512,1,64]{1,3,2,0:T(8,128)(2,1)S(1)}, ...), branch_computations={%region_36.36_spmd, %region_37.37_spmd} | conditional | flops 684854272 | bytes 23464546 | solution.py:656
  444.0 7.6 %collective-permute-done.1 = f32[3,1024]{1,0:T(4,128)S(1)} collective-permute-done((f32[3,1024]{1,0:T(4,128)S(1)}, f32[3,1024]{1,0:T(4,128)S(1)}, u32[]{:S(2)}, u32[]{:S(2)}) %collective-permute-start.1) | collective-permute-done | bytes 12320 | tf_op jit(solution)/shard_map/ppermute | solution.py:262
  456.3 20.7 %reduce-scatter.2.cloned.1.call-done = bf16[512,128]{0,1:T(8,128)(2,1)} async-done(((bf16[2048,128]{0,1:T(8,128)(2,1)}), bf16[512,128]{0,1:T(8,128)(2,1)}) %reduce-scatter.2.cloned.1.call-update) | async-done | bytes 131088 | tf_op jit(solution)/shard_map/reduce_scatter | solution.py:661
  483.6 6.3 convolution_convert_fusion.1
  500.8 6.5 convolution_convert_fusion
  510.2 161.4 %reduce_gradients.1 = (bf16[2,2,64,2304]{3,2,1,0:T(8,128)(2,1)}, bf16[2,2,64,2048]{3,2,1,0:T(8,128)(2,1)}, bf16[2,2,64,1024]{3,2,1,0:T(8,128)(2,1)}, bf16[2,2,64,1024]{3,2,1,0:T(8,128)(2,1)}, f32[8,1024]{1,0:T(8,128)}) custom-call(bf16[4,2,2,64,2304]{4,3,2,1,0:T(8,128)(2,1)} %bitcast.493, bf16[4,2,2,64,2048]{4,3,2,1,0:T(8,128)(2,1)} %bitcast.495, ...), custom_call_target="tpu_custom_call" | custom-call | tf_op jit(solution)/shard_map/reduce_gradients/pallas_call | solution.py:234
  (535 shorter events, 265.6 us)
Async XLA Ops:
  7.2 234.1 %copy-start = (bf16[1024,1024]{1,0:T(8,128)(2,1)S(1)}, bf16[1024,1024]{1,0:T(8,128)(2,1)}, u32[]{:S(2)}) copy-start(bf16[1024,1024]{1,0:T(8,128)(2,1)} %param.54) | copy-start | bytes 6291460
  7.2 227.5 %all-reduce.20.cloned.1.call-start = ((), (), s32[]{:S(2)}) async-start(), calls=%async_computation.1 | async-start | bytes 2097152 | tf_op jit(solution)/shard_map/psum | solution.py:397
  9.5 24.8 %copy-start.98 = (f32[512]{0:T(512)}, f32[512]{0:T(512)S(1)}, u32[]{:S(2)}) copy-start(f32[512]{0:T(512)S(1)} %fusion.231) | copy-start | bytes 6148
  13.7 111.3 %collective-permute-start = (f32[3,1024]{1,0:T(4,128)}, f32[3,1024]{1,0:T(4,128)}, u32[]{:S(2)}, u32[]{:S(2)}) collective-permute-start(f32[3,1024]{1,0:T(4,128)} %fusion.226), channel_id=1, source_target_pairs={{0,8},{8,16},{16,24},{1,9},{9,17},{17,25},{2,10},{10,18},{18,26},{... | collective-permute-start | bytes 36872 | tf_op jit(solution)/shard_map/ppermute | solution.py:262
  27.5 99.5 %copy-start.70 = (f32[1,1024]{1,0:T(1,128)}, f32[1,1024]{1,0:T(1,128)S(1)}, u32[]{:S(2)}) copy-start(f32[1,1024]{1,0:T(1,128)S(1)} %get-tuple-element.1150) | copy-start | bytes 12292
  34.3 18.9 %copy-start.64 = (bf16[512,1,1,64]{0,3,2,1:T(8,128)(2,1)S(1)}, bf16[512,1,1,64]{0,3,2,1:T(8,128)(2,1)}, u32[]{:S(2)}) copy-start(bf16[512,1,1,64]{0,3,2,1:T(8,128)(2,1)} %slice.400) | copy-start | bytes 196612
  37.7 33.2 %copy-start.51 = (f32[512,32]{0,1:T(8,128)}, f32[512,32]{0,1:T(8,128)S(1)}, u32[]{:S(2)}) copy-start(f32[512,32]{0,1:T(8,128)S(1)} %get-tuple-element.1164) | copy-start | bytes 196612
  38.0 33.7 %copy-start.129 = (s32[4]{0:T(128)S(1)}, s32[4]{0:T(128)}, u32[]{:S(2)}) copy-start(s32[4]{0:T(128)} %iota_multiply_fusion) | copy-start | bytes 52
  89.1 198.6 %copy-start.58 = (f32[512,12]{0,1:T(8,128)}, f32[512,12]{0,1:T(8,128)S(1)}, u32[]{:S(2)}) copy-start(f32[512,12]{0,1:T(8,128)S(1)} %get-tuple-element.1147) | copy-start | bytes 73732
  136.6 19.7 %copy-start.119 = (bf16[4,1,12]{2,0,1:T(4,128)(2,1)S(1)}, bf16[4,1,12]{2,0,1:T(4,128)(2,1)}, u32[]{:S(2)}) copy-start(bf16[4,1,12]{2,0,1:T(4,128)(2,1)} %copy.339) | copy-start | bytes 292
  216.3 20.1 %copy-start.78 = (f32[1024]{0:T(1024)S(1)}, f32[1024]{0:T(1024)}, u32[]{:S(2)}) copy-start(f32[1024]{0:T(1024)} %param.51) | copy-start | bytes 12292
  216.4 52.6 %all-reduce.22.cloned.1.call-start = ((), (), s32[]{:S(2)}) async-start(), calls=%async_computation.2 | async-start | bytes 2097152 | tf_op jit(solution)/shard_map/psum | solution.py:397
  248.0 187.1 %all-reduce.24.cloned.1.call-start = ((), (), s32[]{:S(2)}) async-start(), calls=%async_computation.3 | async-start | bytes 524288 | tf_op jit(solution)/shard_map/psum | solution.py:689
  354.3 21.1 %copy-start.65 = (f32[512,12]{0,1:T(8,128)S(1)}, f32[512,12]{0,1:T(8,128)}, u32[]{:S(2)}) copy-start(f32[512,12]{0,1:T(8,128)} %multiply_reduce_fusion.9) | copy-start | bytes 73732
  354.3 21.1 %copy-start.97 = (f32[512]{0:T(512)S(1)}, f32[512]{0:T(512)}, u32[]{:S(2)}) copy-start(f32[512]{0:T(512)} %get-tuple-element.1156) | copy-start | bytes 6148
  354.3 27.0 %copy-start.128 = (f32[12]{0:T(128)S(1)}, f32[12]{0:T(128)}, u32[]{:S(2)}) copy-start(f32[12]{0:T(128)} %param.45) | copy-start | bytes 148
  405.0 72.0 %reduce-scatter.2.cloned.1.call-start = ((), (), s32[]{:S(2)}) async-start(), calls=%async_computation.4 | async-start | bytes 655360 | tf_op jit(solution)/shard_map/reduce_scatter | solution.py:661
  411.1 18.0 %copy-start.37 = (bf16[1024,256]{1,0:T(8,128)(2,1)S(1)}, bf16[1024,256]{1,0:T(8,128)(2,1)}, u32[]{:S(2)}) copy-start(bf16[1024,256]{1,0:T(8,128)(2,1)} %param.48) | copy-start | bytes 1572868
  435.0 72.3 %all-reduce.26.cloned.1.call-start = ((), (), s32[]{:S(2)}) async-start(), calls=%async_computation.5 | async-start | bytes 4194304 | tf_op jit(solution)/shard_map/psum | solution.py:397
  441.3 10.4 %collective-permute-start.1 = (f32[3,1024]{1,0:T(4,128)S(1)}, f32[3,1024]{1,0:T(4,128)S(1)}, u32[]{:S(2)}, u32[]{:S(2)}) collective-permute-start(f32[3,1024]{1,0:T(4,128)S(1)} %pad_add_fusion.1), channel_id=1, source_target_pairs={{8,0},{16,8},{24,16},{9,1},{17,9},{25,17},{10,2},{18,10},{26,18},{... | collective-permute-start | bytes 36872 | tf_op jit(solution)/shard_map/ppermute | solution.py:262
  453.9 24.0 %copy-start.82 = (f32[512]{0:T(512)S(1)}, f32[512]{0:T(512)}, u32[]{:S(2)}) copy-start(f32[512]{0:T(512)} %copy-done.81) | copy-start | bytes 6148
  453.9 24.0 %copy-start.117 = (f32[32]{0:T(128)S(1)}, f32[32]{0:T(128)}, u32[]{:S(2)}) copy-start(f32[32]{0:T(128)} %copy-done.116) | copy-start | bytes 388
  453.9 24.3 %copy-start.43 = (bf16[1024,128]{1,0:T(8,128)(2,1)S(1)}, bf16[1024,128]{1,0:T(8,128)(2,1)}, u32[]{:S(2)}) copy-start(bf16[1024,128]{1,0:T(8,128)(2,1)} %param.49) | copy-start | bytes 786436
  456.3 22.5 %copy-start.22 = (f32[512,1024]{1,0:T(8,128)S(1)}, f32[512,1024]{1,0:T(8,128)}, u32[]{:S(2)}) copy-start(f32[512,1024]{1,0:T(8,128)} %fusion.268) | copy-start | bytes 6291460
  (117 other events, 620.4 us)
Sparse Core Ops, SparseCore 0:
  216.5 18.1 all-reduce.19
  248.1 20.7 all-reduce.21
  405.1 16.4 all-reduce.23
  435.1 41.7 reduce-scatter.1
  483.7 19.5 all-reduce.25

commit v2 on v1

v2 whole, which is shorter than its diff:
```python
import functools

import jax
import jax.numpy as jnp
from jax import lax
from jax.experimental import pallas as pl
from jax.experimental.pallas import tpu as pltpu
from jax.sharding import PartitionSpec as P

HD = 64
eps_norm = 1e-05
rope_base = 10000.0
neg_large = -1e30
highest = lax.Precision.HIGHEST


LANES = 128
MESH = pl.DeviceIdType.MESH


def exchange(source, target, send_sem, recv_sem, device):
    return pltpu.make_async_remote_copy(
        src_ref=source,
        dst_ref=target,
        send_sem=send_sem,
        recv_sem=recv_sem,
        device_id=device,
        device_id_type=MESH,
    )


def column_chunks(widths, most):
    chunks = []
    for group, width in enumerate(widths):
        count = -(-width // most)
        tiles = width // LANES
        start = 0
        for k in range(count):
            size = (tiles // count + (1 if k < tiles % count else 0)) * LANES
            chunks.append((group, start, size))
            start += size
    return chunks


def reduce_kernel(seq_count, batch_count, chunks, *refs):
    count = 1 + max(c[0] for c in chunks)
    groups, refs = refs[:count], refs[count:]
    small_in, refs = refs[0], refs[1:]
    outs, refs = refs[:count], refs[count:]
    small_out, refs = refs[0], refs[1:]
    first_buf, refs = refs[:count], refs[count:]
    second_buf, refs = refs[:count], refs[count:]
    third_buf, refs = refs[:count], refs[count:]
    small_buf, sem_one, sem_two, sem_seq, sem_back, sem_small = refs
    seq, head, batch = lax.axis_index("seq"), lax.axis_index("head"), lax.axis_index("batch")
    low_bit = lax.rem(batch, 2)
    high_bit = batch // 2
    low_peer = (seq, head, batch + 1 - 2 * low_bit)
    high_peer = (seq, head, batch + 2 - 4 * high_bit)
    world = seq_count * batch_count
    mine = seq * batch_count + batch

    def other(step):
        place = lax.rem(mine + step, world)
        return (place // batch_count, head, lax.rem(place, batch_count))

    barrier = pltpu.get_barrier_semaphore()

    def greet(step, carry):
        pl.semaphore_signal(barrier, inc=1, device_id=other(step), device_id_type=MESH)
        return carry

    lax.fori_loop(1, world, greet, 0)
    pl.semaphore_wait(barrier, world - 1)

    def small_copy(step):
        return exchange(
            small_in,
            small_buf.at[mine],
            sem_small.at[0, step],
            sem_small.at[1, step],
            other(step),
        )

    def first_copy(k):
        group, start, size = chunks[k]
        columns = pl.ds(start, size)
        source, target = groups[group], first_buf[group]
        if k % 2 == 0:
            part = source.at[:, :, 1 - low_bit, :, columns]
            peer = low_peer
        else:
            part = source.at[:, 1 - high_bit, :, :, columns]
            peer = high_peer
        return exchange(part, target.at[:, :, :, columns], sem_one.at[0, k], sem_one.at[1, k], peer)

    def second_copy(k):
        group, start, size = chunks[k]
        columns = pl.ds(start, size)
        if k % 2 == 0:
            away, peer = 1 - high_bit, high_peer
        else:
            away, peer = 1 - low_bit, low_peer
        return exchange(
            first_buf[group].at[:, away, :, columns],
            second_buf[group].at[:, :, columns],
            sem_two.at[0, k],
            sem_two.at[1, k],
            peer,
        )

    def seq_copy(k, step):
        group, start, size = chunks[k]
        columns = pl.ds(start, size)
        place = lax.rem(seq + step, seq_count)
        return exchange(
            second_buf[group].at[place, :, columns],
            third_buf[group].at[step - 1, :, columns],
            sem_seq.at[0, k, step - 1],
            sem_seq.at[1, k, step - 1],
            (place, head, batch),
        )

    def back_copy(k, turn):
        group, start, size = chunks[k]
        columns = pl.ds(start, size)
        out = outs[group]
        if (k + turn) % 2 == 0:
            peer = high_peer
        else:
            peer = low_peer
        if turn == 0:
            part = out.at[high_bit, low_bit, :, columns]
        elif k % 2 == 0:
            part = out.at[:, low_bit, :, columns]
        else:
            part = out.at[high_bit, :, :, columns]
        return exchange(part, part, sem_back.at[0, k, turn], sem_back.at[1, k, turn], peer)

    def each_seq(action):
        lax.fori_loop(1, seq_count, lambda step, carry: (action(step), carry)[1], 0)

    def add_first(k):
        group, start, size = chunks[k]
        columns = pl.ds(start, size)

        def one(place, carry):
            if k % 2 == 0:
                own = groups[group][place, :, low_bit, :, columns]
            else:
                own = groups[group][place, high_bit, :, :, columns]
            came = first_buf[group][place, :, :, columns]
            first_buf[group][place, :, :, columns] = (
                own.astype(jnp.float32) + came.astype(jnp.float32)
            ).astype(jnp.bfloat16)
            return carry

        lax.fori_loop(0, seq_count, one, 0)

    def add_second(k):
        group, start, size = chunks[k]
        columns = pl.ds(start, size)
        keep = high_bit if k % 2 == 0 else low_bit

        def one(place, carry):
            own = first_buf[group][place, keep, :, columns]
            came = second_buf[group][place, :, columns]
            second_buf[group][place, :, columns] = (
                own.astype(jnp.float32) + came.astype(jnp.float32)
            ).astype(jnp.bfloat16)
            return carry

        lax.fori_loop(0, seq_count, one, 0)

    def add_third(k):
        group, start, size = chunks[k]
        columns = pl.ds(start, size)

        def one(slot, total):
            return total + third_buf[group][slot, :, columns].astype(jnp.float32)

        total = second_buf[group][seq, :, columns].astype(jnp.float32)
        total = lax.fori_loop(0, seq_count - 1, one, total)
        outs[group][high_bit, low_bit, :, columns] = total.astype(jnp.bfloat16)

    total_chunks = len(chunks)
    ahead = 3
    for k in range(min(ahead, total_chunks)):
        first_copy(k).start()
    lax.fori_loop(1, world, lambda step, carry: (small_copy(step).start(), carry)[1], 0)
    for turn in range(total_chunks + 4):
        k = turn
        if k < total_chunks:
            first_copy(k).wait()
            if k + ahead < total_chunks:
                first_copy(k + ahead).start()
            add_first(k)
            second_copy(k).start()
        k = turn - 1
        if 0 <= k < total_chunks:
            second_copy(k).wait()
            add_second(k)
            each_seq(lambda step: seq_copy(k, step).start())
        k = turn - 2
        if 0 <= k < total_chunks:
            each_seq(lambda step: seq_copy(k, step).wait())
            add_third(k)
            back_copy(k, 0).start()
        k = turn - 3
        if 0 <= k < total_chunks:
            back_copy(k, 0).wait()
            back_copy(k, 1).start()
        k = turn - 4
        if 0 <= k < total_chunks:
            back_copy(k, 1).wait()
    lax.fori_loop(1, world, lambda step, carry: (small_copy(step).wait(), carry)[1], 0)
    small_buf[mine] = small_in[...]
    small_out[...] = lax.fori_loop(
        1, world, lambda place, total: total + small_buf[place], small_buf[0]
    )


def reduce_gradients(groups, small):
    seq_count, batch_count = lax.axis_size("seq"), lax.axis_size("batch")
    world = seq_count * batch_count
    rows = groups[0].shape[0] // world
    widths = [g.shape[1] for g in groups]
    chunks = column_chunks(widths, 512)
    blocks = [g.reshape(seq_count, 2, 2, rows, g.shape[1]) for g in groups]
    vmem = pl.BlockSpec(memory_space=pltpu.VMEM)
    count, parts = len(groups), len(chunks)
    result = pl.pallas_call(
        functools.partial(reduce_kernel, seq_count, batch_count, chunks),
        out_shape=[jax.ShapeDtypeStruct((2, 2, rows, w), jnp.bfloat16) for w in widths]
        + [jax.ShapeDtypeStruct(small.shape, jnp.float32)],
        in_specs=[vmem] * (count + 1),
        out_specs=[vmem] * (count + 1),
        scratch_shapes=[pltpu.VMEM((seq_count, 2, rows, w), jnp.bfloat16) for w in widths]
        + [pltpu.VMEM((seq_count, rows, w), jnp.bfloat16) for w in widths]
        + [pltpu.VMEM((seq_count - 1, rows, w), jnp.bfloat16) for w in widths]
        + [
            pltpu.VMEM((world,) + small.shape, jnp.float32),
            pltpu.SemaphoreType.DMA((2, parts)),
            pltpu.SemaphoreType.DMA((2, parts)),
            pltpu.SemaphoreType.DMA((2, parts, seq_count - 1)),
            pltpu.SemaphoreType.DMA((2, parts, 2)),
            pltpu.SemaphoreType.DMA((2, world)),
        ],
        compiler_params=pltpu.CompilerParams(
            collective_id=0, has_side_effects=True, vmem_limit_bytes=56 << 20
        ),
        name="reduce_gradients",
    )(*blocks, small)
    return [r.reshape(4 * rows, w) for r, w in zip(result[:-1], widths)], result[-1]


def matmul(former, latter):
    return jnp.dot(former, latter, preferred_element_type=jnp.float32)


def matmul_last(former, latter):
    return lax.dot_general(
        former, latter, (((1,), (1,)), ((), ())), preferred_element_type=jnp.float32
    )


def matmul_first(former, latter):
    return lax.dot_general(
        former, latter, (((0,), (0,)), ((), ())), preferred_element_type=jnp.float32
    )


TILE = 128


def sigmoid(v):
    return 1.0 / (1.0 + jnp.exp(-v))


def peer_device():
    return (lax.axis_index("seq"), 1 - lax.axis_index("head"), lax.axis_index("batch"))


def greet_peer(barrier, peer):
    pl.semaphore_signal(barrier, inc=1, device_id=peer, device_id_type=MESH)
    pl.semaphore_wait(barrier, 1)


def tile_rows(i):
    return pl.ds(pl.multiple_of(i * TILE, TILE), TILE)


def each(count, action):
    lax.fori_loop(0, count, lambda i, carry: (action(i), carry)[1], 0)


def feed_kernel(
    y_ref,
    gate_z_ref,
    attention_ref,
    tokens_ref,
    cotangent_ref,
    mamba_gain_ref,
    feed_gain_ref,
    mamba_output_ref,
    attention_out_ref,
    gate_weight_hbm,
    lift_weight_hbm,
    down_weight_hbm,
    out_ref,
    d_second_ref,
    d_y_ref,
    d_gate_z_ref,
    d_attention_ref,
    g_feed_ref,
    g_mixed_ref,
    g_down_ref,
    g_feed_gain_ref,
    g_mamba_gain_ref,
    gate_weight,
    lift_weight,
    down_weight,
    gated,
    g_six,
    inverse_six,
    second,
    inverse_two,
    normed2,
    active,
    d_feed,
    d_mix,
    d_gated,
    square_send,
    square_recv,
    cross_send,
    cross_recv,
    mixed_send,
    mixed_recv,
    lift_send,
    lift_recv,
    norm_send,
    norm_recv,
    weight_sem,
    sem_square,
    sem_cross,
    sem_mixed,
    sem_lift,
    sem_norm,
):
    rows = y_ref.shape[0]
    tiles = rows // TILE
    inner = y_ref.shape[1]
    width = feed_gain_ref.shape[1]
    feed = down_weight.shape[1]
    all_inner = inner * lax.axis_size("head")
    peer = peer_device()
    loads = [
        pltpu.make_async_copy(source, target, weight_sem.at[k])
        for k, (source, target) in enumerate(
            (
                (gate_weight_hbm, gate_weight),
                (lift_weight_hbm, lift_weight),
                (down_weight_hbm, down_weight),
            )
        )
    ]
    for load in loads:
        load.start()
    greet_peer(pltpu.get_barrier_semaphore(), peer)

    def swap(send, recv, sems, i):
        rows_now = tile_rows(i)
        return exchange(send.at[rows_now], recv.at[rows_now], sems.at[0, i], sems.at[1, i], peer)

    def gate_tile(i):
        at = tile_rows(i)
        gate_now = gate_z_ref[at, :]
        value = y_ref[at, :] * gate_now * sigmoid(gate_now)
        g_six[at, :] = value
        square_send[at, :] = jnp.broadcast_to(
            jnp.sum(value * value, axis=1, keepdims=True), (TILE, LANES)
        )
        swap(square_send, square_recv, sem_square, i).start()

    each(tiles, gate_tile)

    def mixed_tile(i):
        at = tile_rows(i)
        swap(square_send, square_recv, sem_square, i).wait()
        total = square_send[at, :] + square_recv[at, :]
        inverse = lax.rsqrt(total[:, :1] / all_inner + eps_norm)
        inverse_six[at, :] = jnp.broadcast_to(inverse, (TILE, LANES))
        low = (g_six[at, :] * inverse * mamba_gain_ref[...]).astype(jnp.bfloat16)
        gated[at, :] = low
        part = matmul_last(low, mamba_output_ref[...]) + matmul_last(
            attention_ref[at, :], attention_out_ref[...]
        )
        mixed_send[at, :] = part.astype(jnp.bfloat16)
        swap(mixed_send, mixed_recv, sem_mixed, i).start()

    each(tiles, mixed_tile)
    for load in loads:
        load.wait()

    def feed_tile(i):
        at = tile_rows(i)
        swap(mixed_send, mixed_recv, sem_mixed, i).wait()
        total = mixed_send[at, :].astype(jnp.float32) + mixed_recv[at, :].astype(jnp.float32)
        hidden = tokens_ref[at, :].astype(jnp.float32) + total
        second[at, :] = hidden
        inverse = lax.rsqrt(jnp.mean(hidden * hidden, axis=1, keepdims=True) + eps_norm)
        inverse_two[at, :] = jnp.broadcast_to(inverse, (TILE, LANES))
        low = (hidden * inverse * feed_gain_ref[...]).astype(jnp.bfloat16)
        normed2[at, :] = low
        gate_now = matmul(low, gate_weight[...])
        lift_now = matmul(low, lift_weight[...])
        sig = sigmoid(gate_now)
        silu = gate_now * sig
        act = (silu * lift_now).astype(jnp.bfloat16)
        active[at, :] = act
        lift_send[at, :] = matmul_last(act, down_weight[...]).astype(jnp.bfloat16)
        swap(lift_send, lift_recv, sem_lift, i).start()
        d_act = matmul(cotangent_ref[at, :], down_weight[...])
        d_gate = (d_act * lift_now * (sig * (1.0 + gate_now * (1.0 - sig)))).astype(jnp.bfloat16)
        d_lift = (d_act * silu).astype(jnp.bfloat16)
        d_feed[at, :feed] = d_gate
        d_feed[at, feed:] = d_lift
        part = matmul_last(d_gate, gate_weight[...]) + matmul_last(d_lift, lift_weight[...])
        norm_send[at, :] = part.astype(jnp.bfloat16)
        swap(norm_send, norm_recv, sem_norm, i).start()

    each(tiles, feed_tile)
    g_feed_gain_ref[...] = jnp.zeros_like(g_feed_gain_ref)
    g_mamba_gain_ref[...] = jnp.zeros_like(g_mamba_gain_ref)

    def norm_tile(i):
        at = tile_rows(i)
        swap(norm_send, norm_recv, sem_norm, i).wait()
        d_norm = norm_send[at, :].astype(jnp.float32) + norm_recv[at, :].astype(jnp.float32)
        hidden = second[at, :]
        inverse = inverse_two[at, :][:, :1]
        e_two = d_norm * feed_gain_ref[...]
        g_feed_gain_ref[...] += jnp.sum(d_norm * hidden * inverse, axis=0, keepdims=True)
        cross = jnp.sum(e_two * hidden, axis=1, keepdims=True) / width
        d_hidden = (
            cotangent_ref[at, :].astype(jnp.float32)
            + inverse * e_two
            - hidden * (inverse * inverse * inverse * cross)
        )
        d_second_ref[at, :] = d_hidden
        low = d_hidden.astype(jnp.bfloat16)
        d_mix[at, :] = low
        d_attention_ref[at, :] = matmul(low, attention_out_ref[...])
        d_gated_now = matmul(low, mamba_output_ref[...])
        d_gated[at, :] = d_gated_now
        six = g_six[at, :]
        g_mamba_gain_ref[...] += jnp.sum(
            d_gated_now * six * inverse_six[at, :][:, :1], axis=0, keepdims=True
        )
        cross_send[at, :] = jnp.broadcast_to(
            jnp.sum(d_gated_now * mamba_gain_ref[...] * six, axis=1, keepdims=True), (TILE, LANES)
        )
        swap(cross_send, cross_recv, sem_cross, i).start()

    each(tiles, norm_tile)

    def gate_back(i):
        at = tile_rows(i)
        swap(cross_send, cross_recv, sem_cross, i).wait()
        cross = (cross_send[at, :] + cross_recv[at, :])[:, :1] / all_inner
        inverse = inverse_six[at, :][:, :1]
        d_six = inverse * (d_gated[at, :] * mamba_gain_ref[...]) - g_six[at, :] * (
            inverse * inverse * inverse * cross
        )
        gate_now = gate_z_ref[at, :]
        sig = sigmoid(gate_now)
        d_y_ref[at, :] = d_six * gate_now * sig
        d_gate_z_ref[at, :] = (
            d_six * y_ref[at, :] * (sig * (1.0 + gate_now * (1.0 - sig)))
        ).astype(jnp.bfloat16)

    each(tiles, gate_back)

    def out_tile(i):
        at = tile_rows(i)
        swap(lift_send, lift_recv, sem_lift, i).wait()
        total = lift_send[at, :].astype(jnp.float32) + lift_recv[at, :].astype(jnp.float32)
        out_ref[at, :] = (second[at, :] + total).astype(jnp.bfloat16)

    each(tiles, out_tile)

    def weight_block(k):
        block = pl.ds(pl.multiple_of(k * 256, 256), 256)
        g_down_ref[block, :] = matmul_first(cotangent_ref[:, block], active[...]).astype(
            jnp.bfloat16
        )
        g_feed_ref[block, :] = matmul_first(normed2[:, block], d_feed[...]).astype(jnp.bfloat16)
        d_mix_now = d_mix[:, block]
        g_mixed_ref[block, :inner] = matmul_first(d_mix_now, gated[...]).astype(jnp.bfloat16)
        g_mixed_ref[block, inner:] = matmul_first(d_mix_now, attention_ref[...]).astype(
            jnp.bfloat16
        )

    each(width // 256, weight_block)


def feed_layer(
    y,
    gate_z,
    attention_low,
    tokens,
    cotangent,
    mamba_gain,
    feed_gain,
    mamba_output,
    attention_out,
    gate_weight,
    lift_weight,
    down_weight,
):
    rows, inner = y.shape
    width = tokens.shape[1]
    feed = gate_weight.shape[1]
    att = attention_low.shape[1]
    tiles = rows // TILE
    vmem = pl.BlockSpec(memory_space=pltpu.VMEM)
    hbm = pl.BlockSpec(memory_space=pl.ANY)
    low, full = jnp.bfloat16, jnp.float32
    shape = jax.ShapeDtypeStruct
    return pl.pallas_call(
        feed_kernel,
        out_shape=[
            shape((rows, width), low),
            shape((rows, width), full),
            shape((rows, inner), full),
            shape((rows, inner), low),
            shape((rows, att), full),
            shape((width, 2 * feed), low),
            shape((width, inner + att), low),
            shape((width, feed), low),
            shape((1, width), full),
            shape((1, inner), full),
        ],
        in_specs=[vmem] * 9 + [hbm] * 3,
        out_specs=[vmem] * 10,
        scratch_shapes=[
            pltpu.VMEM((width, feed), low),
            pltpu.VMEM((width, feed), low),
            pltpu.VMEM((width, feed), low),
            pltpu.VMEM((rows, inner), low),
            pltpu.VMEM((rows, inner), full),
            pltpu.VMEM((rows, LANES), full),
            pltpu.VMEM((rows, width), full),
            pltpu.VMEM((rows, LANES), full),
            pltpu.VMEM((rows, width), low),
            pltpu.VMEM((rows, feed), low),
            pltpu.VMEM((rows, 2 * feed), low),
            pltpu.VMEM((rows, width), low),
            pltpu.VMEM((rows, inner), full),
            pltpu.VMEM((rows, LANES), full),
            pltpu.VMEM((rows, LANES), full),
            pltpu.VMEM((rows, LANES), full),
            pltpu.VMEM((rows, LANES), full),
        ]
        + [pltpu.VMEM((rows, width), low)] * 6
        + [pltpu.SemaphoreType.DMA((3,))]
        + [pltpu.SemaphoreType.DMA((2, tiles))] * 5,
        compiler_params=pltpu.CompilerParams(
            collective_id=1, has_side_effects=True, vmem_limit_bytes=60 << 20
        ),
        name="feed_layer",
    )(
        y,
        gate_z,
        attention_low,
        tokens,
        cotangent,
        mamba_gain[None],
        feed_gain[None],
        mamba_output,
        attention_out,
        gate_weight,
        lift_weight,
        down_weight,
    )


CHUNK = 128
HALO = 8
PIECE = 256


def turn_half(values):
    lane = lax.broadcasted_iota(jnp.int32, values.shape, 1)
    return jnp.where(
        lax.rem(lane, HD) < HD // 2,
        pltpu.roll(values, LANES - HD // 2, 1),
        pltpu.roll(values, HD // 2, 1),
    )


def two_parts(values):
    high = values.astype(jnp.bfloat16)
    return high, (values - high.astype(jnp.float32)).astype(jnp.bfloat16)


def spread_heads(values, spread):
    high, rest = two_parts(values)
    return matmul(high, spread) + matmul(rest, spread)


def sum_heads(values, spread):
    high, rest = two_parts(values)
    return matmul_last(high, spread) + matmul_last(rest, spread)


def spread_matrix(inner, size):
    row = lax.broadcasted_iota(jnp.int32, (LANES, inner), 0)
    lane = lax.broadcasted_iota(jnp.int32, (LANES, inner), 1)
    return jnp.where(lane // size == row, 1.0, 0.0).astype(jnp.bfloat16)


def ordered(count):
    row = lax.broadcasted_iota(jnp.int32, (count, count), 0)
    lane = lax.broadcasted_iota(jnp.int32, (count, count), 1)
    return row >= lane


def halves(values, size):
    lane = lax.broadcasted_iota(jnp.int32, values.shape, 1)
    return jnp.concatenate(
        [jnp.where(lane < size, values, 0.0), jnp.where(lane < size, 0.0, values)], axis=0
    ).astype(jnp.bfloat16)


def soft_plus(v):
    return jnp.maximum(v, 0.0) + jnp.log1p(jnp.exp(-jnp.abs(v)))


def chunk_flags(seg_ref, c):
    window = seg_ref[pl.ds(pl.multiple_of(c * CHUNK, CHUNK), CHUNK + HALO), :]
    own = window[HALO:]
    start = jnp.where(own == window[HALO - 1 : HALO], 1.0, 0.0)
    end = jnp.where(own == own[CHUNK - 1 :], 1.0, 0.0)
    return own, start, end


def greet_seq(barrier, with_peer):
    seq, head, batch = lax.axis_index("seq"), lax.axis_index("head"), lax.axis_index("batch")
    count = lax.axis_size("seq")

    def one(step, carry):
        pl.semaphore_signal(
            barrier,
            inc=1,
            device_id=(lax.rem(seq + step, count), head, batch),
            device_id_type=MESH,
        )
        return carry

    lax.fori_loop(1, count, one, 0)
    if with_peer:
        pl.semaphore_signal(barrier, inc=1, device_id=peer_device(), device_id_type=MESH)
    pl.semaphore_wait(barrier, count - 1 + with_peer)


def mixer_kernel(
    size,
    tokens_ref,
    gain_ref,
    seg_ref,
    table_ref,
    gate_weight,
    input_weight,
    maps_weight,
    step_weight,
    query_weight,
    memory_weight,
    taps_ref,
    bias_ref,
    rate_ref,
    skip_ref,
    gate_z_ref,
    pre_ref,
    conv_ref,
    raw_ref,
    cum_ref,
    y_ref,
    states_ref,
    query_ref,
    memory_ref,
    normed,
    spread_ref,
    act,
    scaled,
    added,
    decay,
    total,
    local,
    state,
    chain_out,
    chain_in,
    sem_memory,
    sem_halo,
    sem_chain,
):
    seq, head, batch = lax.axis_index("seq"), lax.axis_index("head"), lax.axis_index("batch")
    count = lax.axis_size("seq")
    rows = tokens_ref.shape[0]
    tiles = rows // CHUNK
    inner = y_ref.shape[1]
    width = pre_ref.shape[1]
    state_width = (width - inner) // 2
    following = (lax.rem(seq + 1, count), head, batch)
    greet_seq(pltpu.get_barrier_semaphore(), 0)

    def memory_copy(step, place, owner):
        return exchange(
            memory_ref.at[owner],
            memory_ref.at[owner],
            sem_memory.at[0, step],
            sem_memory.at[1, step],
            (place, head, batch),
        )

    halo_copy = exchange(
        pre_ref.at[pl.ds(rows, HALO)],
        pre_ref.at[pl.ds(0, HALO)],
        sem_halo.at[0],
        sem_halo.at[1],
        following,
    )

    def memory_tile(i):
        at = tile_rows(i)
        hidden = tokens_ref[at, :].astype(jnp.float32)
        inverse = lax.rsqrt(jnp.mean(hidden * hidden, axis=1, keepdims=True) + eps_norm)
        low = (hidden * inverse * gain_ref[...]).astype(jnp.bfloat16)
        normed[at, :] = low
        value = matmul(low, memory_weight[...])
        lane = lax.broadcasted_iota(jnp.int32, value.shape, 1)
        turned = value * table_ref[at, :LANES] + turn_half(value) * table_ref[at, LANES:]
        memory_ref[seq, at, :] = jnp.where(lane < HD, turned, value).astype(jnp.bfloat16)

    each(tiles, memory_tile)

    def memory_start(step, carry):
        @pl.when(seq + step < count)
        def _():
            memory_copy(step, lax.rem(seq + step, count), seq).start()

        return carry

    lax.fori_loop(1, count, memory_start, 0)

    def pre_tile(i):
        at = tile_rows(i)
        to = pl.ds(pl.multiple_of(i * TILE + HALO, HALO), TILE)
        low = normed[at, :]
        pre_ref[to, :inner] = matmul(low, input_weight[...])
        pre_ref[to, inner:] = matmul(low, maps_weight[...])

    each(tiles, lambda i: pre_tile(tiles - 1 - i))

    @pl.when(seq < count - 1)
    def _():
        halo_copy.start()

    spread_ref[...] = spread_matrix(inner, size)
    lower = jnp.where(ordered(CHUNK), 1.0, 0.0)

    def project_tile(i):
        at = tile_rows(i)
        low = normed[at, :]
        gate_z_ref[at, :] = matmul(low, gate_weight[...])
        raw = matmul(low, step_weight[...]) + bias_ref[...]
        raw_ref[at, :] = raw
        cum_ref[at, :] = jnp.dot(
            lower, rate_ref[...] * soft_plus(raw), precision=highest
        )
        value = matmul(low, query_weight[...])
        for k in range(value.shape[1] // LANES):
            part = value[:, k * LANES : (k + 1) * LANES]
            turned = part * table_ref[at, :LANES] + turn_half(part) * table_ref[at, LANES:]
            query_ref[at, k * LANES : (k + 1) * LANES] = turned.astype(jnp.bfloat16)

    each(tiles, project_tile)

    @pl.when(seq == 0)
    def _():
        pre_ref[:HALO, :] = jnp.zeros((HALO, width), jnp.float32)

    @pl.when(seq > 0)
    def _():
        halo_copy.wait_recv()

    def conv_tile(i):
        at = tile_rows(i)
        window_at = pl.ds(pl.multiple_of(i * TILE, TILE), TILE + HALO)
        seg = seg_ref[window_at, :]
        own = seg[HALO:]
        masks = [
            jnp.where(seg[HALO - 3 + k : HALO - 3 + k + TILE] == own, 1.0, 0.0) for k in range(3)
        ]
        for j in range(width // LANES):
            columns = slice(j * LANES, (j + 1) * LANES)
            window = pre_ref[window_at, columns]
            summed = taps_ref[3:4, columns] * window[HALO:]
            for k in range(3):
                summed = summed + taps_ref[k : k + 1, columns] * (
                    window[HALO - 3 + k : HALO - 3 + k + TILE] * masks[k]
                )
            conv_ref[at, columns] = summed
            act[at, columns] = summed * sigmoid(summed)

    each(tiles, conv_tile)
    local[...] = jnp.zeros_like(local)
    total[...] = jnp.ones_like(total)

    def input_map(at):
        return act[at, inner : inner + state_width].astype(jnp.bfloat16)

    def output_map(at):
        return act[at, inner + state_width :].astype(jnp.bfloat16)

    def local_chunk(c):
        at = tile_rows(c)
        _, start, end = chunk_flags(seg_ref, c)
        cum = cum_ref[at, :]
        last = cum[CHUNK - 1 :]
        spread = spread_ref[...]
        value = act[at, :inner] * spread_heads(soft_plus(raw_ref[at, :]), spread)
        scaled[at, :] = value.astype(jnp.bfloat16)
        weight = spread_heads(jnp.exp(last - cum) * end, spread)
        fresh = matmul_first(input_map(at), (value * weight).astype(jnp.bfloat16))
        keep = jnp.broadcast_to(jnp.exp(last) * start[CHUNK - 1 :], (HALO, LANES))
        keep = spread_heads(keep, spread)
        added[c] = fresh
        decay[c] = keep
        local[...] = local[...] * keep[:1] + fresh
        total[...] = total[...] * keep

    each(tiles, local_chunk)
    pieces = inner // PIECE

    def chain_copy(p):
        columns = pl.ds(p * PIECE, PIECE)
        return exchange(
            chain_out.at[:, columns],
            chain_in.at[:, columns],
            sem_chain.at[0, p],
            sem_chain.at[1, p],
            following,
        )

    @pl.when(seq == 0)
    def _():
        state[...] = jnp.zeros_like(state)
        chain_out[...] = local[...].astype(jnp.bfloat16)
        if count > 1:
            for p in range(pieces):
                chain_copy(p).start()

    def inside_chunk(c):
        at = tile_rows(c)
        own, _, _ = chunk_flags(seg_ref, c)
        cum = cum_ref[at, :]
        turned = cum.T
        meet = matmul_last(output_map(at), input_map(at))
        meet = jnp.where(ordered(CHUNK) & (own == own.T), meet, 0.0)
        for i in range(inner // LANES):
            columns = slice(i * LANES, (i + 1) * LANES)
            mixing = []
            for h in (2 * i, 2 * i + 1):
                gap = cum[:, h : h + 1] - turned[h : h + 1, :]
                mixing.append(meet * jnp.exp(jnp.minimum(gap, 0.0)))
            y_ref[at, columns] = matmul(
                jnp.concatenate(mixing, axis=1).astype(jnp.bfloat16),
                halves(scaled[at, columns].astype(jnp.float32), size),
            )

    each(tiles, inside_chunk)

    @pl.when(seq > 0)
    def _():
        for p in range(pieces):
            columns = pl.ds(p * PIECE, PIECE)
            chain_copy(p).wait_recv()
            came = chain_in[:, columns].astype(jnp.float32)
            state[:, columns] = came

            @pl.when(seq < count - 1)
            def _():
                chain_out[:, columns] = (
                    came * total[:1, columns] + local[:, columns]
                ).astype(jnp.bfloat16)
                chain_copy(p).start()

    def across_chunk(c):
        at = tile_rows(c)
        _, start, _ = chunk_flags(seg_ref, c)
        now = state[...]
        low = now.astype(jnp.bfloat16)
        states_ref[c] = low
        carried = spread_heads(jnp.exp(cum_ref[at, :]) * start, spread_ref[...])
        y_ref[at, :] += matmul(output_map(at), low) * carried + skip_ref[...] * act[at, :inner]
        state[...] = now * decay[c][:1] + added[c]

    each(tiles, across_chunk)
    states_ref[tiles] = state[...].astype(jnp.bfloat16)

    def memory_wait(step, carry):
        @pl.when(seq + step < count)
        def _():
            memory_copy(step, lax.rem(seq + step, count), seq).wait_send()
            memory_ref[lax.rem(seq + step, count)] = jnp.zeros(memory_ref.shape[1:], jnp.bfloat16)

        @pl.when(seq - step >= 0)
        def _():
            memory_copy(step, seq, lax.rem(seq - step + count, count)).wait_recv()

        return carry

    lax.fori_loop(1, count, memory_wait, 0)

    @pl.when(seq < count - 1)
    def _():
        halo_copy.wait_send()
        for p in range(pieces):
            chain_copy(p).wait_send()


def mixer_forward(
    tokens,
    mixer_gain,
    segments,
    table,
    mamba_gate,
    mamba_input,
    mamba_maps,
    step_weight,
    query_weight,
    memory_weight,
    taps,
    bias,
    rate,
    skip,
):
    rows, width = tokens.shape
    count = lax.axis_size("seq")
    inner = mamba_gate.shape[1]
    conv_width = taps.shape[1]
    state_width = (conv_width - inner) // 2
    query = query_weight.shape[1]
    chunks = rows // CHUNK
    pieces = inner // PIECE
    vmem = pl.BlockSpec(memory_space=pltpu.VMEM)
    low, full = jnp.bfloat16, jnp.float32
    shape = jax.ShapeDtypeStruct
    return pl.pallas_call(
        functools.partial(mixer_kernel, HD),
        out_shape=[
            shape((rows, inner), full),
            shape((rows + HALO, conv_width), full),
            shape((rows, conv_width), full),
            shape((rows, LANES), full),
            shape((rows, LANES), full),
            shape((rows, inner), full),
            shape((chunks + 1, state_width, inner), low),
            shape((rows, query), low),
            shape((count, rows, memory_weight.shape[1]), low),
        ],
        in_specs=[vmem] * 14,
        out_specs=[vmem] * 9,
        scratch_shapes=[
            pltpu.VMEM((rows, width), low),
            pltpu.VMEM((LANES, inner), low),
            pltpu.VMEM((rows, conv_width), full),
            pltpu.VMEM((rows, inner), low),
            pltpu.VMEM((chunks, state_width, inner), full),
            pltpu.VMEM((chunks, HALO, inner), full),
            pltpu.VMEM((HALO, inner), full),
            pltpu.VMEM((state_width, inner), full),
            pltpu.VMEM((state_width, inner), full),
            pltpu.VMEM((state_width, inner), low),
            pltpu.VMEM((state_width, inner), low),
            pltpu.SemaphoreType.DMA((2, count)),
            pltpu.SemaphoreType.DMA((2,)),
            pltpu.SemaphoreType.DMA((2, pieces)),
        ],
        compiler_params=pltpu.CompilerParams(
            collective_id=2, has_side_effects=True, vmem_limit_bytes=60 << 20
        ),
        name="mixer_forward",
    )(
        tokens,
        mixer_gain[None],
        segments,
        table,
        mamba_gate,
        mamba_input,
        mamba_maps,
        step_weight,
        query_weight,
        memory_weight,
        taps,
        bias,
        rate,
        skip,
    )


KEY_TILE = 256


def stacked_heads(values, first, factor):
    lane = lax.broadcasted_iota(jnp.int32, (values.shape[0], LANES), 1)
    keep = (lane < HD) if first else (lane >= HD)
    parts = []
    for h in range(values.shape[1] // HD):
        tile = values[:, (h // 2) * LANES : (h // 2 + 1) * LANES].astype(jnp.float32)
        if (h % 2 == 0) != first:
            tile = pltpu.roll(tile, HD, 1)
        parts.append(jnp.where(keep, tile * factor, 0.0))
    return jnp.concatenate(parts, axis=0).astype(jnp.bfloat16)


def unstacked_heads(values, rows, first):
    lane = lax.broadcasted_iota(jnp.int32, (rows, LANES), 1)
    tiles = []
    for pair in range(values.shape[0] // rows // 2):
        even = values[2 * pair * rows : (2 * pair + 1) * rows]
        odd = values[(2 * pair + 1) * rows : (2 * pair + 2) * rows]
        if first:
            odd = pltpu.roll(odd, HD, 1)
        else:
            even = pltpu.roll(even, HD, 1)
        tiles.append(jnp.where(lane < HD, even, odd))
    return tiles


def score_tile(first_ref, seg_ref, key_seg_ref, memory_ref, queries, i, k):
    heads = queries.shape[0] // TILE
    at = pl.ds(pl.multiple_of(k * KEY_TILE, KEY_TILE), KEY_TILE)
    keys = memory_ref[at, :]
    scores = matmul_last(queries, keys).reshape(heads, TILE, KEY_TILE)
    row = first_ref[0] + i * TILE + lax.broadcasted_iota(jnp.int32, (TILE, KEY_TILE), 0)
    place = k * KEY_TILE + lax.broadcasted_iota(jnp.int32, (TILE, KEY_TILE), 1)
    own = seg_ref[pl.ds(pl.multiple_of(i * TILE, TILE) + HALO, TILE), :]
    own = jnp.concatenate([own] * (KEY_TILE // LANES), axis=1)
    allowed = (place <= row) & (key_seg_ref[0:1, at] == own)
    return keys, at, scores, allowed[None]


def attention_kernel(
    first_ref, low_ref, high_ref, query_ref, memory_ref, seg_ref, key_seg_ref, out_ref, low_out_ref, log_ref
):
    rows = query_ref.shape[0]
    heads = query_ref.shape[1] // HD

    def block(i):
        at_rows = tile_rows(i)
        queries = stacked_heads(query_ref[at_rows, :], True, HD ** (-0.5))
        last = high_ref[i]

        def one(step, carry):
            most, total, acc = carry
            keys, _, scores, allowed = score_tile(
                first_ref, seg_ref, key_seg_ref, memory_ref, queries, i, last - step
            )
            scores = jnp.where(allowed, scores, neg_large).reshape(heads * TILE, KEY_TILE)
            new = jnp.maximum(most, jnp.max(scores, axis=1, keepdims=True))
            weights = jnp.exp(scores - new)
            factor = jnp.exp(most - new)
            total = total * factor + jnp.sum(weights, axis=1, keepdims=True)
            acc = acc * factor + matmul(weights.astype(jnp.bfloat16), keys)
            return new, total, acc

        most, total, acc = lax.fori_loop(
            0,
            last - low_ref[i] + 1,
            one,
            (
                jnp.full((heads * TILE, 1), neg_large, jnp.float32),
                jnp.zeros((heads * TILE, 1), jnp.float32),
                jnp.zeros((heads * TILE, LANES), jnp.float32),
            ),
        )
        for pair, tile in enumerate(unstacked_heads(acc / total, TILE, False)):
            out_ref[at_rows, pair * LANES : (pair + 1) * LANES] = tile
            low_out_ref[at_rows, pair * LANES : (pair + 1) * LANES] = tile.astype(jnp.bfloat16)
        log = most + jnp.log(total)
        lane = lax.broadcasted_iota(jnp.int32, (TILE, LANES), 1)
        logs = jnp.zeros((TILE, LANES), jnp.float32)
        for h in range(heads):
            logs = jnp.where(lane == h, log[h * TILE : (h + 1) * TILE], logs)
        log_ref[at_rows, :] = logs

    each(rows // TILE, block)


def attention_back_kernel(
    first_ref,
    low_ref,
    high_ref,
    query_ref,
    memory_ref,
    seg_ref,
    key_seg_ref,
    out_ref,
    log_ref,
    d_out_ref,
    table_ref,
    d_query_ref,
    d_memory_ref,
    grads,
):
    rows = query_ref.shape[0]
    heads = query_ref.shape[1] // HD
    grads[...] = jnp.zeros_like(grads)

    def block(i):
        at_rows = tile_rows(i)
        queries = stacked_heads(query_ref[at_rows, :], True, HD ** (-0.5))
        d_out = d_out_ref[at_rows, :]
        outer = stacked_heads(d_out, False, 1.0)
        product = d_out * out_ref[at_rows, :]
        lane = lax.broadcasted_iota(jnp.int32, (TILE, LANES), 1)
        deltas, logs = [], []
        for h in range(heads):
            tile = product[:, (h // 2) * LANES : (h // 2 + 1) * LANES]
            mine = (lane < HD) if h % 2 == 0 else (lane >= HD)
            deltas.append(jnp.sum(jnp.where(mine, tile, 0.0), axis=1, keepdims=True))
            logs.append(log_ref[at_rows, h : h + 1])
        delta = jnp.concatenate(deltas, axis=0)
        log = jnp.concatenate(logs, axis=0)
        last = high_ref[i]

        def one(step, total):
            keys, at, scores, allowed = score_tile(
                first_ref, seg_ref, key_seg_ref, memory_ref, queries, i, last - step
            )
            weights = jnp.exp(scores - log.reshape(heads, TILE, 1))
            weights = jnp.where(allowed, weights, 0.0).reshape(heads * TILE, KEY_TILE)
            inner = matmul_last(outer, keys)
            low = (weights * (inner - delta)).astype(jnp.bfloat16)
            grads[at, :] += matmul_first(low, queries) + matmul_first(
                weights.astype(jnp.bfloat16), outer
            )
            return total + matmul(low, keys)

        total = lax.fori_loop(
            0, last - low_ref[i] + 1, one, jnp.zeros((heads * TILE, LANES), jnp.float32)
        )
        for pair, tile in enumerate(unstacked_heads(total * HD ** (-0.5), TILE, True)):
            turned = tile * table_ref[at_rows, :LANES] - turn_half(tile) * table_ref[at_rows, LANES:]
            d_query_ref[at_rows, pair * LANES : (pair + 1) * LANES] = turned.astype(jnp.bfloat16)

    each(rows // TILE, block)
    d_memory_ref[...] = grads[...].astype(jnp.bfloat16)


def attention_specs(count):
    return [pl.BlockSpec(memory_space=pltpu.SMEM)] * 3 + [
        pl.BlockSpec(memory_space=pltpu.VMEM)
    ] * count


def attention_forward(spans, query, memory, segments, key_segments):
    rows, width = query.shape
    full = jnp.float32
    return pl.pallas_call(
        attention_kernel,
        out_shape=[
            jax.ShapeDtypeStruct((rows, width), full),
            jax.ShapeDtypeStruct((rows, width), jnp.bfloat16),
            jax.ShapeDtypeStruct((rows, LANES), full),
        ],
        in_specs=attention_specs(4),
        out_specs=[pl.BlockSpec(memory_space=pltpu.VMEM)] * 3,
        compiler_params=pltpu.CompilerParams(vmem_limit_bytes=56 << 20),
        name="attention_forward",
    )(*spans, query, memory, segments, key_segments)


def attention_back(spans, query, memory, segments, key_segments, out, logs, d_out, table):
    rows, width = query.shape
    return pl.pallas_call(
        attention_back_kernel,
        out_shape=[
            jax.ShapeDtypeStruct((rows, width), jnp.bfloat16),
            jax.ShapeDtypeStruct(memory.shape, jnp.bfloat16),
        ],
        in_specs=attention_specs(8),
        out_specs=[pl.BlockSpec(memory_space=pltpu.VMEM)] * 2,
        scratch_shapes=[pltpu.VMEM(memory.shape, jnp.float32)],
        compiler_params=pltpu.CompilerParams(vmem_limit_bytes=56 << 20),
        name="attention_back",
    )(*spans, query, memory, segments, key_segments, out, logs, d_out, table)


def mixer_back_kernel(
    size,
    tokens_ref,
    gain_ref,
    seg_ref,
    table_ref,
    gate_weight,
    input_weight,
    maps_weight,
    step_weight,
    query_weight,
    memory_weight,
    taps_ref,
    rate_ref,
    skip_ref,
    pre_ref,
    conv_ref,
    raw_ref,
    cum_ref,
    y_ref,
    states_ref,
    d_second_ref,
    d_y_ref,
    d_gate_z_ref,
    d_query_ref,
    d_memory_ref,
    d_tokens_ref,
    g_side_ref,
    g_taps_ref,
    g_gain_ref,
    g_heads_ref,
    normed,
    spread_ref,
    act,
    d_act,
    d_conv,
    d_scaled,
    d_maps,
    row_term,
    added,
    local,
    total,
    state,
    skip_sum,
    side,
    chain_out,
    chain_in,
    maps_send,
    maps_recv,
    memory_recv,
    norm_send,
    norm_recv,
    sem_memory,
    sem_halo,
    sem_chain,
    sem_maps,
    sem_norm,
):
    seq, head, batch = lax.axis_index("seq"), lax.axis_index("head"), lax.axis_index("batch")
    count = lax.axis_size("seq")
    rows = tokens_ref.shape[0]
    tiles = rows // CHUNK
    inner = y_ref.shape[1]
    width = pre_ref.shape[1]
    state_width = (width - inner) // 2
    model = tokens_ref.shape[1]
    peer = peer_device()
    previous = (lax.rem(seq - 1 + count, count), head, batch)
    greet_seq(pltpu.get_barrier_semaphore(), 1)
    spread_ref[...] = spread_matrix(inner, size)
    pieces = inner // PIECE

    def chain_copy(p):
        columns = pl.ds(p * PIECE, PIECE)
        return exchange(
            chain_out.at[:, columns],
            chain_in.at[:, columns],
            sem_chain.at[0, p],
            sem_chain.at[1, p],
            previous,
        )

    def memory_copy(step):
        place = lax.rem(seq - step + count, count)
        return exchange(
            d_memory_ref.at[place],
            memory_recv.at[step - 1],
            sem_memory.at[0, step],
            sem_memory.at[1, step],
            (place, head, batch),
        )

    halo_copy = exchange(
        d_conv.at[pl.ds(0, HALO)],
        d_conv.at[pl.ds(rows, HALO)],
        sem_halo.at[0],
        sem_halo.at[1],
        previous,
    )
    maps_copy = exchange(maps_send, maps_recv, sem_maps.at[0], sem_maps.at[1], peer)

    def norm_copy(i):
        at = tile_rows(i)
        return exchange(
            norm_send.at[at], norm_recv.at[at], sem_norm.at[0, i], sem_norm.at[1, i], peer
        )

    def input_map(at):
        return act[at, inner : inner + state_width].astype(jnp.bfloat16)

    def output_map(at):
        return act[at, inner + state_width :].astype(jnp.bfloat16)

    def keep_of(c, start):
        last = cum_ref[tile_rows(c), :][CHUNK - 1 :]
        keep = jnp.broadcast_to(jnp.exp(last) * start[CHUNK - 1 :], (HALO, LANES))
        return spread_heads(keep, spread_ref[...])

    def carried_of(c, start):
        return spread_heads(jnp.exp(cum_ref[tile_rows(c), :]) * start, spread_ref[...])

    def activate(i):
        at = tile_rows(i)
        value = conv_ref[at, :]
        act[at, :] = value * sigmoid(value)

    each(tiles, activate)
    local[...] = jnp.zeros_like(local)
    total[...] = jnp.ones_like(total)

    def local_chunk(step):
        c = tiles - 1 - step
        at = tile_rows(c)
        _, start, _ = chunk_flags(seg_ref, c)
        keep = keep_of(c, start)
        value = (d_y_ref[at, :] * carried_of(c, start)).astype(jnp.bfloat16)
        fresh = matmul_first(output_map(at), value)
        added[c] = fresh
        local[...] = local[...] * keep[:1] + fresh
        total[...] = total[...] * keep

    each(tiles, local_chunk)

    @pl.when(seq == count - 1)
    def _():
        state[...] = jnp.zeros_like(state)
        chain_out[...] = local[...].astype(jnp.bfloat16)
        if count > 1:
            for p in range(pieces):
                chain_copy(p).start()

    skip_sum[...] = jnp.zeros_like(skip_sum)

    def inside_chunk(c):
        at = tile_rows(c)
        own, start, _ = chunk_flags(seg_ref, c)
        cum = cum_ref[at, :]
        turned = cum.T
        spread = spread_ref[...]
        low_in, low_out = input_map(at), output_map(at)
        allowed = ordered(CHUNK).astype(jnp.float32).T * jnp.where(own == own.T, 1.0, 0.0)
        meet = matmul_last(low_in, low_out) * allowed
        value = act[at, :inner]
        scaled = value * spread_heads(soft_plus(raw_ref[at, :]), spread)
        d_y = d_y_ref[at, :]
        d_meet = jnp.zeros((CHUNK, CHUNK), jnp.float32)
        for i in range(inner // LANES):
            columns = slice(i * LANES, (i + 1) * LANES)
            d_tile = d_y[:, columns]
            d_mixing = matmul_last(halves(scaled[:, columns], size), d_tile.astype(jnp.bfloat16))
            mixing = []
            for k, h in enumerate((2 * i, 2 * i + 1)):
                gap = turned[h : h + 1, :] - cum[:, h : h + 1]
                fade = jnp.exp(jnp.minimum(gap, 0.0))
                mixing.append(meet * fade)
                d_meet = d_meet + d_mixing[k * CHUNK : (k + 1) * CHUNK] * fade
            d_scaled[at, columns] = matmul(
                jnp.concatenate(mixing, axis=1).astype(jnp.bfloat16), halves(d_tile, size)
            )
        d_meet = (d_meet * allowed).astype(jnp.bfloat16)
        d_maps[at, :state_width] = matmul(d_meet, low_out)
        carried = (d_y * carried_of(c, start)).astype(jnp.bfloat16)
        d_maps[at, state_width:] = matmul_first(d_meet, low_in) + matmul_last(
            carried, states_ref[c]
        )
        product = d_y * value
        skip_sum[...] += jnp.sum(product, axis=0, keepdims=True)
        low = d_y.astype(jnp.bfloat16).astype(jnp.float32)
        row_term[at, :] = sum_heads(low * (y_ref[at, :] - skip_ref[...] * value), spread)

    each(tiles, inside_chunk)

    @pl.when(seq < count - 1)
    def _():
        for p in range(pieces):
            columns = pl.ds(p * PIECE, PIECE)
            chain_copy(p).wait_recv()
            came = chain_in[:, columns].astype(jnp.float32)
            state[:, columns] = came

            @pl.when(seq > 0)
            def _():
                chain_out[:, columns] = (
                    came * total[:1, columns] + local[:, columns]
                ).astype(jnp.bfloat16)
                chain_copy(p).start()

    def memory_start(step, carry):
        @pl.when(seq - step >= 0)
        def _():
            memory_copy(step).start()

        return carry

    lax.fori_loop(1, count, memory_start, 0)
    g_heads_ref[...] = jnp.zeros_like(g_heads_ref)
    upper = jnp.where(ordered(CHUNK), 1.0, 0.0).T

    def across_chunk(step):
        c = tiles - 1 - step
        at = tile_rows(c)
        _, start, end = chunk_flags(seg_ref, c)
        spread = spread_ref[...]
        cum = cum_ref[at, :]
        last = cum[CHUNK - 1 :]
        now = state[...]
        low = now.astype(jnp.bfloat16)
        raw = raw_ref[at, :]
        steps = soft_plus(raw)
        steps_wide = spread_heads(steps, spread)
        value = act[at, :inner]
        scaled = value * steps_wide
        weight = spread_heads(jnp.exp(last - cum) * end, spread)
        d_value = d_scaled[at, :] + matmul(input_map(at), low) * weight
        d_maps[at, :state_width] += matmul_last((scaled * weight).astype(jnp.bfloat16), low)
        final = jnp.sum(
            states_ref[c + 1].astype(jnp.float32) * low.astype(jnp.float32), axis=0, keepdims=True
        )
        final = sum_heads(jnp.broadcast_to(final, (HALO, inner)), spread)[:1]
        low_scaled = scaled.astype(jnp.bfloat16).astype(jnp.float32)
        d_cum = row_term[at, :] - sum_heads(low_scaled * d_value, spread)
        d_rate = jnp.dot(upper, d_cum, precision=highest) + final
        rate = rate_ref[...]
        d_steps = sum_heads(value * d_value, spread) + rate * d_rate
        d_raw = d_steps * sigmoid(raw)
        g_heads_ref[0:1, :] += rate * jnp.sum(steps * d_rate, axis=0, keepdims=True)
        g_heads_ref[1:2, :] += jnp.sum(d_raw, axis=0, keepdims=True)
        side[at, 2 * inner + 2 * state_width : 2 * inner + 2 * state_width + LANES] = d_raw.astype(
            jnp.bfloat16
        )
        d_act[at, :inner] = steps_wide * d_value + skip_ref[...] * d_y_ref[at, :]
        state[...] = now * keep_of(c, start)[:1] + added[c]

    each(tiles, across_chunk)
    g_heads_ref[2:3, :] = sum_heads(jnp.broadcast_to(skip_sum[:1], (HALO, inner)), spread_ref[...])[
        :1
    ]
    maps_send[...] = d_maps[...].astype(jnp.bfloat16)
    maps_copy.start()

    def copy_tile(i):
        at = tile_rows(i)
        side[at, :inner] = d_gate_z_ref[at, :]
        hidden = tokens_ref[at, :].astype(jnp.float32)
        inverse = lax.rsqrt(jnp.mean(hidden * hidden, axis=1, keepdims=True) + eps_norm)
        normed[at, :] = (hidden * inverse * gain_ref[...]).astype(jnp.bfloat16)

    each(tiles, copy_tile)
    maps_copy.wait()

    def conv_back_tile(i):
        at = tile_rows(i)
        d_act[at, inner:] = maps_send[at, :].astype(jnp.float32) + maps_recv[at, :].astype(
            jnp.float32
        )
        value = conv_ref[at, :]
        sig = sigmoid(value)
        d_conv[at, :] = d_act[at, :] * (sig * (1.0 + value * (1.0 - sig)))

    each(tiles, conv_back_tile)

    @pl.when(seq > 0)
    def _():
        halo_copy.start()

    @pl.when(seq == count - 1)
    def _():
        d_conv[pl.ds(rows, HALO), :] = jnp.zeros((HALO, width), jnp.float32)

    @pl.when(seq < count - 1)
    def _():
        halo_copy.wait_recv()

    g_taps_ref[...] = jnp.zeros_like(g_taps_ref)

    def taps_tile(i):
        at = tile_rows(i)
        window_at = pl.ds(pl.multiple_of(i * TILE, TILE), TILE + HALO)
        seg = seg_ref[pl.ds(pl.multiple_of(i * TILE, TILE), TILE + 2 * HALO), :]
        own = seg[HALO : HALO + TILE]
        before = [
            jnp.where(seg[HALO - 3 + k : HALO - 3 + k + TILE] == own, 1.0, 0.0) for k in range(3)
        ]
        after = [
            jnp.where(seg[HALO + 3 - k : HALO + 3 - k + TILE] == own, 1.0, 0.0) for k in range(3)
        ]
        for j in range(width // LANES):
            columns = slice(j * LANES, (j + 1) * LANES)
            window = pre_ref[window_at, columns]
            grads = d_conv[window_at, columns]
            own_grad = grads[:TILE]
            summed = taps_ref[3:4, columns] * own_grad
            g_taps_ref[3:4, columns] += jnp.sum(own_grad * window[HALO:], axis=0, keepdims=True)
            for k in range(3):
                summed = summed + taps_ref[k : k + 1, columns] * (
                    grads[3 - k : 3 - k + TILE] * after[k]
                )
                g_taps_ref[k : k + 1, columns] += jnp.sum(
                    own_grad * (window[HALO - 3 + k : HALO - 3 + k + TILE] * before[k]),
                    axis=0,
                    keepdims=True,
                )
            side[at, inner + j * LANES : inner + (j + 1) * LANES] = summed.astype(jnp.bfloat16)

    each(tiles, taps_tile)
    query_at = 2 * inner + 2 * state_width + LANES
    query_width = d_query_ref.shape[1]
    memory_at = query_at + query_width

    def memory_wait(step, carry):
        @pl.when(seq - step >= 0)
        def _():
            memory_copy(step).wait_send()

        @pl.when(seq + step < count)
        def _():
            memory_copy(step).wait_recv()

        return carry

    lax.fori_loop(1, count, memory_wait, 0)

    def memory_tile(i):
        at = tile_rows(i)

        def one(step, carry):
            came = memory_recv[step - 1, at, :].astype(jnp.float32)
            return carry + jnp.where(seq + step < count, came, 0.0)

        grad = lax.fori_loop(1, count, one, d_memory_ref[seq, at, :].astype(jnp.float32))
        lane = lax.broadcasted_iota(jnp.int32, grad.shape, 1)
        turned = grad * table_ref[at, :LANES] - turn_half(grad) * table_ref[at, LANES:]
        side[at, memory_at : memory_at + LANES] = jnp.where(lane < HD, turned, grad).astype(
            jnp.bfloat16
        )
        side[at, query_at:memory_at] = d_query_ref[at, :]

    each(tiles, memory_tile)

    def norm_tile(i):
        at = tile_rows(i)
        maps_at = 2 * inner
        step_at = maps_at + 2 * state_width
        part = (
            matmul_last(side[at, :inner], gate_weight[...])
            + matmul_last(side[at, inner:maps_at], input_weight[...])
            + matmul_last(side[at, maps_at:step_at], maps_weight[...]) / lax.axis_size("head")
            + matmul_last(side[at, step_at:query_at], step_weight[...])
            + matmul_last(side[at, query_at:memory_at], query_weight[...])
            + matmul_last(side[at, memory_at:], memory_weight[...])
        )
        norm_send[at, :] = part.astype(jnp.bfloat16)
        norm_copy(i).start()

    each(tiles, norm_tile)

    def weight_block(k):
        block = pl.ds(pl.multiple_of(k * 256, 256), 256)
        g_side_ref[block, :] = matmul_first(normed[:, block], side[...]).astype(jnp.bfloat16)

    each(model // 256, weight_block)
    g_gain_ref[...] = jnp.zeros_like(g_gain_ref)

    def last_tile(i):
        at = tile_rows(i)
        norm_copy(i).wait()
        d_norm = norm_send[at, :].astype(jnp.float32) + norm_recv[at, :].astype(jnp.float32)
        hidden = tokens_ref[at, :].astype(jnp.float32)
        inverse = lax.rsqrt(jnp.mean(hidden * hidden, axis=1, keepdims=True) + eps_norm)
        e_one = d_norm * gain_ref[...]
        cross = jnp.sum(e_one * hidden, axis=1, keepdims=True) / model
        d_tokens_ref[at, :] = (
            d_second_ref[at, :] + inverse * e_one - hidden * (inverse * inverse * inverse * cross)
        )
        g_gain_ref[...] += jnp.sum(d_norm * hidden * inverse, axis=0, keepdims=True)

    each(tiles, last_tile)

    @pl.when(seq > 0)
    def _():
        halo_copy.wait_send()
        for p in range(pieces):
            chain_copy(p).wait_send()


def mixer_back(
    tokens,
    mixer_gain,
    segments,
    table,
    mamba_gate,
    mamba_input,
    mamba_maps,
    step_weight,
    query_weight,
    memory_weight,
    taps,
    rate,
    skip,
    *saved,
):
    rows, model = tokens.shape
    count = lax.axis_size("seq")
    inner = mamba_gate.shape[1]
    width = taps.shape[1]
    state_width = (width - inner) // 2
    chunks = rows // CHUNK
    pieces = inner // PIECE
    side = 2 * inner + 2 * state_width + LANES + query_weight.shape[1] + memory_weight.shape[1]
    vmem = pl.BlockSpec(memory_space=pltpu.VMEM)
    low, full = jnp.bfloat16, jnp.float32
    shape = jax.ShapeDtypeStruct
    return pl.pallas_call(
        functools.partial(mixer_back_kernel, HD),
        out_shape=[
            shape((rows, model), full),
            shape((model, side), low),
            shape((HALO, width), full),
            shape((1, model), full),
            shape((HALO, LANES), full),
        ],
        in_specs=[vmem] * (13 + len(saved)),
        out_specs=[vmem] * 5,
        scratch_shapes=[
            pltpu.VMEM((rows, model), low),
            pltpu.VMEM((LANES, inner), low),
            pltpu.VMEM((rows, width), full),
            pltpu.VMEM((rows, width), full),
            pltpu.VMEM((rows + HALO, width), full),
            pltpu.VMEM((rows, inner), full),
            pltpu.VMEM((rows, 2 * state_width), full),
            pltpu.VMEM((rows, LANES), full),
            pltpu.VMEM((chunks, state_width, inner), full),
            pltpu.VMEM((state_width, inner), full),
            pltpu.VMEM((HALO, inner), full),
            pltpu.VMEM((state_width, inner), full),
            pltpu.VMEM((1, inner), full),
            pltpu.VMEM((rows, side), low),
            pltpu.VMEM((state_width, inner), low),
            pltpu.VMEM((state_width, inner), low),
            pltpu.VMEM((rows, 2 * state_width), low),
            pltpu.VMEM((rows, 2 * state_width), low),
            pltpu.VMEM((max(count - 1, 1), rows, memory_weight.shape[1]), low),
            pltpu.VMEM((rows, model), low),
            pltpu.VMEM((rows, model), low),
            pltpu.SemaphoreType.DMA((2, count)),
            pltpu.SemaphoreType.DMA((2,)),
            pltpu.SemaphoreType.DMA((2, pieces)),
            pltpu.SemaphoreType.DMA((2,)),
            pltpu.SemaphoreType.DMA((2, chunks)),
        ],
        compiler_params=pltpu.CompilerParams(
            collective_id=3, has_side_effects=True, vmem_limit_bytes=60 << 20
        ),
        name="mixer_back",
    )(
        tokens,
        mixer_gain[None],
        segments,
        table,
        mamba_gate,
        mamba_input,
        mamba_maps,
        step_weight,
        query_weight,
        memory_weight,
        taps,
        rate,
        skip,
        *saved,
    )


def rotation_table(position):
    half = HD // 2
    lane = jnp.arange(LANES)
    inverse_freq = rope_base ** (-(lane % half).astype(jnp.float32) / half)
    angles = position.astype(jnp.float32)[:, None] * inverse_freq[None, :]
    sign = jnp.where(lane % HD < half, -1.0, 1.0)
    return jnp.concatenate([jnp.cos(angles), sign[None, :] * jnp.sin(angles)], axis=1)


def body(
    tokens,
    seg_ids,
    mixer_gain,
    mamba_gate,
    mamba_input,
    mamba_maps,
    mamba_step,
    conv_inner,
    conv_maps,
    log_rate,
    step_bias,
    skip_gain,
    mamba_gain,
    mamba_output,
    query_weight,
    memory_weight,
    attention_out,
    feed_gain,
    gate_weight,
    lift_weight,
    down_weight,
    cotangent,
):
    tokens, cotangent = tokens[0], cotangent[0]
    rows, wide = tokens.shape
    tap_count, inner = conv_inner.shape
    head_count = log_rate.shape[0]
    segments = seg_ids[0]
    offset = lax.axis_index("seq") * rows
    padded = jnp.concatenate(
        [jnp.full((HALO,), -1, jnp.int32), segments, jnp.full((HALO,), -2, jnp.int32)]
    )
    window = lax.dynamic_slice_in_dim(padded, offset, rows + 2 * HALO)
    window_wide = jnp.broadcast_to(
        window.astype(jnp.float32)[:, None], (rows + 2 * HALO, LANES)
    )
    key_segments = segments.astype(jnp.float32)[None]
    table = rotation_table(offset + jnp.arange(rows, dtype=jnp.int32))
    starts = offset + jnp.arange(rows // TILE, dtype=jnp.int32) * TILE
    reach = segments[KEY_TILE - 1 :: KEY_TILE]
    low = jnp.sum(
        (reach[None, :] < window[HALO : HALO + rows : TILE][:, None]).astype(jnp.int32), axis=1
    )
    spans = (offset[None], low, (starts + TILE - 1) // KEY_TILE)

    def lanes_of(values):
        return jnp.pad(values, (0, LANES - head_count))[None]

    step_weight = jnp.pad(mamba_step, ((0, 0), (0, LANES - head_count)))
    taps = jnp.pad(
        jnp.concatenate([conv_inner, conv_maps], axis=1), ((0, HALO - tap_count), (0, 0))
    )
    bias, rate = lanes_of(step_bias), lanes_of(-jnp.exp(log_rate))
    skip = jnp.repeat(skip_gain, inner // head_count)[None]
    gate_z, pre, conv, raw, cum, y, states, query, memory = mixer_forward(
        tokens,
        mixer_gain,
        window_wide,
        table,
        mamba_gate,
        mamba_input,
        mamba_maps,
        step_weight,
        query_weight,
        memory_weight,
        taps,
        bias,
        rate,
        skip,
    )
    all_memory = memory.reshape(memory.shape[0] * rows, memory.shape[2])
    attention, attention_low, logs = attention_forward(
        spans, query, all_memory, window_wide, key_segments
    )
    (
        layer_out,
        d_second,
        d_y,
        d_gate_z,
        d_attention,
        g_feed,
        g_mixed,
        g_down,
        g_feed_gain,
        g_mamba_gain,
    ) = feed_layer(
        y,
        gate_z,
        attention_low,
        tokens,
        cotangent,
        mamba_gain,
        feed_gain,
        mamba_output,
        attention_out,
        gate_weight,
        lift_weight,
        down_weight,
    )
    d_query, d_memory = attention_back(
        spans, query, all_memory, window_wide, key_segments, attention, logs, d_attention, table
    )
    grad_tokens, g_side, g_taps, g_mixer_gain, g_heads = mixer_back(
        tokens,
        mixer_gain,
        window_wide,
        table,
        mamba_gate,
        mamba_input,
        mamba_maps,
        step_weight,
        query_weight,
        memory_weight,
        taps,
        rate,
        skip,
        pre,
        conv,
        raw,
        cum,
        y,
        states,
        d_second,
        d_y,
        d_gate_z,
        d_query,
        d_memory.reshape(memory.shape),
    )
    small = jnp.concatenate(
        [
            g_taps[:tap_count],
            jnp.pad(g_mamba_gain, ((0, 0), (0, wide - inner))),
            g_mixer_gain,
            g_feed_gain,
            jnp.pad(g_heads[:3].reshape(1, 3 * LANES), ((0, 0), (0, wide - 3 * LANES))),
        ],
        axis=0,
    )
    (mixer_sum, feed_sum, mixed_sum, down_sum), small = reduce_gradients(
        [g_side, g_feed, g_mixed, g_down], small
    )
    edges = [0]
    for width in (
        inner,
        inner,
        conv_maps.shape[1],
        LANES,
        query_weight.shape[1],
        memory_weight.shape[1],
    ):
        edges.append(edges[-1] + width)
    pieces = [mixer_sum[:, a:b].astype(jnp.float32) for a, b in zip(edges[:-1], edges[1:])]
    own_rows = wide // lax.axis_size("seq")
    own_at = lax.axis_index("seq") * own_rows
    feed = gate_weight.shape[1]
    return (
        layer_out[None],
        grad_tokens[None],
        lax.dynamic_slice_in_dim(small[5], own_at, own_rows),
        pieces[0],
        pieces[1],
        pieces[2],
        pieces[3][:, :head_count],
        small[:tap_count, :inner],
        small[:tap_count, inner:],
        small[7, :head_count],
        small[7, LANES : LANES + head_count],
        small[7, 2 * LANES : 2 * LANES + head_count],
        small[4, :inner],
        mixed_sum[:, :inner].astype(jnp.float32),
        pieces[4],
        pieces[5],
        mixed_sum[:, inner:].astype(jnp.float32),
        lax.dynamic_slice_in_dim(small[6], own_at, own_rows),
        feed_sum[:, :feed].astype(jnp.float32),
        feed_sum[:, feed:].astype(jnp.float32),
        down_sum.astype(jnp.float32),
    )


def solution(mesh):
    return jax.shard_map(
        body,
        mesh=mesh,
        in_specs=(
            P("batch", "seq", None),
            P("batch", None),
            P(),
            P(None, "head"),
            P(None, "head"),
            P(),
            P(None, "head"),
            P(None, "head"),
            P(),
            P("head"),
            P("head"),
            P("head"),
            P("head"),
            P(None, "head"),
            P(None, "head"),
            P(None, "head"),
            P(None, "head"),
            P(),
            P(None, "head"),
            P(None, "head"),
            P(None, "head"),
            P("batch", "seq", None),
        ),
        out_specs=(
            P("batch", "seq", None),
            P("batch", "seq", None),
            P("seq"),
            P("seq", "head"),
            P("seq", "head"),
            P("seq", None),
            P("seq", "head"),
            P(None, "head"),
            P(),
            P("head"),
            P("head"),
            P("head"),
            P("head"),
            P("seq", "head"),
            P("seq", "head"),
            P("seq", "head"),
            P("seq", "head"),
            P("seq"),
            P("seq", "head"),
            P("seq", "head"),
            P("seq", "head"),
        ),
        check_vma=False,
    )
```

time: 707 us -> 368 us (0.52); the launches traced: 697 us -> 367 us
  Pallas kernels: 161 us -> 328 us
  matrix products: 162 us -> 0 us
  blocking collectives: 105 us -> 0 us
  other arithmetic: 93.9 us -> 17.1 us
  local copies, waits for them, and re-layouts: 81.3 us -> 21 us
  waiting for transfers between devices: 58.7 us -> 0 us
  between operations: 17 us -> 0.76 us
  loops' own time: 10.1 us -> 0 us
  starting transfers between devices: 8 us -> 0 us
    pallas_call x0 -> x5, Pallas kernels: none -> 161 us  [the longest x1 85 us: mixer_back(): pl.pallas_call(functools.partial(mixer_back_kernel, HD), out_shape=[shape...]
    dot_general x44 -> x0, matrix products: 159 us -> none  [the longest x3 53.6 us: output_part(): inside = jnp.einsum('tsh,shp->thp', mixing, scan_input, precision=highest)]
    all_gather x5 -> x0, blocking collectives: 101 us -> none  [the longest x2 52 us: entering(): lax.all_gather(part.astype(kind), axis)]
    psum x4 -> x0, waiting for transfers between devices: 30.3 us -> none  [the longest x3 30.3 us: head_total(): lax.psum(partial_sum.astype(jnp.bfloat16), 'head').astype(jnp.float32)]
    dynamic_slice x25 -> x1, local copies, waits for them, and re-layouts: 27.8 us -> 0.56 us  [body(): lax.dynamic_slice_in_dim(small[5], own_at, own_rows)]
    reduce_sum x13 -> x1, other arithmetic: 24.6 us -> 0.7 us  [body(): jnp.sum((reach[None, :] < window[HALO:HALO + rows:TILE][:, None]).astype(...]
    reduce_scatter x1 -> x0, waiting for transfers between devices: 20.7 us -> none  [body(): lax.psum_scatter(pair_blocks.reshape(total_rows, memory_heads * 2 * HD).a...]
    another operation x15 -> x0, other arithmetic: 15.7 us -> none
  transfers between devices with their start and end apart: 7 -> 0, of which waited for: 4 -> 0; matrix products, arithmetic and copies ran while one was open for 15% -> 0% of each run, Pallas kernels for 0% -> 0%
where the time goes in v2:
time: 368 us; the launch traced here: 367 us
  Pallas kernels  328 us (89%)
  local copies, waits for them, and re-layouts  21 us (6%)
  other arithmetic  17.1 us (5%)
    pallas_call x1, Pallas kernels, reduce_gradients(): pl.pallas_call(functools.partial(reduce_kernel, seq_count, batch_count, c...  167 us
    pallas_call x1, Pallas kernels, mixer_back(): pl.pallas_call(functools.partial(mixer_back_kernel, HD), out_shape=[shape...  85 us
    pallas_call x1, Pallas kernels, feed_layer(): pl.pallas_call(feed_kernel, out_shape=[shape((rows, width), low), shape((...  36 us
    pallas_call x1, Pallas kernels, mixer_forward(): pl.pallas_call(functools.partial(mixer_kernel, HD), out_shape=[shape((row...  26.6 us
    pallas_call x1, Pallas kernels, attention_back(): pl.pallas_call(attention_back_kernel, out_shape=[jax.ShapeDtypeStruct((ro...  7.42 us

profile of v2, /device:TPU:0, one launch (start us, length us, event | category | flops | bytes accessed | tf_op | source)
XLA Modules:
  0.0 366.6 jit_solution(10600517510311353137)
XLA Ops:
  2.6 1.2 pad_bitcast_fusion
  3.8 1.3 broadcast_in_dim.56.mamba_gain_ref
  5.1 1.3 convert_element_type.73.key_seg_ref
  9.4 1.3 select_maximum_fusion.taps_ref
  13.3 1.0 multiply_cosine_fusion
  15.1 26.6 %mixer_forward.1 = (f32[512,768]{1,0:T(8,128)}, f32[520,1024]{1,0:T(8,128)}, f32[512,1024]{1,0:T(8,128)}, f32[512,128]{1,0:T(8,128)}, f32[512,128]{1,0:T(8,128)}...) custom-call(bf16[512,1024]{1,0:T(8,128)(2,1)} %bitcast.38, ...), custom_call_target="tpu_custom_call" | custom-call | tf_op jit(solution)/shard_map/mixer_forward/pallas_call | solution.py:960
  41.8 5.6 %attention_forward.1 = (f32[512,256]{1,0:T(8,128)}, bf16[512,256]{1,0:T(8,128)(2,1)}, f32[512,128]{1,0:T(8,128)}) custom-call(s32[1]{0:T(128)} %bitcast.5.first_ref, s32[4]{0:T(128)} %convert_reduce_fusion.low_ref, s32[4]{0:T(128)} %and_select_fusion.high_ref, bf16[512,256]{1,0:T(8,128)(2,1)} %get-tuple-element.57.query_ref, bf16[2048,128]{1,0:T(8,128)(2,1)} %bitcast.46, ...), custom_call_target="tpu_custom_call" | custom-call | tf_op jit(solution)/shard_map/attention_forward/pallas_call | solution.py:1172
  47.4 36.0 %feed_layer.1 = (bf16[512,1024]{1,0:T(8,128)(2,1)}, f32[512,1024]{1,0:T(8,128)}, f32[512,768]{1,0:T(8,128)}, bf16[512,768]{1,0:T(8,128)(2,1)}, f32[512,256]{1,0:...) custom-call(f32[512,768]{1,0:T(8,128)} %get-tuple-element.55.y_ref, ...), custom_call_target="tpu_custom_call" | custom-call | tf_op jit(solution)/shard_map/feed_layer/pallas_call | solution.py:530
  83.5 7.4 %attention_back.1 = (bf16[512,256]{1,0:T(8,128)(2,1)}, bf16[2048,128]{1,0:T(8,128)(2,1)}) custom-call(s32[1]{0:T(128)} %bitcast.5.first_ref, s32[4]{0:T(128)} %convert_reduce_fusion.low_ref, s32[4]{0:T(128)} %and_select_fusion.high_ref, bf16[512,256]{1,0:T(8,128)(2,1)} %get-tuple-element.57.query_ref, bf16[2048,128]{1,0:T(8,128)(2,1)} %bitcast.47, ...), custom_call_target="tpu_custom_call" | custom-call | tf_op jit(solution)/shard_map/attention_back/pallas_call | solution.py:1188
  90.9 85.0 %mixer_back.1 = (f32[512,1024]{1,0:T(8,128)}, bf16[1024,2304]{1,0:T(8,128)(2,1)}, f32[8,1024]{1,0:T(8,128)}, f32[1,1024]{1,0:T(1,128)}, f32[8,128]{1,0:T(8,128)}) custom-call(bf16[512,1024]{1,0:T(8,128)(2,1)} %bitcast.40, f32[1,1024]{1,0:T(1,128)} %bitcast.61, f32[528,128]{1,0:T(8,128)} %broadcast_in_dim.49.seg_ref, f32[512,256]{1,0:T(8,128)} %pad_maximum_fusion.table_ref, ...), custom_call_target="tpu_custom_call" | custom-call | tf_op jit(solution)/shard_map/mixer_back/pallas_call | solution.py:1634
  177.3 1.3 concatenate.15.refs_4_
  178.6 166.9 %reduce_gradients.1 = (bf16[2,2,64,2304]{3,2,1,0:T(8,128)(2,1)}, bf16[2,2,64,2048]{3,2,1,0:T(8,128)(2,1)}, bf16[2,2,64,1024]{3,2,1,0:T(8,128)(2,1)}, bf16[2,2,64,1024]{3,2,1,0:T(8,128)(2,1)}, f32[8,1024]{1,0:T(8,128)}) custom-call(bf16[4,2,2,64,2304]{4,3,2,1,0:T(8,128)(2,1)} %bitcast.41, bf16[4,2,2,64,2048]{4,3,2,1,0:T(8,128)(2,1)} %bitcast.42, ...), custom_call_target="tpu_custom_call" | custom-call | tf_op jit(solution)/shard_map/reduce_gradients/pallas_call | solution.py:232
  345.6 1.3 slice_bitcast_fusion.1
  346.9 1.3 slice_reduce_fusion
  348.2 1.3 slice.82
  350.4 1.3 slice.81
  354.4 1.5 slice_convert_fusion.8
  355.9 1.6 slice_convert_fusion.5
  357.5 2.0 slice_convert_fusion.2
  360.3 1.2 slice_convert_fusion.3
  361.6 1.1 bitcast_convert_fusion
  362.7 1.6 slice_convert_fusion
  364.3 1.0 copy.52
  365.2 1.3 copy.53
  (42 shorter events, 14.2 us)
Async XLA Ops:
  90.9 85.7 %copy-start.6 = (f32[1,768]{1,0:T(1,128)S(1)}, f32[1,768]{1,0:T(1,128)}, u32[]{:S(2)}) copy-start(f32[1,768]{1,0:T(1,128)} %get-tuple-element.80) | copy-start | bytes 9220
  90.9 86.4 %copy-start.5 = (f32[1,1024]{1,0:T(1,128)S(1)}, f32[1,1024]{1,0:T(1,128)}, u32[]{:S(2)}) copy-start(f32[1,1024]{1,0:T(1,128)} %get-tuple-element.82) | copy-start | bytes 12292
  345.6 13.9 %copy-start.1 = (bf16[2,2,64,2304]{3,2,1,0:T(8,128)(2,1)S(1)}, bf16[2,2,64,2304]{3,2,1,0:T(8,128)(2,1)}, u32[]{:S(2)}) copy-start(bf16[2,2,64,2304]{3,2,1,0:T(8,128)(2,1)} %get-tuple-element.85) | copy-start | bytes 3538948
  357.5 4.1 %copy-start.4 = (bf16[2,2,64,1024]{3,2,1,0:T(8,128)(2,1)S(1)}, bf16[2,2,64,1024]{3,2,1,0:T(8,128)(2,1)}, u32[]{:S(2)}) copy-start(bf16[2,2,64,1024]{3,2,1,0:T(8,128)(2,1)} %get-tuple-element.88) | copy-start | bytes 1572868
  360.3 2.4 copy-start.2
  361.6 2.7 copy-start.3
  362.7 2.5 copy-start

commit v3 on v2

--- a/solution.py
+++ b/solution.py
@@ -15,6 +15,8 @@
 
 
 LANES = 128
+MOST = 512
+AHEAD = 4
 MESH = pl.DeviceIdType.MESH
 
 
@@ -29,10 +31,18 @@
     )
 
 
-def column_chunks(widths, most):
+def each(count, action):
+    span(0, count, action)
+
+
+def span(first, last, action):
+    lax.fori_loop(first, last, lambda i, carry: (action(i), carry)[1], 0)
+
+
+def column_chunks(widths):
     chunks = []
     for group, width in enumerate(widths):
-        count = -(-width // most)
+        count = -(-width // MOST)
         tiles = width // LANES
         start = 0
         for k in range(count):
@@ -42,216 +52,295 @@
     return chunks
 
 
-def reduce_kernel(seq_count, batch_count, chunks, *refs):
+def seq_blocks(grad):
+    count = lax.axis_size("seq")
+    return grad.reshape(count, 2, 2, grad.shape[0] // count // 4, grad.shape[1])
+
+
+def peer_device():
+    return (lax.axis_index("seq"), 1 - lax.axis_index("head"), lax.axis_index("batch"))
+
+
+def other_device(step):
+    seq, batch = lax.axis_index("seq"), lax.axis_index("batch")
+    batches = lax.axis_size("batch")
+    place = lax.rem(seq * batches + batch + step, lax.axis_size("seq") * batches)
+    return (place // batches, lax.axis_index("head"), lax.rem(place, batches))
+
+
+def greet_all(barrier, with_peer):
+    world = lax.axis_size("seq") * lax.axis_size("batch")
+    span(
+        1,
+        world,
+        lambda step: pl.semaphore_signal(
+            barrier, inc=1, device_id=other_device(step), device_id_type=MESH
+        ),
+    )
+    if with_peer:
+        pl.semaphore_signal(barrier, inc=1, device_id=peer_device(), device_id_type=MESH)
+    pl.semaphore_wait(barrier, world - 1 + (1 if with_peer else 0))
+
+
+class SmallSum:
+    def __init__(self, source, slots, sems):
+        self.source, self.slots, self.sems = source, slots, sems
+        self.world = slots.shape[0]
+        self.mine = lax.axis_index("seq") * lax.axis_size("batch") + lax.axis_index("batch")
+
+    def copy(self, step):
+        return exchange(
+            self.source,
+            self.slots.at[self.mine],
+            self.sems.at[0, step],
+            self.sems.at[1, step],
+            other_device(step),
+        )
+
+    def start(self):
+        span(1, self.world, lambda step: self.copy(step).start())
+
+    def finish(self):
+        span(1, self.world, lambda step: self.copy(step).wait())
+        self.slots[self.mine] = self.source[...]
+        return lax.fori_loop(
+            1, self.world, lambda k, total: total + self.slots[k], self.slots[0]
+        )
+
+
+def small_scratch(shape):
+    world = lax.axis_size("seq") * lax.axis_size("batch")
+    return [
+        pltpu.VMEM(shape, jnp.float32),
+        pltpu.VMEM((world,) + shape, jnp.float32),
+        pltpu.SemaphoreType.DMA((2, world)),
+    ]
+
+
+class Reduction:
+    def __init__(self, chunks, sources, outs, scratch):
+        self.chunks, self.sources, self.outs = chunks, sources, outs
+        groups = len(sources)
+        scratch = list(scratch)
+        self.first, self.second, self.third = (
+            scratch[:groups],
+            scratch[groups : 2 * groups],
+            scratch[2 * groups : 3 * groups],
+        )
+        self.own, self.sem_own, self.sem_one, self.sem_two, self.sem_seq, self.sem_back = scratch[
+            3 * groups :
+        ]
+        self.count = lax.axis_size("seq")
+        self.seq, self.head = lax.axis_index("seq"), lax.axis_index("head")
+        self.batch = lax.axis_index("batch")
+        self.low, self.high = lax.rem(self.batch, 2), self.batch // 2
+        self.low_peer = (self.seq, self.head, self.batch + 1 - 2 * self.low)
+        self.high_peer = (self.seq, self.head, self.batch + 2 - 4 * self.high)
+        self.turn = self.sent = self.held = self.limit = 0
+
+    def place(self, k):
+        group, start, size = self.chunks[k]
+        return group, pl.ds(start, size)
+
+    def first_copy(self, k):
+        group, columns = self.place(k)
+        if k % 2 == 0:
+            part, peer = (
+                self.sources[group].at[:, :, 1 - self.low, :, columns],
+                self.low_peer,
+            )
+        else:
+            part, peer = (
+                self.sources[group].at[:, 1 - self.high, :, :, columns],
+                self.high_peer,
+            )
+        return exchange(
+            part,
+            self.first[group].at[:, :, :, columns],
+            self.sem_one.at[0, k],
+            self.sem_one.at[1, k],
+            peer,
+        )
+
+    def own_copy(self, k):
+        group, columns = self.place(k)
+        size = self.chunks[k][2]
+        if k % 2 == 0:
+            part = self.sources[group].at[:, :, self.low, :, columns]
+        else:
+            part = self.sources[group].at[:, self.high, :, :, columns]
+        return pltpu.make_async_copy(
+            part, self.own.at[k % 2, :, :, :, pl.ds(0, size)], self.sem_own.at[k]
+        )
+
+    def second_copy(self, k):
+        group, columns = self.place(k)
+        if k % 2 == 0:
+            away, peer = 1 - self.high, self.high_peer
+        else:
+            away, peer = 1 - self.low, self.low_peer
+        return exchange(
+            self.first[group].at[:, away, :, columns],
+            self.second[group].at[:, :, columns],
+            self.sem_two.at[0, k],
+            self.sem_two.at[1, k],
+            peer,
+        )
+
+    def seq_copy(self, k, step):
+        group, columns = self.place(k)
+        place = lax.rem(self.seq + step, self.count)
+        return exchange(
+            self.second[group].at[place, :, columns],
+            self.third[group].at[step - 1, :, columns],
+            self.sem_seq.at[0, k, step - 1],
+            self.sem_seq.at[1, k, step - 1],
+            (place, self.head, self.batch),
+        )
+
+    def back_copy(self, k, turn):
+        group, columns = self.place(k)
+        out = self.outs[group]
+        peer = self.high_peer if (k + turn) % 2 == 0 else self.low_peer
+        if turn == 0:
+            part = out.at[self.high, self.low, :, columns]
+        elif k % 2 == 0:
+            part = out.at[:, self.low, :, columns]
+        else:
+            part = out.at[self.high, :, :, columns]
+        return exchange(part, part, self.sem_back.at[0, k, turn], self.sem_back.at[1, k, turn], peer)
+
+    def add_first(self, k):
+        group, columns = self.place(k)
+        size = self.chunks[k][2]
+
+        def one(place):
+            own = self.own[k % 2, place, :, :, :size].astype(jnp.float32)
+            came = self.first[group][place, :, :, columns].astype(jnp.float32)
+            self.first[group][place, :, :, columns] = (own + came).astype(jnp.bfloat16)
+
+        each(self.count, one)
+
+    def add_second(self, k):
+        group, columns = self.place(k)
+        keep = self.high if k % 2 == 0 else self.low
+
+        def one(place):
+            own = self.first[group][place, keep, :, columns].astype(jnp.float32)
+            came = self.second[group][place, :, columns].astype(jnp.float32)
+            self.second[group][place, :, columns] = (own + came).astype(jnp.bfloat16)
+
+        each(self.count, one)
+
+    def add_third(self, k):
+        group, columns = self.place(k)
+        total = lax.fori_loop(
+            0,
+            self.count - 1,
+            lambda slot, total: total + self.third[group][slot, :, columns].astype(jnp.float32),
+            self.second[group][self.seq, :, columns].astype(jnp.float32),
+        )
+        self.outs[group][self.high, self.low, :, columns] = total.astype(jnp.bfloat16)
+
+    def refill(self):
+        while self.sent < min(self.limit, self.turn + AHEAD):
+            self.first_copy(self.sent).start()
+            self.sent += 1
+        while self.held < min(self.limit, self.turn + 2):
+            self.own_copy(self.held).start()
+            self.held += 1
+
+    def allow(self, limit):
+        self.limit = limit
+        self.refill()
+
+    def advance(self):
+        total = len(self.chunks)
+        k = self.turn
+        if k < total:
+            self.first_copy(k).wait()
+            self.own_copy(k).wait()
+            self.add_first(k)
+            self.second_copy(k).start()
+        self.turn += 1
+        self.refill()
+        k = self.turn - 2
+        if 0 <= k < total:
+            self.second_copy(k).wait()
+            self.add_second(k)
+            span(1, self.count, lambda step: self.seq_copy(k, step).start())
+        k = self.turn - 3
+        if 0 <= k < total:
+            span(1, self.count, lambda step: self.seq_copy(k, step).wait())
+            self.add_third(k)
+            self.back_copy(k, 0).start()
+        k = self.turn - 4
+        if 0 <= k < total:
+            self.back_copy(k, 0).wait()
+            self.back_copy(k, 1).start()
+        k = self.turn - 5
+        if 0 <= k < total:
+            self.back_copy(k, 1).wait()
+
+    def finish(self):
+        while self.turn < len(self.chunks) + 4:
+            self.advance()
+
+
+def reduction_scratch(chunks, widths, rows):
+    count = lax.axis_size("seq")
+    parts = len(chunks)
+    most = max(size for _, _, size in chunks)
+    low = jnp.bfloat16
+    return (
+        [pltpu.VMEM((count, 2, rows, w), low) for w in widths]
+        + [pltpu.VMEM((count, rows, w), low) for w in widths]
+        + [pltpu.VMEM((max(count - 1, 1), rows, w), low) for w in widths]
+        + [
+            pltpu.VMEM((2, count, 2, rows, most), low),
+            pltpu.SemaphoreType.DMA((parts,)),
+            pltpu.SemaphoreType.DMA((2, parts)),
+            pltpu.SemaphoreType.DMA((2, parts)),
+            pltpu.SemaphoreType.DMA((2, parts, max(count - 1, 1))),
+            pltpu.SemaphoreType.DMA((2, parts, 2)),
+        ]
+    )
+
+
+def reduce_kernel(chunks, *refs):
     count = 1 + max(c[0] for c in chunks)
-    groups, refs = refs[:count], refs[count:]
-    small_in, refs = refs[0], refs[1:]
+    sources, refs = refs[:count], refs[count:]
+    small_given, refs = refs[0], refs[1:]
     outs, refs = refs[:count], refs[count:]
-    small_out, refs = refs[0], refs[1:]
-    first_buf, refs = refs[:count], refs[count:]
-    second_buf, refs = refs[:count], refs[count:]
-    third_buf, refs = refs[:count], refs[count:]
-    small_buf, sem_one, sem_two, sem_seq, sem_back, sem_small = refs
-    seq, head, batch = lax.axis_index("seq"), lax.axis_index("head"), lax.axis_index("batch")
-    low_bit = lax.rem(batch, 2)
-    high_bit = batch // 2
-    low_peer = (seq, head, batch + 1 - 2 * low_bit)
-    high_peer = (seq, head, batch + 2 - 4 * high_bit)
-    world = seq_count * batch_count
-    mine = seq * batch_count + batch
-
-    def other(step):
-        place = lax.rem(mine + step, world)
-        return (place // batch_count, head, lax.rem(place, batch_count))
-
-    barrier = pltpu.get_barrier_semaphore()
-
-    def greet(step, carry):
-        pl.semaphore_signal(barrier, inc=1, device_id=other(step), device_id_type=MESH)
-        return carry
-
-    lax.fori_loop(1, world, greet, 0)
-    pl.semaphore_wait(barrier, world - 1)
-
-    def small_copy(step):
-        return exchange(
-            small_in,
-            small_buf.at[mine],
-            sem_small.at[0, step],
-            sem_small.at[1, step],
-            other(step),
-        )
-
-    def first_copy(k):
-        group, start, size = chunks[k]
-        columns = pl.ds(start, size)
-        source, target = groups[group], first_buf[group]
-        if k % 2 == 0:
-            part = source.at[:, :, 1 - low_bit, :, columns]
-            peer = low_peer
-        else:
-            part = source.at[:, 1 - high_bit, :, :, columns]
-            peer = high_peer
-        return exchange(part, target.at[:, :, :, columns], sem_one.at[0, k], sem_one.at[1, k], peer)
-
-    def second_copy(k):
-        group, start, size = chunks[k]
-        columns = pl.ds(start, size)
-        if k % 2 == 0:
-            away, peer = 1 - high_bit, high_peer
-        else:
-            away, peer = 1 - low_bit, low_peer
-        return exchange(
-            first_buf[group].at[:, away, :, columns],
-            second_buf[group].at[:, :, columns],
-            sem_two.at[0, k],
-            sem_two.at[1, k],
-            peer,
-        )
-
-    def seq_copy(k, step):
-        group, start, size = chunks[k]
-        columns = pl.ds(start, size)
-        place = lax.rem(seq + step, seq_count)
-        return exchange(
-            second_buf[group].at[place, :, columns],
-            third_buf[group].at[step - 1, :, columns],
-            sem_seq.at[0, k, step - 1],
-            sem_seq.at[1, k, step - 1],
-            (place, head, batch),
-        )
-
-    def back_copy(k, turn):
-        group, start, size = chunks[k]
-        columns = pl.ds(start, size)
-        out = outs[group]
-        if (k + turn) % 2 == 0:
-            peer = high_peer
-        else:
-            peer = low_peer
-        if turn == 0:
-            part = out.at[high_bit, low_bit, :, columns]
-        elif k % 2 == 0:
-            part = out.at[:, low_bit, :, columns]
-        else:
-            part = out.at[high_bit, :, :, columns]
-        return exchange(part, part, sem_back.at[0, k, turn], sem_back.at[1, k, turn], peer)
-
-    def each_seq(action):
-        lax.fori_loop(1, seq_count, lambda step, carry: (action(step), carry)[1], 0)
-
-    def add_first(k):
-        group, start, size = chunks[k]
-        columns = pl.ds(start, size)
-
-        def one(place, carry):
-            if k % 2 == 0:
-                own = groups[group][place, :, low_bit, :, columns]
-            else:
-                own = groups[group][place, high_bit, :, :, columns]
-            came = first_buf[group][place, :, :, columns]
-            first_buf[group][place, :, :, columns] = (
-                own.astype(jnp.float32) + came.astype(jnp.float32)
-            ).astype(jnp.bfloat16)
-            return carry
-
-        lax.fori_loop(0, seq_count, one, 0)
-
-    def add_second(k):
-        group, start, size = chunks[k]
-        columns = pl.ds(start, size)
-        keep = high_bit if k % 2 == 0 else low_bit
-
-        def one(place, carry):
-            own = first_buf[group][place, keep, :, columns]
-            came = second_buf[group][place, :, columns]
-            second_buf[group][place, :, columns] = (
-                own.astype(jnp.float32) + came.astype(jnp.float32)
-            ).astype(jnp.bfloat16)
-            return carry
-
-        lax.fori_loop(0, seq_count, one, 0)
-
-    def add_third(k):
-        group, start, size = chunks[k]
-        columns = pl.ds(start, size)
-
-        def one(slot, total):
-            return total + third_buf[group][slot, :, columns].astype(jnp.float32)
-
-        total = second_buf[group][seq, :, columns].astype(jnp.float32)
-        total = lax.fori_loop(0, seq_count - 1, one, total)
-        outs[group][high_bit, low_bit, :, columns] = total.astype(jnp.bfloat16)
-
-    total_chunks = len(chunks)
-    ahead = 3
-    for k in range(min(ahead, total_chunks)):
-        first_copy(k).start()
-    lax.fori_loop(1, world, lambda step, carry: (small_copy(step).start(), carry)[1], 0)
-    for turn in range(total_chunks + 4):
-        k = turn
-        if k < total_chunks:
-            first_copy(k).wait()
-            if k + ahead < total_chunks:
-                first_copy(k + ahead).start()
-            add_first(k)
-            second_copy(k).start()
-        k = turn - 1
-        if 0 <= k < total_chunks:
-            second_copy(k).wait()
-            add_second(k)
-            each_seq(lambda step: seq_copy(k, step).start())
-        k = turn - 2
-        if 0 <= k < total_chunks:
-            each_seq(lambda step: seq_copy(k, step).wait())
-            add_third(k)
-            back_copy(k, 0).start()
-        k = turn - 3
-        if 0 <= k < total_chunks:
-            back_copy(k, 0).wait()
-            back_copy(k, 1).start()
-        k = turn - 4
-        if 0 <= k < total_chunks:
-            back_copy(k, 1).wait()
-    lax.fori_loop(1, world, lambda step, carry: (small_copy(step).wait(), carry)[1], 0)
-    small_buf[mine] = small_in[...]
-    small_out[...] = lax.fori_loop(
-        1, world, lambda place, total: total + small_buf[place], small_buf[0]
-    )
-
-
-def reduce_gradients(groups, small):
-    seq_count, batch_count = lax.axis_size("seq"), lax.axis_size("batch")
-    world = seq_count * batch_count
-    rows = groups[0].shape[0] // world
-    widths = [g.shape[1] for g in groups]
-    chunks = column_chunks(widths, 512)
-    blocks = [g.reshape(seq_count, 2, 2, rows, g.shape[1]) for g in groups]
+    small_out, small_in, small_buf, sem_small, *refs = refs
+    greet_all(pltpu.get_barrier_semaphore(), False)
+    reduction = Reduction(chunks, sources, outs, refs)
+    reduction.allow(len(chunks))
+    small_in[...] = small_given[...]
+    small_sum = SmallSum(small_in, small_buf, sem_small)
+    small_sum.start()
+    reduction.finish()
+    small_out[...] = small_sum.finish()
+
+
+def reduce_gradients(grads, small):
+    widths = [g.shape[1] for g in grads]
+    chunks = column_chunks(widths)
+    blocks = [seq_blocks(g) for g in grads]
+    rows = blocks[0].shape[3]
     vmem = pl.BlockSpec(memory_space=pltpu.VMEM)
-    count, parts = len(groups), len(chunks)
-    result = pl.pallas_call(
-        functools.partial(reduce_kernel, seq_count, batch_count, chunks),
+    return pl.pallas_call(
+        functools.partial(reduce_kernel, chunks),
         out_shape=[jax.ShapeDtypeStruct((2, 2, rows, w), jnp.bfloat16) for w in widths]
         + [jax.ShapeDtypeStruct(small.shape, jnp.float32)],
-        in_specs=[vmem] * (count + 1),
-        out_specs=[vmem] * (count + 1),
-        scratch_shapes=[pltpu.VMEM((seq_count, 2, rows, w), jnp.bfloat16) for w in widths]
-        + [pltpu.VMEM((seq_count, rows, w), jnp.bfloat16) for w in widths]
-        + [pltpu.VMEM((seq_count - 1, rows, w), jnp.bfloat16) for w in widths]
-        + [
-            pltpu.VMEM((world,) + small.shape, jnp.float32),
-            pltpu.SemaphoreType.DMA((2, parts)),
-            pltpu.SemaphoreType.DMA((2, parts)),
-            pltpu.SemaphoreType.DMA((2, parts, seq_count - 1)),
-            pltpu.SemaphoreType.DMA((2, parts, 2)),
-            pltpu.SemaphoreType.DMA((2, world)),
-        ],
+        in_specs=[pl.BlockSpec(memory_space=pl.ANY)] * len(grads) + [vmem],
+        out_specs=[vmem] * (len(grads) + 1),
+        scratch_shapes=small_scratch(small.shape) + reduction_scratch(chunks, widths, rows),
         compiler_params=pltpu.CompilerParams(
             collective_id=0, has_side_effects=True, vmem_limit_bytes=56 << 20
         ),
         name="reduce_gradients",
     )(*blocks, small)
-    return [r.reshape(4 * rows, w) for r, w in zip(result[:-1], widths)], result[-1]
 
 
 def matmul(former, latter):
@@ -277,10 +366,6 @@
     return 1.0 / (1.0 + jnp.exp(-v))
 
 
-def peer_device():
-    return (lax.axis_index("seq"), 1 - lax.axis_index("head"), lax.axis_index("batch"))
-
-
 def greet_peer(barrier, peer):
     pl.semaphore_signal(barrier, inc=1, device_id=peer, device_id_type=MESH)
     pl.semaphore_wait(barrier, 1)
@@ -290,8 +375,11 @@
     return pl.ds(pl.multiple_of(i * TILE, TILE), TILE)
 
 
-def each(count, action):
-    lax.fori_loop(0, count, lambda i, carry: (action(i), carry)[1], 0)
+FEED_TILE = 256
+
+
+def feed_rows(i):
+    return pl.ds(pl.multiple_of(i * FEED_TILE, FEED_TILE), FEED_TILE)
 
 
 def feed_kernel(
@@ -300,6 +388,7 @@
     attention_ref,
     tokens_ref,
     cotangent_ref,
+    mixer_gain_ref,
     mamba_gain_ref,
     feed_gain_ref,
     mamba_output_ref,
@@ -315,11 +404,13 @@
     g_feed_ref,
     g_mixed_ref,
     g_down_ref,
+    g_gate_ref,
     g_feed_gain_ref,
     g_mamba_gain_ref,
     gate_weight,
     lift_weight,
     down_weight,
+    normed,
     gated,
     g_six,
     inverse_six,
@@ -348,7 +439,7 @@
     sem_norm,
 ):
     rows = y_ref.shape[0]
-    tiles = rows // TILE
+    tiles = rows // FEED_TILE
     inner = y_ref.shape[1]
     width = feed_gain_ref.shape[1]
     feed = down_weight.shape[1]
@@ -369,27 +460,30 @@
     greet_peer(pltpu.get_barrier_semaphore(), peer)
 
     def swap(send, recv, sems, i):
-        rows_now = tile_rows(i)
+        rows_now = feed_rows(i)
         return exchange(send.at[rows_now], recv.at[rows_now], sems.at[0, i], sems.at[1, i], peer)
 
     def gate_tile(i):
-        at = tile_rows(i)
+        at = feed_rows(i)
+        hidden = tokens_ref[at, :].astype(jnp.float32)
+        inverse = lax.rsqrt(jnp.mean(hidden * hidden, axis=1, keepdims=True) + eps_norm)
+        normed[at, :] = (hidden * inverse * mixer_gain_ref[...]).astype(jnp.bfloat16)
         gate_now = gate_z_ref[at, :]
         value = y_ref[at, :] * gate_now * sigmoid(gate_now)
         g_six[at, :] = value
         square_send[at, :] = jnp.broadcast_to(
-            jnp.sum(value * value, axis=1, keepdims=True), (TILE, LANES)
+            jnp.sum(value * value, axis=1, keepdims=True), (FEED_TILE, LANES)
         )
         swap(square_send, square_recv, sem_square, i).start()
 
     each(tiles, gate_tile)
 
     def mixed_tile(i):
-        at = tile_rows(i)
+        at = feed_rows(i)
         swap(square_send, square_recv, sem_square, i).wait()
         total = square_send[at, :] + square_recv[at, :]
         inverse = lax.rsqrt(total[:, :1] / all_inner + eps_norm)
-        inverse_six[at, :] = jnp.broadcast_to(inverse, (TILE, LANES))
+        inverse_six[at, :] = jnp.broadcast_to(inverse, (FEED_TILE, LANES))
         low = (g_six[at, :] * inverse * mamba_gain_ref[...]).astype(jnp.bfloat16)
         gated[at, :] = low
         part = matmul_last(low, mamba_output_ref[...]) + matmul_last(
@@ -403,13 +497,13 @@
         load.wait()
 
     def feed_tile(i):
-        at = tile_rows(i)
+        at = feed_rows(i)
         swap(mixed_send, mixed_recv, sem_mixed, i).wait()
         total = mixed_send[at, :].astype(jnp.float32) + mixed_recv[at, :].astype(jnp.float32)
         hidden = tokens_ref[at, :].astype(jnp.float32) + total
         second[at, :] = hidden
         inverse = lax.rsqrt(jnp.mean(hidden * hidden, axis=1, keepdims=True) + eps_norm)
-        inverse_two[at, :] = jnp.broadcast_to(inverse, (TILE, LANES))
+        inverse_two[at, :] = jnp.broadcast_to(inverse, (FEED_TILE, LANES))
         low = (hidden * inverse * feed_gain_ref[...]).astype(jnp.bfloat16)
         normed2[at, :] = low
         gate_now = matmul(low, gate_weight[...])
@@ -434,7 +528,7 @@
     g_mamba_gain_ref[...] = jnp.zeros_like(g_mamba_gain_ref)
 
     def norm_tile(i):
-        at = tile_rows(i)
+        at = feed_rows(i)
         swap(norm_send, norm_recv, sem_norm, i).wait()
         d_norm = norm_send[at, :].astype(jnp.float32) + norm_recv[at, :].astype(jnp.float32)
         hidden = second[at, :]
@@ -458,14 +552,14 @@
             d_gated_now * six * inverse_six[at, :][:, :1], axis=0, keepdims=True
         )
         cross_send[at, :] = jnp.broadcast_to(
-            jnp.sum(d_gated_now * mamba_gain_ref[...] * six, axis=1, keepdims=True), (TILE, LANES)
+            jnp.sum(d_gated_now * mamba_gain_ref[...] * six, axis=1, keepdims=True), (FEED_TILE, LANES)
         )
         swap(cross_send, cross_recv, sem_cross, i).start()
 
     each(tiles, norm_tile)
 
     def gate_back(i):
-        at = tile_rows(i)
+        at = feed_rows(i)
         swap(cross_send, cross_recv, sem_cross, i).wait()
         cross = (cross_send[at, :] + cross_recv[at, :])[:, :1] / all_inner
         inverse = inverse_six[at, :][:, :1]
@@ -482,7 +576,7 @@
     each(tiles, gate_back)
 
     def out_tile(i):
-        at = tile_rows(i)
+        at = feed_rows(i)
         swap(lift_send, lift_recv, sem_lift, i).wait()
         total = lift_send[at, :].astype(jnp.float32) + lift_recv[at, :].astype(jnp.float32)
         out_ref[at, :] = (second[at, :] + total).astype(jnp.bfloat16)
@@ -495,6 +589,9 @@
             jnp.bfloat16
         )
         g_feed_ref[block, :] = matmul_first(normed2[:, block], d_feed[...]).astype(jnp.bfloat16)
+        g_gate_ref[block, :] = matmul_first(normed[:, block], d_gate_z_ref[...]).astype(
+            jnp.bfloat16
+        )
         d_mix_now = d_mix[:, block]
         g_mixed_ref[block, :inner] = matmul_first(d_mix_now, gated[...]).astype(jnp.bfloat16)
         g_mixed_ref[block, inner:] = matmul_first(d_mix_now, attention_ref[...]).astype(
@@ -510,6 +607,7 @@
     attention_low,
     tokens,
     cotangent,
+    mixer_gain,
     mamba_gain,
     feed_gain,
     mamba_output,
@@ -522,7 +620,7 @@
     width = tokens.shape[1]
     feed = gate_weight.shape[1]
     att = attention_low.shape[1]
-    tiles = rows // TILE
+    tiles = rows // FEED_TILE
     vmem = pl.BlockSpec(memory_space=pltpu.VMEM)
     hbm = pl.BlockSpec(memory_space=pl.ANY)
     low, full = jnp.bfloat16, jnp.float32
@@ -538,15 +636,17 @@
             shape((width, 2 * feed), low),
             shape((width, inner + att), low),
             shape((width, feed), low),
+            shape((width, inner), low),
             shape((1, width), full),
             shape((1, inner), full),
         ],
-        in_specs=[vmem] * 9 + [hbm] * 3,
-        out_specs=[vmem] * 10,
+        in_specs=[vmem] * 10 + [hbm] * 3,
+        out_specs=[vmem] * 11,
         scratch_shapes=[
             pltpu.VMEM((width, feed), low),
             pltpu.VMEM((width, feed), low),
             pltpu.VMEM((width, feed), low),
+            pltpu.VMEM((rows, width), low),
             pltpu.VMEM((rows, inner), low),
             pltpu.VMEM((rows, inner), full),
             pltpu.VMEM((rows, LANES), full),
@@ -575,6 +675,7 @@
         attention_low,
         tokens,
         cotangent,
+        mixer_gain[None],
         mamba_gain[None],
         feed_gain[None],
         mamba_output,
@@ -665,7 +766,6 @@
 
 
 def mixer_kernel(
-    size,
     tokens_ref,
     gain_ref,
     seg_ref,
@@ -766,7 +866,7 @@
     def _():
         halo_copy.start()
 
-    spread_ref[...] = spread_matrix(inner, size)
+    spread_ref[...] = spread_matrix(inner, HD)
     lower = jnp.where(ordered(CHUNK), 1.0, 0.0)
 
     def project_tile(i):
@@ -876,7 +976,7 @@
                 mixing.append(meet * jnp.exp(jnp.minimum(gap, 0.0)))
             y_ref[at, columns] = matmul(
                 jnp.concatenate(mixing, axis=1).astype(jnp.bfloat16),
-                halves(scaled[at, columns].astype(jnp.float32), size),
+                halves(scaled[at, columns].astype(jnp.float32), HD),
             )
 
     each(tiles, inside_chunk)
@@ -958,7 +1058,7 @@
     low, full = jnp.bfloat16, jnp.float32
     shape = jax.ShapeDtypeStruct
     return pl.pallas_call(
-        functools.partial(mixer_kernel, HD),
+        mixer_kernel,
         out_shape=[
             shape((rows, inner), full),
             shape((rows + HALO, conv_width), full),
@@ -994,7 +1094,7 @@
         name="mixer_forward",
     )(
         tokens,
-        mixer_gain[None],
+        mixer_gain,
         segments,
         table,
         mamba_gate,
@@ -1022,15 +1122,15 @@
         if (h % 2 == 0) != first:
             tile = pltpu.roll(tile, HD, 1)
         parts.append(jnp.where(keep, tile * factor, 0.0))
-    return jnp.concatenate(parts, axis=0).astype(jnp.bfloat16)
-
-
-def unstacked_heads(values, rows, first):
-    lane = lax.broadcasted_iota(jnp.int32, (rows, LANES), 1)
+    return jnp.concatenate(parts, axis=0)
+
+
+def unstacked_heads(turned, first):
+    heads = turned.shape[1] // TILE
+    blocks = [turned[:, h * TILE : (h + 1) * TILE].T for h in range(heads)]
+    lane = lax.broadcasted_iota(jnp.int32, (TILE, LANES), 1)
     tiles = []
-    for pair in range(values.shape[0] // rows // 2):
-        even = values[2 * pair * rows : (2 * pair + 1) * rows]
-        odd = values[(2 * pair + 1) * rows : (2 * pair + 2) * rows]
+    for even, odd in zip(blocks[::2], blocks[1::2]):
         if first:
             odd = pltpu.roll(odd, HD, 1)
         else:
@@ -1039,64 +1139,131 @@
     return tiles
 
 
-def score_tile(first_ref, seg_ref, key_seg_ref, memory_ref, queries, i, k):
-    heads = queries.shape[0] // TILE
+def key_tile(seg_turned, key_seg_ref, first, i, k, heads):
     at = pl.ds(pl.multiple_of(k * KEY_TILE, KEY_TILE), KEY_TILE)
-    keys = memory_ref[at, :]
-    scores = matmul_last(queries, keys).reshape(heads, TILE, KEY_TILE)
-    row = first_ref[0] + i * TILE + lax.broadcasted_iota(jnp.int32, (TILE, KEY_TILE), 0)
-    place = k * KEY_TILE + lax.broadcasted_iota(jnp.int32, (TILE, KEY_TILE), 1)
-    own = seg_ref[pl.ds(pl.multiple_of(i * TILE, TILE) + HALO, TILE), :]
-    own = jnp.concatenate([own] * (KEY_TILE // LANES), axis=1)
-    allowed = (place <= row) & (key_seg_ref[0:1, at] == own)
-    return keys, at, scores, allowed[None]
+    place = k * KEY_TILE + lax.broadcasted_iota(jnp.int32, (KEY_TILE, TILE), 0)
+    row = first + i * TILE + lax.broadcasted_iota(jnp.int32, (KEY_TILE, TILE), 1)
+    allowed = jnp.where((place <= row) & (key_seg_ref[at, :] == seg_turned), 1.0, 0.0)
+    return at, jnp.concatenate([allowed] * heads, axis=1) > 0.5
+
+
+def query_segments(seg_ref, i):
+    own = seg_ref[pl.ds(pl.multiple_of(i * TILE, TILE) + HALO, TILE), :].T
+    return jnp.concatenate([own] * (KEY_TILE // TILE), axis=0)
+
+
+def attend_block(first, low, high, i, queries_in, memory_of, seg_ref, key_seg_ref):
+    heads = queries_in.shape[1] // HD
+    turned = stacked_heads(queries_in, True, HD ** (-0.5)).T.astype(jnp.bfloat16)
+    segs = query_segments(seg_ref, i)
+    wide = heads * TILE
+
+    def one(step, carry):
+        most, total, acc = carry
+        k = high - step
+        at, allowed = key_tile(segs, key_seg_ref, first, i, k, heads)
+        keys = memory_of(at)
+        scores = jnp.where(allowed, matmul(keys, turned), neg_large)
+        new = jnp.maximum(most, jnp.max(scores, axis=0, keepdims=True))
+        weights = jnp.exp(scores - new)
+        factor = jnp.exp(most - new)
+        total = total * factor + jnp.sum(weights, axis=0, keepdims=True)
+        acc = acc * factor + matmul_first(keys, weights.astype(jnp.bfloat16))
+        return new, total, acc
+
+    most, total, acc = lax.fori_loop(
+        0,
+        high - low + 1,
+        one,
+        (
+            jnp.full((1, wide), neg_large, jnp.float32),
+            jnp.zeros((1, wide), jnp.float32),
+            jnp.zeros((LANES, wide), jnp.float32),
+        ),
+    )
+    return acc / total, most + jnp.log(total)
+
+
+def attend_back_block(
+    first, low, high, i, queries_in, d_out, out, log, memory_of, seg_ref, key_seg_ref, grads
+):
+    heads = queries_in.shape[1] // HD
+    queries = stacked_heads(queries_in, True, HD ** (-0.5))
+    outer = stacked_heads(d_out, False, 1.0)
+    queries_turned, outer_turned = queries.T.astype(jnp.bfloat16), outer.T.astype(jnp.bfloat16)
+    queries, outer = queries.astype(jnp.bfloat16), outer.astype(jnp.bfloat16)
+    segs = query_segments(seg_ref, i)
+    row = lax.broadcasted_iota(jnp.int32, (HALO, heads * HD), 0)
+    lane = lax.broadcasted_iota(jnp.int32, (HALO, heads * HD), 1)
+    pick = jnp.where(lane // HD == row, 1.0, 0.0).astype(jnp.bfloat16)
+    high_part, low_part = two_parts(d_out * out)
+    deltas = matmul_last(pick, high_part) + matmul_last(pick, low_part)
+    delta = jnp.concatenate([deltas[h : h + 1] for h in range(heads)], axis=1)
+
+    def one(step, total):
+        at, allowed = key_tile(segs, key_seg_ref, first, i, high - step, heads)
+        keys = memory_of(at)
+        weights = jnp.exp(matmul(keys, queries_turned) - log)
+        weights = jnp.where(allowed, weights, 0.0)
+        slope = (weights * (matmul(keys, outer_turned) - delta)).astype(jnp.bfloat16)
+        grads[at, :] += matmul(slope, queries) + matmul(weights.astype(jnp.bfloat16), outer)
+        return total + matmul_first(keys, slope)
+
+    total = lax.fori_loop(
+        0, high - low + 1, one, jnp.zeros((LANES, heads * TILE), jnp.float32)
+    )
+    return total * HD ** (-0.5)
 
 
 def attention_kernel(
-    first_ref, low_ref, high_ref, query_ref, memory_ref, seg_ref, key_seg_ref, out_ref, low_out_ref, log_ref
+    first_ref,
+    low_ref,
+    high_ref,
+    query_ref,
+    memory_ref,
+    seg_ref,
+    key_seg_ref,
+    out_ref,
+    low_out_ref,
+    log_ref,
 ):
-    rows = query_ref.shape[0]
-    heads = query_ref.shape[1] // HD
-
     def block(i):
         at_rows = tile_rows(i)
-        queries = stacked_heads(query_ref[at_rows, :], True, HD ** (-0.5))
-        last = high_ref[i]
-
-        def one(step, carry):
-            most, total, acc = carry
-            keys, _, scores, allowed = score_tile(
-                first_ref, seg_ref, key_seg_ref, memory_ref, queries, i, last - step
-            )
-            scores = jnp.where(allowed, scores, neg_large).reshape(heads * TILE, KEY_TILE)
-            new = jnp.maximum(most, jnp.max(scores, axis=1, keepdims=True))
-            weights = jnp.exp(scores - new)
-            factor = jnp.exp(most - new)
-            total = total * factor + jnp.sum(weights, axis=1, keepdims=True)
-            acc = acc * factor + matmul(weights.astype(jnp.bfloat16), keys)
-            return new, total, acc
-
-        most, total, acc = lax.fori_loop(
-            0,
-            last - low_ref[i] + 1,
-            one,
-            (
-                jnp.full((heads * TILE, 1), neg_large, jnp.float32),
-                jnp.zeros((heads * TILE, 1), jnp.float32),
-                jnp.zeros((heads * TILE, LANES), jnp.float32),
-            ),
-        )
-        for pair, tile in enumerate(unstacked_heads(acc / total, TILE, False)):
-            out_ref[at_rows, pair * LANES : (pair + 1) * LANES] = tile
-            low_out_ref[at_rows, pair * LANES : (pair + 1) * LANES] = tile.astype(jnp.bfloat16)
-        log = most + jnp.log(total)
-        lane = lax.broadcasted_iota(jnp.int32, (TILE, LANES), 1)
-        logs = jnp.zeros((TILE, LANES), jnp.float32)
-        for h in range(heads):
-            logs = jnp.where(lane == h, log[h * TILE : (h + 1) * TILE], logs)
-        log_ref[at_rows, :] = logs
-
-    each(rows // TILE, block)
+        turned, log = attend_block(
+            first_ref[0],
+            low_ref[i],
+            high_ref[i],
+            i,
+            query_ref[at_rows, :],
+            lambda at: memory_ref[at, :],
+            seg_ref,
+            key_seg_ref,
+        )
+        for pair, tile in enumerate(unstacked_heads(turned, False)):
+            columns = slice(pair * LANES, (pair + 1) * LANES)
+            out_ref[at_rows, columns] = tile
+            low_out_ref[at_rows, columns] = tile.astype(jnp.bfloat16)
+        log_ref[i] = jnp.broadcast_to(log, log_ref.shape[1:])
+
+    each(query_ref.shape[0] // TILE, block)
+
+
+def attention_forward(spans, query, memory, segments, key_segments):
+    rows, width = query.shape
+    full = jnp.float32
+    vmem = pl.BlockSpec(memory_space=pltpu.VMEM)
+    return pl.pallas_call(
+        attention_kernel,
+        out_shape=[
+            jax.ShapeDtypeStruct((rows, width), full),
+            jax.ShapeDtypeStruct((rows, width), jnp.bfloat16),
+            jax.ShapeDtypeStruct((rows // TILE, HALO, width // HD * TILE), full),
+        ],
+        in_specs=[pl.BlockSpec(memory_space=pltpu.SMEM)] * 3 + [vmem] * 4,
+        out_specs=[vmem] * 3,
+        compiler_params=pltpu.CompilerParams(vmem_limit_bytes=56 << 20),
+        name="attention_forward",
+    )(*spans, query, memory, segments, key_segments)
 
 
 def attention_back_kernel(
@@ -1115,148 +1282,126 @@
     d_memory_ref,
     grads,
 ):
-    rows = query_ref.shape[0]
-    heads = query_ref.shape[1] // HD
     grads[...] = jnp.zeros_like(grads)
 
     def block(i):
-        at_rows = tile_rows(i)
-        queries = stacked_heads(query_ref[at_rows, :], True, HD ** (-0.5))
-        d_out = d_out_ref[at_rows, :]
-        outer = stacked_heads(d_out, False, 1.0)
-        product = d_out * out_ref[at_rows, :]
-        lane = lax.broadcasted_iota(jnp.int32, (TILE, LANES), 1)
-        deltas, logs = [], []
-        for h in range(heads):
-            tile = product[:, (h // 2) * LANES : (h // 2 + 1) * LANES]
-            mine = (lane < HD) if h % 2 == 0 else (lane >= HD)
-            deltas.append(jnp.sum(jnp.where(mine, tile, 0.0), axis=1, keepdims=True))
-            logs.append(log_ref[at_rows, h : h + 1])
-        delta = jnp.concatenate(deltas, axis=0)
-        log = jnp.concatenate(logs, axis=0)
-        last = high_ref[i]
-
-        def one(step, total):
-            keys, at, scores, allowed = score_tile(
-                first_ref, seg_ref, key_seg_ref, memory_ref, queries, i, last - step
-            )
-            weights = jnp.exp(scores - log.reshape(heads, TILE, 1))
-            weights = jnp.where(allowed, weights, 0.0).reshape(heads * TILE, KEY_TILE)
-            inner = matmul_last(outer, keys)
-            low = (weights * (inner - delta)).astype(jnp.bfloat16)
-            grads[at, :] += matmul_first(low, queries) + matmul_first(
-                weights.astype(jnp.bfloat16), outer
-            )
-            return total + matmul(low, keys)
-
-        total = lax.fori_loop(
-            0, last - low_ref[i] + 1, one, jnp.zeros((heads * TILE, LANES), jnp.float32)
-        )
-        for pair, tile in enumerate(unstacked_heads(total * HD ** (-0.5), TILE, True)):
-            turned = tile * table_ref[at_rows, :LANES] - turn_half(tile) * table_ref[at_rows, LANES:]
-            d_query_ref[at_rows, pair * LANES : (pair + 1) * LANES] = turned.astype(jnp.bfloat16)
-
-    each(rows // TILE, block)
+        at = tile_rows(i)
+        d_turned = attend_back_block(
+            first_ref[0],
+            low_ref[i],
+            high_ref[i],
+            i,
+            query_ref[at, :],
+            d_out_ref[at, :],
+            out_ref[at, :],
+            log_ref[i][:1],
+            lambda key_at: memory_ref[key_at, :],
+            seg_ref,
+            key_seg_ref,
+            grads,
+        )
+        for pair, tile in enumerate(unstacked_heads(d_turned, True)):
+            turned = tile * table_ref[at, :LANES] - turn_half(tile) * table_ref[at, LANES:]
+            d_query_ref[at, pair * LANES : (pair + 1) * LANES] = turned.astype(jnp.bfloat16)
+
+    each(query_ref.shape[0] // TILE, block)
     d_memory_ref[...] = grads[...].astype(jnp.bfloat16)
 
 
-def attention_specs(count):
-    return [pl.BlockSpec(memory_space=pltpu.SMEM)] * 3 + [
-        pl.BlockSpec(memory_space=pltpu.VMEM)
-    ] * count
-
-
-def attention_forward(spans, query, memory, segments, key_segments):
-    rows, width = query.shape
-    full = jnp.float32
-    return pl.pallas_call(
-        attention_kernel,
-        out_shape=[
-            jax.ShapeDtypeStruct((rows, width), full),
-            jax.ShapeDtypeStruct((rows, width), jnp.bfloat16),
-            jax.ShapeDtypeStruct((rows, LANES), full),
-        ],
-        in_specs=attention_specs(4),
-        out_specs=[pl.BlockSpec(memory_space=pltpu.VMEM)] * 3,
-        compiler_params=pltpu.CompilerParams(vmem_limit_bytes=56 << 20),
-        name="attention_forward",
-    )(*spans, query, memory, segments, key_segments)
-
-
 def attention_back(spans, query, memory, segments, key_segments, out, logs, d_out, table):
-    rows, width = query.shape
+    vmem = pl.BlockSpec(memory_space=pltpu.VMEM)
     return pl.pallas_call(
         attention_back_kernel,
         out_shape=[
-            jax.ShapeDtypeStruct((rows, width), jnp.bfloat16),
+            jax.ShapeDtypeStruct(query.shape, jnp.bfloat16),
             jax.ShapeDtypeStruct(memory.shape, jnp.bfloat16),
         ],
-        in_specs=attention_specs(8),
-        out_specs=[pl.BlockSpec(memory_space=pltpu.VMEM)] * 2,
+        in_specs=[pl.BlockSpec(memory_space=pltpu.SMEM)] * 3 + [vmem] * 8,
+        out_specs=[vmem] * 2,
         scratch_shapes=[pltpu.VMEM(memory.shape, jnp.float32)],
         compiler_params=pltpu.CompilerParams(vmem_limit_bytes=56 << 20),
         name="attention_back",
     )(*spans, query, memory, segments, key_segments, out, logs, d_out, table)
 
 
-def mixer_back_kernel(
-    size,
-    tokens_ref,
-    gain_ref,
-    seg_ref,
-    table_ref,
-    gate_weight,
-    input_weight,
-    maps_weight,
-    step_weight,
-    query_weight,
-    memory_weight,
-    taps_ref,
-    rate_ref,
-    skip_ref,
-    pre_ref,
-    conv_ref,
-    raw_ref,
-    cum_ref,
-    y_ref,
-    states_ref,
-    d_second_ref,
-    d_y_ref,
-    d_gate_z_ref,
-    d_query_ref,
-    d_memory_ref,
-    d_tokens_ref,
-    g_side_ref,
-    g_taps_ref,
-    g_gain_ref,
-    g_heads_ref,
-    normed,
-    spread_ref,
-    act,
-    d_act,
-    d_conv,
-    d_scaled,
-    d_maps,
-    row_term,
-    added,
-    local,
-    total,
-    state,
-    skip_sum,
-    side,
-    chain_out,
-    chain_in,
-    maps_send,
-    maps_recv,
-    memory_recv,
-    norm_send,
-    norm_recv,
-    sem_memory,
-    sem_halo,
-    sem_chain,
-    sem_maps,
-    sem_norm,
-):
+def mixer_back_kernel(merged, chunks, *refs):
+    refs = list(refs)
+
+    def take(names):
+        nonlocal refs
+        now, refs = refs[: len(names)], refs[len(names) :]
+        return now
+
+    (
+        tokens_ref,
+        gain_ref,
+        seg_ref,
+        table_ref,
+        gate_weight,
+        input_weight,
+        maps_weight,
+        step_weight,
+        query_weight,
+        memory_weight,
+        taps_ref,
+        rate_ref,
+        skip_ref,
+        pre_ref,
+        conv_ref,
+        raw_ref,
+        cum_ref,
+        y_ref,
+        states_ref,
+        d_second_ref,
+        d_y_ref,
+        d_gate_z_ref,
+    ) = take(range(22))
+    if merged:
+        (
+            query_ref,
+            memory_ref,
+            key_seg_ref,
+            attention_ref,
+            logs_ref,
+            d_attention_ref,
+            feed_gain_ref,
+            mamba_gain_ref,
+        ) = take(range(8))
+        early = take(range(4))
+        d_tokens_ref, *outs, small_out = take(range(7))
+    else:
+        d_query_ref, d_memory_ref = take(range(2))
+        d_tokens_ref, g_side_ref, g_taps_ref, g_gain_ref, g_heads_ref = take(range(5))
+    (
+        normed,
+        spread_ref,
+        act,
+        d_conv,
+        d_scaled,
+        d_maps,
+        row_term,
+        added,
+        local,
+        total,
+        state,
+        skip_sum,
+        side,
+        chain_out,
+        chain_in,
+        maps_send,
+        maps_recv,
+        memory_recv,
+        norm_send,
+        norm_recv,
+        sem_memory,
+        sem_halo,
+        sem_chain,
+        sem_maps,
+        sem_norm,
+    ) = take(range(25))
+    if merged:
+        g_side_ref, grads, d_memory_ref, small_in, small_buf, sem_small = take(range(6))
+        g_taps_ref = g_gain_ref = g_heads_ref = small_in
     seq, head, batch = lax.axis_index("seq"), lax.axis_index("head"), lax.axis_index("batch")
     count = lax.axis_size("seq")
     rows = tokens_ref.shape[0]
@@ -1267,9 +1412,22 @@
     model = tokens_ref.shape[1]
     peer = peer_device()
     previous = (lax.rem(seq - 1 + count, count), head, batch)
-    greet_seq(pltpu.get_barrier_semaphore(), 1)
-    spread_ref[...] = spread_matrix(inner, size)
     pieces = inner // PIECE
+    step_at = width
+    query_at = step_at + LANES
+    memory_at = query_at + query_weight.shape[1]
+    if merged:
+        greet_all(pltpu.get_barrier_semaphore(), True)
+        reduction = Reduction(chunks, list(early) + [g_side_ref], outs, refs)
+        reduction.allow(sum(1 for c in chunks if c[0] < len(early)))
+        advance = reduction.advance
+    else:
+        greet_seq(pltpu.get_barrier_semaphore(), 1)
+
+        def advance():
+            return None
+
+    spread_ref[...] = spread_matrix(inner, HD)
 
     def chain_copy(p):
         columns = pl.ds(p * PIECE, PIECE)
@@ -1350,6 +1508,68 @@
             for p in range(pieces):
                 chain_copy(p).start()
 
+    if merged:
+        first = seq * rows
+        grads[...] = jnp.zeros_like(grads)
+
+        def attention_block(i):
+            at = tile_rows(i)
+            d_turned = attend_back_block(
+                first,
+                0,
+                (first + i * TILE + TILE - 1) // KEY_TILE,
+                i,
+                query_ref[at, :],
+                d_attention_ref[at, :],
+                attention_ref[at, :],
+                logs_ref[i][:1],
+                lambda key_at: memory_ref[key_at, :],
+                seg_ref,
+                key_seg_ref,
+                grads,
+            )
+            for pair, tile in enumerate(unstacked_heads(d_turned, True)):
+                turned = tile * table_ref[at, :LANES] - turn_half(tile) * table_ref[at, LANES:]
+                columns = pl.ds(query_at + pair * LANES, LANES)
+                side[at, columns] = turned.astype(jnp.bfloat16)
+
+        half = tiles // 2
+        span(0, half, attention_block)
+        advance()
+        span(half, tiles, attention_block)
+        advance()
+
+        def low_block(place):
+            at = pl.ds(pl.multiple_of(place * rows, rows), rows)
+            d_memory_ref[place] = grads[at, :].astype(jnp.bfloat16)
+
+        each(count, low_block)
+
+    def chain_wait(p):
+        columns = pl.ds(p * PIECE, PIECE)
+        chain_copy(p).wait_recv()
+        came = chain_in[:, columns].astype(jnp.float32)
+        state[:, columns] = came
+        return came
+
+    @pl.when((seq > 0) & (seq < count - 1))
+    def _():
+        for p in range(pieces):
+            columns = pl.ds(p * PIECE, PIECE)
+            came = chain_wait(p)
+            chain_out[:, columns] = (came * total[:1, columns] + local[:, columns]).astype(
+                jnp.bfloat16
+            )
+            chain_copy(p).start()
+
+    def memory_start(step, carry):
+        @pl.when(seq - step >= 0)
+        def _():
+            memory_copy(step).start()
+
+        return carry
+
+    lax.fori_loop(1, count, memory_start, 0)
     skip_sum[...] = jnp.zeros_like(skip_sum)
 
     def inside_chunk(c):
@@ -1368,7 +1588,7 @@
         for i in range(inner // LANES):
             columns = slice(i * LANES, (i + 1) * LANES)
             d_tile = d_y[:, columns]
-            d_mixing = matmul_last(halves(scaled[:, columns], size), d_tile.astype(jnp.bfloat16))
+            d_mixing = matmul_last(halves(scaled[:, columns], HD), d_tile.astype(jnp.bfloat16))
             mixing = []
             for k, h in enumerate((2 * i, 2 * i + 1)):
                 gap = turned[h : h + 1, :] - cum[:, h : h + 1]
@@ -1376,7 +1596,7 @@
                 mixing.append(meet * fade)
                 d_meet = d_meet + d_mixing[k * CHUNK : (k + 1) * CHUNK] * fade
             d_scaled[at, columns] = matmul(
-                jnp.concatenate(mixing, axis=1).astype(jnp.bfloat16), halves(d_tile, size)
+                jnp.concatenate(mixing, axis=1).astype(jnp.bfloat16), halves(d_tile, HD)
             )
         d_meet = (d_meet * allowed).astype(jnp.bfloat16)
         d_maps[at, :state_width] = matmul(d_meet, low_out)
@@ -1389,32 +1609,29 @@
         low = d_y.astype(jnp.bfloat16).astype(jnp.float32)
         row_term[at, :] = sum_heads(low * (y_ref[at, :] - skip_ref[...] * value), spread)
 
-    each(tiles, inside_chunk)
-
-    @pl.when(seq < count - 1)
+    span(0, tiles // 2, inside_chunk)
+    advance()
+    span(tiles // 2, tiles, inside_chunk)
+    advance()
+
+    @pl.when((seq == 0) & (seq < count - 1))
     def _():
         for p in range(pieces):
-            columns = pl.ds(p * PIECE, PIECE)
-            chain_copy(p).wait_recv()
-            came = chain_in[:, columns].astype(jnp.float32)
-            state[:, columns] = came
-
-            @pl.when(seq > 0)
-            def _():
-                chain_out[:, columns] = (
-                    came * total[:1, columns] + local[:, columns]
-                ).astype(jnp.bfloat16)
-                chain_copy(p).start()
-
-    def memory_start(step, carry):
-        @pl.when(seq - step >= 0)
-        def _():
-            memory_copy(step).start()
-
-        return carry
-
-    lax.fori_loop(1, count, memory_start, 0)
-    g_heads_ref[...] = jnp.zeros_like(g_heads_ref)
+            chain_wait(p)
+
+    if merged:
+        small_in[...] = jnp.zeros_like(small_in)
+        small_in[4:5, :inner] = mamba_gain_ref[...]
+        small_in[6:7, :] = feed_gain_ref[...]
+    else:
+        g_heads_ref[...] = jnp.zeros_like(g_heads_ref)
+
+    gain_row = 5 if merged else 0
+
+    def add_heads(k, values):
+        row, lane = (7, k * LANES) if merged else (k, 0)
+        g_heads_ref[row : row + 1, lane : lane + LANES] += values
+
     upper = jnp.where(ordered(CHUNK), 1.0, 0.0).T
 
     def across_chunk(step):
@@ -1444,24 +1661,22 @@
         rate = rate_ref[...]
         d_steps = sum_heads(value * d_value, spread) + rate * d_rate
         d_raw = d_steps * sigmoid(raw)
-        g_heads_ref[0:1, :] += rate * jnp.sum(steps * d_rate, axis=0, keepdims=True)
-        g_heads_ref[1:2, :] += jnp.sum(d_raw, axis=0, keepdims=True)
-        side[at, 2 * inner + 2 * state_width : 2 * inner + 2 * state_width + LANES] = d_raw.astype(
-            jnp.bfloat16
-        )
-        d_act[at, :inner] = steps_wide * d_value + skip_ref[...] * d_y_ref[at, :]
+        add_heads(0, rate * jnp.sum(steps * d_rate, axis=0, keepdims=True))
+        add_heads(1, jnp.sum(d_raw, axis=0, keepdims=True))
+        side[at, step_at:query_at] = d_raw.astype(jnp.bfloat16)
+        d_conv[at, :inner] = steps_wide * d_value + skip_ref[...] * d_y_ref[at, :]
         state[...] = now * keep_of(c, start)[:1] + added[c]
 
-    each(tiles, across_chunk)
-    g_heads_ref[2:3, :] = sum_heads(jnp.broadcast_to(skip_sum[:1], (HALO, inner)), spread_ref[...])[
-        :1
-    ]
+    span(0, tiles // 2, across_chunk)
+    advance()
+    span(tiles // 2, tiles, across_chunk)
+    advance()
+    add_heads(2, sum_heads(jnp.broadcast_to(skip_sum[:1], (HALO, inner)), spread_ref[...])[:1])
     maps_send[...] = d_maps[...].astype(jnp.bfloat16)
     maps_copy.start()
 
     def copy_tile(i):
         at = tile_rows(i)
-        side[at, :inner] = d_gate_z_ref[at, :]
         hidden = tokens_ref[at, :].astype(jnp.float32)
         inverse = lax.rsqrt(jnp.mean(hidden * hidden, axis=1, keepdims=True) + eps_norm)
         normed[at, :] = (hidden * inverse * gain_ref[...]).astype(jnp.bfloat16)
@@ -1471,12 +1686,12 @@
 
     def conv_back_tile(i):
         at = tile_rows(i)
-        d_act[at, inner:] = maps_send[at, :].astype(jnp.float32) + maps_recv[at, :].astype(
+        d_conv[at, inner:] = maps_send[at, :].astype(jnp.float32) + maps_recv[at, :].astype(
             jnp.float32
         )
         value = conv_ref[at, :]
         sig = sigmoid(value)
-        d_conv[at, :] = d_act[at, :] * (sig * (1.0 + value * (1.0 - sig)))
+        d_conv[at, :] = d_conv[at, :] * (sig * (1.0 + value * (1.0 - sig)))
 
     each(tiles, conv_back_tile)
 
@@ -1492,7 +1707,8 @@
     def _():
         halo_copy.wait_recv()
 
-    g_taps_ref[...] = jnp.zeros_like(g_taps_ref)
+    if not merged:
+        g_taps_ref[...] = jnp.zeros_like(g_taps_ref)
 
     def taps_tile(i):
         at = tile_rows(i)
@@ -1521,12 +1737,10 @@
                     axis=0,
                     keepdims=True,
                 )
-            side[at, inner + j * LANES : inner + (j + 1) * LANES] = summed.astype(jnp.bfloat16)
+            side[at, j * LANES : (j + 1) * LANES] = summed.astype(jnp.bfloat16)
 
     each(tiles, taps_tile)
-    query_at = 2 * inner + 2 * state_width + LANES
-    query_width = d_query_ref.shape[1]
-    memory_at = query_at + query_width
+    advance()
 
     def memory_wait(step, carry):
         @pl.when(seq - step >= 0)
@@ -1554,18 +1768,34 @@
         side[at, memory_at : memory_at + LANES] = jnp.where(lane < HD, turned, grad).astype(
             jnp.bfloat16
         )
-        side[at, query_at:memory_at] = d_query_ref[at, :]
+        if not merged:
+            side[at, query_at:memory_at] = d_query_ref[at, :]
 
     each(tiles, memory_tile)
+
+    def weight_block(k):
+        block = pl.ds(pl.multiple_of(k * 256, 256), 256)
+        grad = matmul_first(normed[:, block], side[...])
+        if merged:
+            _, high, low, own, columns = g_side_ref.shape
+            parts = 256 // (high * low * own)
+            g_side_ref[pl.ds(k * parts, parts)] = grad.reshape(
+                parts, high, low, own, columns
+            ).astype(jnp.bfloat16)
+        else:
+            g_side_ref[block, :] = grad.astype(jnp.bfloat16)
+
+    each(model // 256, weight_block)
+    if merged:
+        reduction.allow(len(chunks))
+    advance()
 
     def norm_tile(i):
         at = tile_rows(i)
-        maps_at = 2 * inner
-        step_at = maps_at + 2 * state_width
         part = (
-            matmul_last(side[at, :inner], gate_weight[...])
-            + matmul_last(side[at, inner:maps_at], input_weight[...])
-            + matmul_last(side[at, maps_at:step_at], maps_weight[...]) / lax.axis_size("head")
+            matmul_last(d_gate_z_ref[at, :], gate_weight[...])
+            + matmul_last(side[at, :inner], input_weight[...])
+            + matmul_last(side[at, inner:step_at], maps_weight[...]) / lax.axis_size("head")
             + matmul_last(side[at, step_at:query_at], step_weight[...])
             + matmul_last(side[at, query_at:memory_at], query_weight[...])
             + matmul_last(side[at, memory_at:], memory_weight[...])
@@ -1575,12 +1805,9 @@
 
     each(tiles, norm_tile)
 
-    def weight_block(k):
-        block = pl.ds(pl.multiple_of(k * 256, 256), 256)
-        g_side_ref[block, :] = matmul_first(normed[:, block], side[...]).astype(jnp.bfloat16)
-
-    each(model // 256, weight_block)
-    g_gain_ref[...] = jnp.zeros_like(g_gain_ref)
+    advance()
+    if not merged:
+        g_gain_ref[...] = jnp.zeros_like(g_gain_ref)
 
     def last_tile(i):
         at = tile_rows(i)
@@ -1593,9 +1820,16 @@
         d_tokens_ref[at, :] = (
             d_second_ref[at, :] + inverse * e_one - hidden * (inverse * inverse * inverse * cross)
         )
-        g_gain_ref[...] += jnp.sum(d_norm * hidden * inverse, axis=0, keepdims=True)
+        g_gain_ref[gain_row : gain_row + 1, :] += jnp.sum(
+            d_norm * hidden * inverse, axis=0, keepdims=True
+        )
 
     each(tiles, last_tile)
+    if merged:
+        small_sum = SmallSum(small_in, small_buf, sem_small)
+        small_sum.start()
+        reduction.finish()
+        small_out[...] = small_sum.finish()
 
     @pl.when(seq > 0)
     def _():
@@ -1604,92 +1838,181 @@
             chain_copy(p).wait_send()
 
 
-def mixer_back(
-    tokens,
-    mixer_gain,
-    segments,
-    table,
-    mamba_gate,
-    mamba_input,
-    mamba_maps,
-    step_weight,
-    query_weight,
-    memory_weight,
-    taps,
-    rate,
-    skip,
-    *saved,
-):
+def mixer_back(common, saved, attention=None, grads=None):
+    tokens = common[0]
     rows, model = tokens.shape
+    gate_weight, query_weight, memory_weight, taps = common[4], common[8], common[9], common[10]
+    merged = grads is not None
     count = lax.axis_size("seq")
-    inner = mamba_gate.shape[1]
+    inner = gate_weight.shape[1]
     width = taps.shape[1]
     state_width = (width - inner) // 2
-    chunks = rows // CHUNK
+    tiles = rows // CHUNK
     pieces = inner // PIECE
-    side = 2 * inner + 2 * state_width + LANES + query_weight.shape[1] + memory_weight.shape[1]
+    memory_width = memory_weight.shape[1]
+    side = width + LANES + query_weight.shape[1] + memory_width
     vmem = pl.BlockSpec(memory_space=pltpu.VMEM)
+    hbm = pl.BlockSpec(memory_space=pl.ANY)
     low, full = jnp.bfloat16, jnp.float32
     shape = jax.ShapeDtypeStruct
-    return pl.pallas_call(
-        functools.partial(mixer_back_kernel, HD),
-        out_shape=[
+    operands = [*common, *saved]
+    in_specs = [vmem] * (len(operands) + len(attention))
+    operands += attention
+    chunks = None
+    scratch = [
+        pltpu.VMEM((rows, model), low),
+        pltpu.VMEM((LANES, inner), low),
+        pltpu.VMEM((rows, width), full),
+        pltpu.VMEM((rows + HALO, width), full),
+        pltpu.VMEM((rows, inner), full),
+        pltpu.VMEM((rows, 2 * state_width), full),
+        pltpu.VMEM((rows, LANES), full),
+        pltpu.VMEM((tiles, state_width, inner), full),
+        pltpu.VMEM((state_width, inner), full),
+        pltpu.VMEM((HALO, inner), full),
+        pltpu.VMEM((state_width, inner), full),
+        pltpu.VMEM((1, inner), full),
+        pltpu.VMEM((rows, side), low),
+        pltpu.VMEM((state_width, inner), low),
+        pltpu.VMEM((state_width, inner), low),
+        pltpu.VMEM((rows, 2 * state_width), low),
+        pltpu.VMEM((rows, 2 * state_width), low),
+        pltpu.VMEM((max(count - 1, 1), rows, memory_width), low),
+        pltpu.VMEM((rows, model), low),
+        pltpu.VMEM((rows, model), low),
+        pltpu.SemaphoreType.DMA((2, count)),
+        pltpu.SemaphoreType.DMA((2,)),
+        pltpu.SemaphoreType.DMA((2, pieces)),
+        pltpu.SemaphoreType.DMA((2,)),
+        pltpu.SemaphoreType.DMA((2, tiles)),
+    ]
+    if merged:
+        blocks = [seq_blocks(g) for g in grads]
+        widths = [g.shape[1] for g in grads] + [side]
+        chunks = column_chunks(widths)
+        operands += blocks
+        in_specs += [hbm] * len(blocks)
+        own = blocks[0].shape[3]
+        small = (HALO, model)
+        out_shape = (
+            [shape((rows, model), full)]
+            + [shape((2, 2, own, w), low) for w in widths]
+            + [shape(small, full)]
+        )
+        scratch += [
+            pltpu.VMEM(blocks[0].shape[:4] + (side,), low),
+            pltpu.VMEM((count * rows, memory_width), full),
+            pltpu.VMEM((count, rows, memory_width), low),
+        ]
+        scratch += small_scratch(small) + reduction_scratch(chunks, widths, own)
+    else:
+        out_shape = [
             shape((rows, model), full),
             shape((model, side), low),
             shape((HALO, width), full),
             shape((1, model), full),
             shape((HALO, LANES), full),
-        ],
-        in_specs=[vmem] * (13 + len(saved)),
-        out_specs=[vmem] * 5,
-        scratch_shapes=[
-            pltpu.VMEM((rows, model), low),
-            pltpu.VMEM((LANES, inner), low),
-            pltpu.VMEM((rows, width), full),
-            pltpu.VMEM((rows, width), full),
-            pltpu.VMEM((rows + HALO, width), full),
-            pltpu.VMEM((rows, inner), full),
-            pltpu.VMEM((rows, 2 * state_width), full),
-            pltpu.VMEM((rows, LANES), full),
-            pltpu.VMEM((chunks, state_width, inner), full),
-            pltpu.VMEM((state_width, inner), full),
-            pltpu.VMEM((HALO, inner), full),
-            pltpu.VMEM((state_width, inner), full),
-            pltpu.VMEM((1, inner), full),
-            pltpu.VMEM((rows, side), low),
-            pltpu.VMEM((state_width, inner), low),
-            pltpu.VMEM((state_width, inner), low),
-            pltpu.VMEM((rows, 2 * state_width), low),
-            pltpu.VMEM((rows, 2 * state_width), low),
-            pltpu.VMEM((max(count - 1, 1), rows, memory_weight.shape[1]), low),
-            pltpu.VMEM((rows, model), low),
-            pltpu.VMEM((rows, model), low),
-            pltpu.SemaphoreType.DMA((2, count)),
-            pltpu.SemaphoreType.DMA((2,)),
-            pltpu.SemaphoreType.DMA((2, pieces)),
-            pltpu.SemaphoreType.DMA((2,)),
-            pltpu.SemaphoreType.DMA((2, chunks)),
-        ],
+        ]
+    return pl.pallas_call(
+        functools.partial(mixer_back_kernel, merged, chunks),
+        out_shape=out_shape,
+        in_specs=in_specs,
+        out_specs=[vmem] * len(out_shape),
+        scratch_shapes=scratch,
         compiler_params=pltpu.CompilerParams(
-            collective_id=3, has_side_effects=True, vmem_limit_bytes=60 << 20
+            collective_id=3, has_side_effects=True, vmem_limit_bytes=62 << 20
         ),
         name="mixer_back",
-    )(
-        tokens,
-        mixer_gain[None],
-        segments,
-        table,
-        mamba_gate,
-        mamba_input,
-        mamba_maps,
-        step_weight,
-        query_weight,
-        memory_weight,
-        taps,
-        rate,
-        skip,
-        *saved,
-    )
+    )(*operands)
+
+
+def finish_kernel(sizes, down, feed, mixed, gate, side, small, *outs):
+    inner, maps, heads, query, own = sizes
+    full = jnp.float32
+    seq = lax.axis_index("seq")
+    wide = small.shape[1]
+    columns = [0, inner, inner + maps, inner + maps + heads]
+    query_at = inner + maps + LANES
+    (
+        o_gate_z,
+        o_inner,
+        o_maps,
+        o_step,
+        o_output,
+        o_query,
+        o_memory,
+        o_attention,
+        o_gate,
+        o_lift,
+        o_down,
+        o_conv_inner,
+        o_conv_maps,
+        o_mixer_gain,
+        o_rate,
+        o_bias,
+        o_skip,
+        o_mamba_gain,
+        o_feed_gain,
+    ) = outs
+    o_gate_z[...] = gate[...].astype(full)
+    o_inner[...] = side[:, : columns[1]].astype(full)
+    o_maps[...] = side[:, columns[1] : columns[2]].astype(full)
+    o_step[...] = side[:, columns[2] : columns[2] + LANES].astype(full)[:, :heads]
+    o_query[...] = side[:, query_at : query_at + query].astype(full)
+    o_memory[...] = side[:, query_at + query :].astype(full)
+    o_output[...] = mixed[:, :inner].astype(full)
+    o_attention[...] = mixed[:, inner:].astype(full)
+    o_gate[...] = feed[:, : o_gate.shape[1]].astype(full)
+    o_lift[...] = feed[:, o_gate.shape[1] :].astype(full)
+    o_down[...] = down[...].astype(full)
+    value = small[...]
+    o_conv_inner[...] = value[:4, :inner]
+    o_conv_maps[...] = value[:4, inner:]
+    turned = pltpu.roll(value, lax.rem(wide - seq * own, wide), 1)
+    o_mixer_gain[...] = turned[5:6, :own]
+    o_feed_gain[...] = turned[6:7, :own]
+    for k, out in enumerate((o_rate, o_bias, o_skip)):
+        out[...] = value[7:8, k * LANES : (k + 1) * LANES][:, :heads]
+    o_mamba_gain[...] = value[4:5, :inner]
+
+
+def finish_outputs(sums, small, sizes):
+    inner, maps, heads, query, own = sizes
+    rows = own
+    sums = [s.reshape(rows, s.shape[-1]) for s in sums]
+    down, feed, mixed, gate, side = sums
+    half = feed.shape[1] // 2
+    memory = side.shape[1] - inner - maps - LANES - query
+    shapes = [
+        (rows, inner),
+        (rows, inner),
+        (rows, maps),
+        (rows, heads),
+        (rows, inner),
+        (rows, query),
+        (rows, memory),
+        (rows, mixed.shape[1] - inner),
+        (rows, half),
+        (rows, half),
+        (rows, half),
+        (4, inner),
+        (4, maps),
+        (1, own),
+        (1, heads),
+        (1, heads),
+        (1, heads),
+        (1, inner),
+        (1, own),
+    ]
+    vmem = pl.BlockSpec(memory_space=pltpu.VMEM)
+    return pl.pallas_call(
+        functools.partial(finish_kernel, sizes),
+        out_shape=[jax.ShapeDtypeStruct(s, jnp.float32) for s in shapes],
+        in_specs=[vmem] * 6,
+        out_specs=[vmem] * len(shapes),
+        compiler_params=pltpu.CompilerParams(vmem_limit_bytes=32 << 20),
+        name="finish_outputs",
+    )(*sums, small)
 
 
 def rotation_table(position):
@@ -1738,7 +2061,9 @@
     window_wide = jnp.broadcast_to(
         window.astype(jnp.float32)[:, None], (rows + 2 * HALO, LANES)
     )
-    key_segments = segments.astype(jnp.float32)[None]
+    key_segments = jnp.broadcast_to(
+        segments.astype(jnp.float32)[:, None], (segments.shape[0], LANES)
+    )
     table = rotation_table(offset + jnp.arange(rows, dtype=jnp.int32))
     starts = offset + jnp.arange(rows // TILE, dtype=jnp.int32) * TILE
     reach = segments[KEY_TILE - 1 :: KEY_TILE]
@@ -1756,9 +2081,9 @@
     )
     bias, rate = lanes_of(step_bias), lanes_of(-jnp.exp(log_rate))
     skip = jnp.repeat(skip_gain, inner // head_count)[None]
-    gate_z, pre, conv, raw, cum, y, states, query, memory = mixer_forward(
+    common = [
         tokens,
-        mixer_gain,
+        mixer_gain[None],
         window_wide,
         table,
         mamba_gate,
@@ -1768,9 +2093,9 @@
         query_weight,
         memory_weight,
         taps,
-        bias,
-        rate,
-        skip,
+    ]
+    gate_z, pre, conv, raw, cum, y, states, query, memory = mixer_forward(
+        *common, bias, rate, skip
     )
     all_memory = memory.reshape(memory.shape[0] * rows, memory.shape[2])
     attention, attention_low, logs = attention_forward(
@@ -1785,6 +2110,7 @@
         g_feed,
         g_mixed,
         g_down,
+        g_gate,
         g_feed_gain,
         g_mamba_gain,
     ) = feed_layer(
@@ -1793,6 +2119,7 @@
         attention_low,
         tokens,
         cotangent,
+        mixer_gain,
         mamba_gain,
         feed_gain,
         mamba_output,
@@ -1801,84 +2128,95 @@
         lift_weight,
         down_weight,
     )
-    d_query, d_memory = attention_back(
-        spans, query, all_memory, window_wide, key_segments, attention, logs, d_attention, table
-    )
-    grad_tokens, g_side, g_taps, g_mixer_gain, g_heads = mixer_back(
-        tokens,
-        mixer_gain,
-        window_wide,
-        table,
-        mamba_gate,
-        mamba_input,
-        mamba_maps,
-        step_weight,
-        query_weight,
-        memory_weight,
-        taps,
-        rate,
-        skip,
-        pre,
-        conv,
-        raw,
-        cum,
-        y,
-        states,
-        d_second,
-        d_y,
-        d_gate_z,
-        d_query,
-        d_memory.reshape(memory.shape),
-    )
-    small = jnp.concatenate(
-        [
-            g_taps[:tap_count],
-            jnp.pad(g_mamba_gain, ((0, 0), (0, wide - inner))),
-            g_mixer_gain,
-            g_feed_gain,
-            jnp.pad(g_heads[:3].reshape(1, 3 * LANES), ((0, 0), (0, wide - 3 * LANES))),
-        ],
-        axis=0,
-    )
-    (mixer_sum, feed_sum, mixed_sum, down_sum), small = reduce_gradients(
-        [g_side, g_feed, g_mixed, g_down], small
-    )
-    edges = [0]
-    for width in (
-        inner,
+    common += [rate, skip]
+    saved = [pre, conv, raw, cum, y, states, d_second, d_y, d_gate_z]
+    early = [g_down, g_feed, g_mixed, g_gate]
+    if lax.axis_size("seq") <= 4:
+        grad_tokens, *sums, small = mixer_back(
+            common,
+            saved,
+            [
+                query,
+                all_memory,
+                key_segments,
+                attention,
+                logs,
+                d_attention,
+                g_feed_gain,
+                g_mamba_gain,
+            ],
+            early,
+        )
+    else:
+        d_query, d_memory = attention_back(
+            spans, query, all_memory, window_wide, key_segments, attention, logs, d_attention, table
+        )
+        grad_tokens, g_side, g_taps, g_mixer_gain, g_heads = mixer_back(
+            common, saved, [d_query, d_memory.reshape(memory.shape)]
+        )
+        *sums, small = reduce_gradients(
+            early + [g_side],
+            jnp.concatenate(
+                [
+                    g_taps[:tap_count],
+                    jnp.pad(g_mamba_gain, ((0, 0), (0, wide - inner))),
+                    g_mixer_gain,
+                    g_feed_gain,
+                    jnp.pad(g_heads[:3].reshape(1, 3 * LANES), ((0, 0), (0, wide - 3 * LANES))),
+                ],
+                axis=0,
+            ),
+        )
+    sizes = (
         inner,
         conv_maps.shape[1],
-        LANES,
+        head_count,
         query_weight.shape[1],
-        memory_weight.shape[1],
-    ):
-        edges.append(edges[-1] + width)
-    pieces = [mixer_sum[:, a:b].astype(jnp.float32) for a, b in zip(edges[:-1], edges[1:])]
-    own_rows = wide // lax.axis_size("seq")
-    own_at = lax.axis_index("seq") * own_rows
-    feed = gate_weight.shape[1]
+        wide // lax.axis_size("seq"),
+    )
+    (
+        o_gate_z,
+        o_inner,
+        o_maps,
+        o_step,
+        o_output,
+        o_query,
+        o_memory,
+        o_attention,
+        o_gate,
+        o_lift,
+        o_down,
+        o_conv_inner,
+        o_conv_maps,
+        o_mixer_gain,
+        o_rate,
+        o_bias,
+        o_skip,
+        o_mamba_gain,
+        o_feed_gain,
+    ) = finish_outputs(sums, small, sizes)
     return (
         layer_out[None],
         grad_tokens[None],
-        lax.dynamic_slice_in_dim(small[5], own_at, own_rows),
-        pieces[0],
-        pieces[1],
-        pieces[2],
-        pieces[3][:, :head_count],
-        small[:tap_count, :inner],
-        small[:tap_count, inner:],
-        small[7, :head_count],
-        small[7, LANES : LANES + head_count],
-        small[7, 2 * LANES : 2 * LANES + head_count],
-        small[4, :inner],
-        mixed_sum[:, :inner].astype(jnp.float32),
-        pieces[4],
-        pieces[5],
-        mixed_sum[:, inner:].astype(jnp.float32),
-        lax.dynamic_slice_in_dim(small[6], own_at, own_rows),
-        feed_sum[:, :feed].astype(jnp.float32),
-        feed_sum[:, feed:].astype(jnp.float32),
-        down_sum.astype(jnp.float32),
+        o_mixer_gain[0],
+        o_gate_z,
+        o_inner,
+        o_maps,
+        o_step,
+        o_conv_inner,
+        o_conv_maps,
+        o_rate[0],
+        o_bias[0],
+        o_skip[0],
+        o_mamba_gain[0],
+        o_output,
+        o_query,
+        o_memory,
+        o_attention,
+        o_feed_gain[0],
+        o_gate,
+        o_lift,
+        o_down,
     )
 
 

time: 368 us -> 292 us (0.79)
  Pallas kernels: 328 us -> 271 us
  other arithmetic: 17.1 us -> 4.37 us
  local copies, waits for them, and re-layouts: 21 us -> 15.9 us
    pallas_call x4 -> x3, Pallas kernels: 286 us -> 234 us  [the longest x1 204 us: mixer_back(): pl.pallas_call(functools.partial(mixer_back_kernel, merged, chunks), out_...]
    convert_element_type x8 -> x1, other arithmetic: 11.2 us -> 0.01 us  [body(): segments.astype(jnp.float32)[:, None]]
    slice x5 -> x0, local copies, waits for them, and re-layouts: 5.57 us -> none  [the longest x1 1.34 us: body(): small[4, :inner]]
    unnamed x20 -> x34, local copies, waits for them, and re-layouts: 4.63 us -> 10.1 us
    pallas_call x1, Pallas kernels: 36 us -> 30.8 us  [feed_layer(): pl.pallas_call(feed_kernel, out_shape=[shape((rows, width), low), shape((...]
where the time goes in v3:
time: 292 us
  Pallas kernels  271 us (93%)
  local copies, waits for them, and re-layouts  15.9 us (5%)
  other arithmetic  4.37 us (1%)
    pallas_call x1, Pallas kernels, mixer_back(): pl.pallas_call(functools.partial(mixer_back_kernel, merged, chunks), out_...  204 us
    pallas_call x1, Pallas kernels, feed_layer(): pl.pallas_call(feed_kernel, out_shape=[shape((rows, width), low), shape((...  30.8 us
    pallas_call x1, Pallas kernels, mixer_forward(): pl.pallas_call(mixer_kernel, out_shape=[shape((rows, inner), full), shape...  26.7 us
    unnamed x34, local copies, waits for them, and re-layouts  10.1 us
    pallas_call x1, Pallas kernels, attention_forward(): pl.pallas_call(attention_kernel, out_shape=[jax.ShapeDtypeStruct((rows, w...  6.18 us

profile of v3, /device:TPU:0, one launch (start us, length us, event | category | flops | bytes accessed | tf_op | source)
XLA Modules:
  0.0 291.6 jit_solution(17584996836492078978)
XLA Ops:
  0.7 0.8 concatenate.9
  1.6 0.8 broadcast_in_dim.54.seg_ref.refs_2_
  2.4 1.0 multiply_cosine_fusion
  3.4 0.8 pad_maximum_fusion.table_ref.refs_3_
  4.3 0.9 copy.45
  5.2 0.8 pad.15.step_weight.refs_7_
  6.0 0.6 select_maximum_fusion.taps_ref.refs_10_
  7.2 0.7 broadcast_in_dim_reshape.3.skip_ref.refs_12_
  7.9 26.7 %mixer_forward.1 = (f32[512,768]{1,0:T(8,128)}, f32[520,1024]{1,0:T(8,128)}, f32[512,1024]{1,0:T(8,128)}, f32[512,128]{1,0:T(8,128)}, f32[512,128]{1,0:T(8,128)}...) custom-call(bf16[512,1024]{1,0:T(8,128)(2,1)} %bitcast.32, ...), custom_call_target="tpu_custom_call" | custom-call | tf_op jit(solution)/shard_map/mixer_forward/pallas_call | solution.py:1060
  34.8 0.7 convert_reduce_fusion.low_ref
  36.0 1.3 broadcast_in_dim.61.key_seg_ref.refs_24_
  37.3 6.2 %attention_forward.1 = (f32[512,256]{1,0:T(8,128)}, bf16[512,256]{1,0:T(8,128)(2,1)}, f32[4,8,512]{2,1,0:T(8,128)}) custom-call(s32[1]{0:T(128)} %bitcast.5.first_ref, s32[4]{0:T(128)} %convert_reduce_fusion.low_ref, s32[4]{0:T(128)} %and_select_fusion.high_ref, bf16[512,256]{1,0:T(8,128)(2,1)} %get-tuple-element.72.query_ref.refs_22_, ...), custom_call_target="tpu_custom_call" | custom-call | tf_op jit(solution)/shard_map/attention_forward/pallas_call | solution.py:1255
  44.1 30.8 %feed_layer.1 = (bf16[512,1024]{1,0:T(8,128)(2,1)}, f32[512,1024]{1,0:T(8,128)}, f32[512,768]{1,0:T(8,128)}, bf16[512,768]{1,0:T(8,128)(2,1)}, f32[512,256]{1,0:...) custom-call(f32[512,768]{1,0:T(8,128)} %get-tuple-element.70.y_ref.r, ...), custom_call_target="tpu_custom_call" | custom-call | tf_op jit(solution)/shard_map/feed_layer/pallas_call | solution.py:628
  74.9 204.1 %mixer_back.1 = (f32[512,1024]{1,0:T(8,128)}, bf16[2,2,64,1024]{3,2,1,0:T(8,128)(2,1)}, bf16[2,2,64,2048]{3,2,1,0:T(8,128)(2,1)}, bf16[2,2,64,1024]{3,2,1,0:T(8,...) custom-call(bf16[512,1024]{1,0:T(8,128)(2,1)} %bitcast.34, ...), custom_call_target="tpu_custom_call" | custom-call | tf_op jit(solution)/shard_map/mixer_back/pallas_call | solution.py:1916
  279.0 1.2 copy-done
  280.3 1.1 copy-done.1
  281.4 1.0 copy-done.2
  282.4 1.0 copy-done.3
  283.5 1.0 copy-done.4
  284.5 0.8 copy-done.5
  285.2 2.8 finish_outputs.1
  288.1 0.7 copy.46
  289.4 1.0 copy.49
  290.3 1.3 copy.50
  (38 shorter events, 2.6 us)
Async XLA Ops:
  0.7 5.3 %copy-start.10 = (f32[4,256]{1,0:T(4,128)S(1)}, f32[4,256]{1,0:T(4,128)}, u32[]{:S(2)}) copy-start(f32[4,256]{1,0:T(4,128)} %param.30) | copy-start | bytes 12292
  0.7 5.3 %copy-start.9 = (f32[4,768]{1,0:T(4,128)S(1)}, f32[4,768]{1,0:T(4,128)}, u32[]{:S(2)}) copy-start(f32[4,768]{1,0:T(4,128)} %param.29) | copy-start | bytes 36868
  0.7 5.9 %copy-start.14 = (f32[12]{0:T(128)S(1)}, f32[12]{0:T(128)}, u32[]{:S(2)}) copy-start(f32[12]{0:T(128)} %param.31) | copy-start | bytes 148
  0.7 5.9 %copy-start.13 = (f32[12]{0:T(128)S(1)}, f32[12]{0:T(128)}, u32[]{:S(2)}) copy-start(f32[12]{0:T(128)} %param.32) | copy-start | bytes 148
  0.7 6.5 %copy-start.12 = (f32[12]{0:T(128)S(1)}, f32[12]{0:T(128)}, u32[]{:S(2)}) copy-start(f32[12]{0:T(128)} %param.33) | copy-start | bytes 148
  7.9 26.7 %copy-start.8 = (s32[1,2048]{1,0:T(1,128)S(1)}, s32[1,2048]{1,0:T(1,128)}, u32[]{:S(2)}) copy-start(s32[1,2048]{1,0:T(1,128)} %param.23) | copy-start | bytes 24580
  34.6 8.9 %copy-start.11 = (f32[768]{0:T(1024)S(1)}, f32[768]{0:T(1024)}, u32[]{:S(2)}) copy-start(f32[768]{0:T(1024)} %param.34) | copy-start | bytes 9220
  74.9 214.5 %copy-start.7 = (bf16[512,1024]{1,0:T(8,128)(2,1)S(1)}, bf16[512,1024]{1,0:T(8,128)(2,1)}, u32[]{:S(2)}) copy-start(bf16[512,1024]{1,0:T(8,128)(2,1)} %get-tuple-element.75) | copy-start | bytes 3145732
  279.0 1.2 copy-start
  280.3 1.1 copy-start.1
  281.4 1.0 copy-start.2
  282.4 1.0 copy-start.3
  283.5 1.0 copy-start.4
  284.5 0.8 copy-start.5
  285.2 5.1 %copy-start.6 = (f32[512,1024]{1,0:T(8,128)S(1)}, f32[512,1024]{1,0:T(8,128)}, u32[]{:S(2)}) copy-start(f32[512,1024]{1,0:T(8,128)} %get-tuple-element.93) | copy-start | bytes 6291460

commit v4 on v3

--- a/solution.py
+++ b/solution.py
@@ -16,7 +16,11 @@
 
 LANES = 128
 MOST = 512
-AHEAD = 4
+TAIL = (512, 384, 256, 128, 128, 128)
+AHEAD = 7
+EARLIER = 3
+LAG = 3
+PATTERN = (0, 1, 2, 0, 1, 3, 0, 1, 0, 1, 2, 0, 1, 3, 0, 1)
 MESH = pl.DeviceIdType.MESH
 
 
@@ -44,17 +48,27 @@
     for group, width in enumerate(widths):
         count = -(-width // MOST)
         tiles = width // LANES
+        sizes = [(tiles // count + (1 if k < tiles % count else 0)) * LANES for k in range(count)]
+        if group == len(widths) - 1 and width == sum(TAIL):
+            sizes = TAIL
         start = 0
-        for k in range(count):
-            size = (tiles // count + (1 if k < tiles % count else 0)) * LANES
+        for size in sizes:
             chunks.append((group, start, size))
             start += size
     return chunks
 
 
+def seq_bits():
+    return (lax.axis_size("seq") - 1).bit_length()
+
+
+def place_bits(place, bits):
+    return tuple(lax.rem(place // 2 ** (bits - 1 - b), 2) for b in range(bits))
+
+
 def seq_blocks(grad):
-    count = lax.axis_size("seq")
-    return grad.reshape(count, 2, 2, grad.shape[0] // count // 4, grad.shape[1])
+    bits = seq_bits() + 2
+    return grad.reshape((2,) * bits + (grad.shape[0] >> bits, grad.shape[1]))
 
 
 def peer_device():
@@ -118,135 +132,135 @@
 
 
 class Reduction:
-    def __init__(self, chunks, sources, outs, scratch):
-        self.chunks, self.sources, self.outs = chunks, sources, outs
+    def __init__(self, chunks, sources, outs, scratch, given=()):
+        self.chunks, self.sources, self.outs, self.given = chunks, sources, outs, given
         groups = len(sources)
+        self.bits = seq_bits() + 2
         scratch = list(scratch)
-        self.first, self.second, self.third = (
-            scratch[:groups],
-            scratch[groups : 2 * groups],
-            scratch[2 * groups : 3 * groups],
-        )
-        self.own, self.sem_own, self.sem_one, self.sem_two, self.sem_seq, self.sem_back = scratch[
-            3 * groups :
-        ]
-        self.count = lax.axis_size("seq")
+        self.parts = [scratch[k * groups : (k + 1) * groups] for k in range(self.bits)]
+        self.own, self.sem_own, self.sem_halve, self.sem_back = scratch[self.bits * groups :]
+        self.setup()
+
+    def setup(self):
         self.seq, self.head = lax.axis_index("seq"), lax.axis_index("head")
         self.batch = lax.axis_index("batch")
-        self.low, self.high = lax.rem(self.batch, 2), self.batch // 2
-        self.low_peer = (self.seq, self.head, self.batch + 1 - 2 * self.low)
-        self.high_peer = (self.seq, self.head, self.batch + 2 - 4 * self.high)
-        self.turn = self.sent = self.held = self.limit = 0
+        place = self.seq * 4 + self.batch
+        self.mine = [lax.rem(place // 2 ** (self.bits - 1 - k), 2) for k in range(self.bits)]
+        self.done = [0] * (self.bits + 2)
+        self.sent = self.held = self.limit = 0
+
+    def peer(self, bit):
+        step = (1 - 2 * self.mine[bit]) * 2 ** (self.bits - 1 - bit)
+        if bit < self.bits - 2:
+            return (self.seq + step // 4, self.head, self.batch)
+        return (self.seq, self.head, self.batch + step)
+
+    def order(self, k):
+        low, high, last = self.bits - 1, self.bits - 2, self.bits - 3
+        rest = [b for b in range(self.bits - 3, -1, -1)]
+        if last < 0:
+            return [low, high] if k % 2 == 0 else [high, low]
+        kind = PATTERN[k % len(PATTERN)]
+        if kind == 0:
+            return [low, high] + rest
+        if kind == 1:
+            return [high, low] + rest
+        if kind == 2:
+            return [last, low, high] + rest[1:]
+        return [last, high, low] + rest[1:]
 
     def place(self, k):
         group, start, size = self.chunks[k]
         return group, pl.ds(start, size)
 
+    def cut(self, k, step, kept):
+        order = self.order(k)
+        left = [b for b in range(self.bits) if b not in order[:step]]
+        bit = order[step]
+        value = self.mine[bit] if kept else 1 - self.mine[bit]
+        return tuple(value if b == bit else slice(None) for b in left)
+
+    def halve_copy(self, k, step):
+        group, columns = self.place(k)
+        source = self.sources[group] if step == 0 else self.parts[step - 1][group]
+        target = self.parts[step][group]
+        away = self.cut(k, step, False)
+        return exchange(
+            source.at[away + (slice(None), columns)],
+            target.at[(slice(None),) * (len(away) - 1) + (slice(None), columns)],
+            self.sem_halve.at[0, k, step],
+            self.sem_halve.at[1, k, step],
+            self.peer(self.order(k)[step]),
+        )
+
     def first_copy(self, k):
         group, columns = self.place(k)
-        if k % 2 == 0:
-            part, peer = (
-                self.sources[group].at[:, :, 1 - self.low, :, columns],
-                self.low_peer,
-            )
-        else:
-            part, peer = (
-                self.sources[group].at[:, 1 - self.high, :, :, columns],
-                self.high_peer,
-            )
-        return exchange(
-            part,
-            self.first[group].at[:, :, :, columns],
-            self.sem_one.at[0, k],
-            self.sem_one.at[1, k],
-            peer,
+        if group >= len(self.given) or k >= EARLIER:
+            return self.halve_copy(k, 0)
+        where = (slice(None),) * self.bits + (columns,)
+        return pltpu.make_async_copy(
+            self.given[group].at[where], self.parts[0][group].at[where], self.sem_halve.at[0, k, 0]
         )
 
     def own_copy(self, k):
         group, columns = self.place(k)
         size = self.chunks[k][2]
-        if k % 2 == 0:
-            part = self.sources[group].at[:, :, self.low, :, columns]
-        else:
-            part = self.sources[group].at[:, self.high, :, :, columns]
+        kept = self.cut(k, 0, True)
         return pltpu.make_async_copy(
-            part, self.own.at[k % 2, :, :, :, pl.ds(0, size)], self.sem_own.at[k]
-        )
-
-    def second_copy(self, k):
+            self.sources[group].at[kept + (slice(None), columns)],
+            self.own.at[(k % 2,) + (slice(None),) * self.bits + (pl.ds(0, size),)],
+            self.sem_own.at[k],
+        )
+
+    def add(self, k, step):
         group, columns = self.place(k)
-        if k % 2 == 0:
-            away, peer = 1 - self.high, self.high_peer
-        else:
-            away, peer = 1 - self.low, self.low_peer
-        return exchange(
-            self.first[group].at[:, away, :, columns],
-            self.second[group].at[:, :, columns],
-            self.sem_two.at[0, k],
-            self.sem_two.at[1, k],
-            peer,
-        )
-
-    def seq_copy(self, k, step):
-        group, columns = self.place(k)
-        place = lax.rem(self.seq + step, self.count)
-        return exchange(
-            self.second[group].at[place, :, columns],
-            self.third[group].at[step - 1, :, columns],
-            self.sem_seq.at[0, k, step - 1],
-            self.sem_seq.at[1, k, step - 1],
-            (place, self.head, self.batch),
+        size = self.chunks[k][2]
+        target = self.parts[step][group]
+        left = self.bits - 1 - step
+
+        def one(index):
+            every = index + (slice(None), columns)
+            if step == 0:
+                own = self.own[(k % 2,) + index + (slice(None), slice(0, size))]
+            else:
+                kept = self.cut(k, step, True)
+                spot = [v for v in kept]
+                rest = iter(index)
+                spot = tuple(v if not isinstance(v, slice) else next(rest) for v in spot)
+                own = self.parts[step - 1][group][spot + (slice(None), columns)]
+            value = own + target[every]
+            if step == self.bits - 1:
+                self.outs[group][self.mine[-2], self.mine[-1], :, columns] = value
+            else:
+                target[every] = value
+
+        span(
+            0,
+            2**left,
+            lambda n: one(place_bits(n, left)),
         )
 
     def back_copy(self, k, turn):
         group, columns = self.place(k)
         out = self.outs[group]
-        peer = self.high_peer if (k + turn) % 2 == 0 else self.low_peer
+        high, low = self.mine[-2], self.mine[-1]
+        first_low = self.order(k).index(self.bits - 1) < self.order(k).index(self.bits - 2)
+        bit = self.bits - 2 if first_low == (turn == 0) else self.bits - 1
         if turn == 0:
-            part = out.at[self.high, self.low, :, columns]
-        elif k % 2 == 0:
-            part = out.at[:, self.low, :, columns]
+            part = out.at[high, low, :, columns]
+        elif first_low:
+            part = out.at[:, low, :, columns]
         else:
-            part = out.at[self.high, :, :, columns]
-        return exchange(part, part, self.sem_back.at[0, k, turn], self.sem_back.at[1, k, turn], peer)
-
-    def add_first(self, k):
-        group, columns = self.place(k)
-        size = self.chunks[k][2]
-
-        def one(place):
-            own = self.own[k % 2, place, :, :, :size].astype(jnp.float32)
-            came = self.first[group][place, :, :, columns].astype(jnp.float32)
-            self.first[group][place, :, :, columns] = (own + came).astype(jnp.bfloat16)
-
-        each(self.count, one)
-
-    def add_second(self, k):
-        group, columns = self.place(k)
-        keep = self.high if k % 2 == 0 else self.low
-
-        def one(place):
-            own = self.first[group][place, keep, :, columns].astype(jnp.float32)
-            came = self.second[group][place, :, columns].astype(jnp.float32)
-            self.second[group][place, :, columns] = (own + came).astype(jnp.bfloat16)
-
-        each(self.count, one)
-
-    def add_third(self, k):
-        group, columns = self.place(k)
-        total = lax.fori_loop(
-            0,
-            self.count - 1,
-            lambda slot, total: total + self.third[group][slot, :, columns].astype(jnp.float32),
-            self.second[group][self.seq, :, columns].astype(jnp.float32),
-        )
-        self.outs[group][self.high, self.low, :, columns] = total.astype(jnp.bfloat16)
+            part = out.at[high, :, :, columns]
+        return exchange(
+            part, part, self.sem_back.at[0, k, turn], self.sem_back.at[1, k, turn], self.peer(bit)
+        )
 
     def refill(self):
-        while self.sent < min(self.limit, self.turn + AHEAD):
+        while self.sent < min(self.limit, self.done[0] + AHEAD):
             self.first_copy(self.sent).start()
             self.sent += 1
-        while self.held < min(self.limit, self.turn + 2):
+        while self.held < min(self.limit, self.done[0] + 2):
             self.own_copy(self.held).start()
             self.held += 1
 
@@ -255,56 +269,60 @@
         self.refill()
 
     def advance(self):
-        total = len(self.chunks)
-        k = self.turn
-        if k < total:
-            self.first_copy(k).wait()
-            self.own_copy(k).wait()
-            self.add_first(k)
-            self.second_copy(k).start()
-        self.turn += 1
-        self.refill()
-        k = self.turn - 2
-        if 0 <= k < total:
-            self.second_copy(k).wait()
-            self.add_second(k)
-            span(1, self.count, lambda step: self.seq_copy(k, step).start())
-        k = self.turn - 3
-        if 0 <= k < total:
-            span(1, self.count, lambda step: self.seq_copy(k, step).wait())
-            self.add_third(k)
-            self.back_copy(k, 0).start()
-        k = self.turn - 4
-        if 0 <= k < total:
-            self.back_copy(k, 0).wait()
-            self.back_copy(k, 1).start()
-        k = self.turn - 5
-        if 0 <= k < total:
-            self.back_copy(k, 1).wait()
+        stages = self.bits + 2
+        for step in range(stages - 1, -1, -1):
+            k = self.done[step]
+            before = self.done[step - 1] if step else self.limit
+            if k >= before or (step and before - k < LAG and before < self.limit):
+                continue
+            if step < self.bits:
+                if step == 0:
+                    self.first_copy(k).wait()
+                    self.own_copy(k).wait()
+                else:
+                    self.halve_copy(k, step).wait()
+                self.add(k, step)
+                if step + 1 < self.bits:
+                    self.halve_copy(k, step + 1).start()
+                else:
+                    self.back_copy(k, 0).start()
+            elif step == self.bits:
+                self.back_copy(k, 0).wait()
+                self.back_copy(k, 1).start()
+            else:
+                self.back_copy(k, 1).wait()
+            self.done[step] += 1
+            if step == 0:
+                self.refill()
 
     def finish(self):
-        while self.turn < len(self.chunks) + 4:
+        while self.done[-1] < len(self.chunks):
             self.advance()
 
 
+class FirstHalving(Reduction):
+    def __init__(self, chunks, sources, targets, sems):
+        self.chunks, self.sources = chunks, sources
+        self.bits = seq_bits() + 2
+        self.parts, self.sem_halve = [targets], sems
+        self.setup()
+
+
 def reduction_scratch(chunks, widths, rows):
-    count = lax.axis_size("seq")
+    bits = seq_bits() + 2
     parts = len(chunks)
     most = max(size for _, _, size in chunks)
     low = jnp.bfloat16
-    return (
-        [pltpu.VMEM((count, 2, rows, w), low) for w in widths]
-        + [pltpu.VMEM((count, rows, w), low) for w in widths]
-        + [pltpu.VMEM((max(count - 1, 1), rows, w), low) for w in widths]
-        + [
-            pltpu.VMEM((2, count, 2, rows, most), low),
-            pltpu.SemaphoreType.DMA((parts,)),
-            pltpu.SemaphoreType.DMA((2, parts)),
-            pltpu.SemaphoreType.DMA((2, parts)),
-            pltpu.SemaphoreType.DMA((2, parts, max(count - 1, 1))),
-            pltpu.SemaphoreType.DMA((2, parts, 2)),
-        ]
-    )
+    return [
+        pltpu.VMEM((2,) * (bits - 1 - step) + (rows, w), low)
+        for step in range(bits)
+        for w in widths
+    ] + [
+        pltpu.VMEM((2,) * bits + (rows, most), low),
+        pltpu.SemaphoreType.DMA((parts,)),
+        pltpu.SemaphoreType.DMA((2, parts, bits)),
+        pltpu.SemaphoreType.DMA((2, parts, 2)),
+    ]
 
 
 def reduce_kernel(chunks, *refs):
@@ -327,7 +345,7 @@
     widths = [g.shape[1] for g in grads]
     chunks = column_chunks(widths)
     blocks = [seq_blocks(g) for g in grads]
-    rows = blocks[0].shape[3]
+    rows = blocks[0].shape[-2]
     vmem = pl.BlockSpec(memory_space=pltpu.VMEM)
     return pl.pallas_call(
         functools.partial(reduce_kernel, chunks),
@@ -366,9 +384,10 @@
     return 1.0 / (1.0 + jnp.exp(-v))
 
 
-def greet_peer(barrier, peer):
-    pl.semaphore_signal(barrier, inc=1, device_id=peer, device_id_type=MESH)
-    pl.semaphore_wait(barrier, 1)
+def greet(barrier, devices):
+    for device in devices:
+        pl.semaphore_signal(barrier, inc=1, device_id=device, device_id_type=MESH)
+    pl.semaphore_wait(barrier, len(devices))
 
 
 def tile_rows(i):
@@ -382,62 +401,69 @@
     return pl.ds(pl.multiple_of(i * FEED_TILE, FEED_TILE), FEED_TILE)
 
 
-def feed_kernel(
-    y_ref,
-    gate_z_ref,
-    attention_ref,
-    tokens_ref,
-    cotangent_ref,
-    mixer_gain_ref,
-    mamba_gain_ref,
-    feed_gain_ref,
-    mamba_output_ref,
-    attention_out_ref,
-    gate_weight_hbm,
-    lift_weight_hbm,
-    down_weight_hbm,
-    out_ref,
-    d_second_ref,
-    d_y_ref,
-    d_gate_z_ref,
-    d_attention_ref,
-    g_feed_ref,
-    g_mixed_ref,
-    g_down_ref,
-    g_gate_ref,
-    g_feed_gain_ref,
-    g_mamba_gain_ref,
-    gate_weight,
-    lift_weight,
-    down_weight,
-    normed,
-    gated,
-    g_six,
-    inverse_six,
-    second,
-    inverse_two,
-    normed2,
-    active,
-    d_feed,
-    d_mix,
-    d_gated,
-    square_send,
-    square_recv,
-    cross_send,
-    cross_recv,
-    mixed_send,
-    mixed_recv,
-    lift_send,
-    lift_recv,
-    norm_send,
-    norm_recv,
-    weight_sem,
-    sem_square,
-    sem_cross,
-    sem_mixed,
-    sem_lift,
-    sem_norm,
-):
+def feed_kernel(merged, *refs):
+    (
+        y_ref,
+        gate_z_ref,
+        attention_ref,
+        tokens_ref,
+        cotangent_ref,
+        mixer_gain_ref,
+        mamba_gain_ref,
+        feed_gain_ref,
+        mamba_output_ref,
+        attention_out_ref,
+        gate_weight_hbm,
+        lift_weight_hbm,
+        down_weight_hbm,
+        out_ref,
+        d_second_ref,
+        d_y_ref,
+        d_gate_z_ref,
+        d_attention_ref,
+        g_feed_ref,
+        g_mixed_ref,
+        g_down_ref,
+        g_gate_ref,
+        g_feed_gain_ref,
+        g_mamba_gain_ref,
+    ) = refs[: 24]
+    refs = refs[24:]
+    if merged:
+        came_refs, refs = refs[:2], refs[2:]
+    (
+        gate_weight,
+        lift_weight,
+        down_weight,
+        normed,
+        gated,
+        g_six,
+        inverse_six,
+        second,
+        inverse_two,
+        normed2,
+        active,
+        d_feed,
+        d_mix,
+        d_gated,
+        square_send,
+        square_recv,
+        cross_send,
+        cross_recv,
+        mixed_send,
+        mixed_recv,
+        lift_send,
+        lift_recv,
+        norm_send,
+        norm_recv,
+        weight_sem,
+        sem_square,
+        sem_cross,
+        sem_mixed,
+        sem_lift,
+        sem_norm,
+        *sem_first,
+    ) = refs
     rows = y_ref.shape[0]
     tiles = rows // FEED_TILE
     inner = y_ref.shape[1]
@@ -457,7 +483,16 @@
     ]
     for load in loads:
         load.start()
-    greet_peer(pltpu.get_barrier_semaphore(), peer)
+    devices = [peer]
+    if merged:
+        first = FirstHalving(
+            column_chunks((g_down_ref.shape[-1], g_feed_ref.shape[-1]))[:EARLIER],
+            [g_down_ref, g_feed_ref],
+            came_refs,
+            sem_first[0],
+        )
+        devices += [first.peer(bit) for bit in range(first.bits - 3, first.bits)]
+    greet(pltpu.get_barrier_semaphore(), devices)
 
     def swap(send, recv, sems, i):
         rows_now = feed_rows(i)
@@ -524,6 +559,28 @@
         swap(norm_send, norm_recv, sem_norm, i).start()
 
     each(tiles, feed_tile)
+    blocks = lax.axis_size("seq") if merged else width // 256
+
+    def store(target, k, grad):
+        if merged:
+            index = place_bits(k, seq_bits())
+            target[index] = grad.reshape(target.shape[len(index) :]).astype(jnp.bfloat16)
+        else:
+            target[pl.ds(pl.multiple_of(k * 256, 256), 256), :] = grad.astype(jnp.bfloat16)
+
+    def block_columns(k):
+        size = width // blocks
+        return pl.ds(pl.multiple_of(k * size, LANES), size)
+
+    def feed_weights(k):
+        block = block_columns(k)
+        store(g_down_ref, k, matmul_first(cotangent_ref[:, block], active[...]))
+        store(g_feed_ref, k, matmul_first(normed2[:, block], d_feed[...]))
+
+    each(blocks, feed_weights)
+    if merged:
+        for k in range(EARLIER):
+            first.halve_copy(k, 0).start()
     g_feed_gain_ref[...] = jnp.zeros_like(g_feed_gain_ref)
     g_mamba_gain_ref[...] = jnp.zeros_like(g_mamba_gain_ref)
 
@@ -583,22 +640,20 @@
 
     each(tiles, out_tile)
 
-    def weight_block(k):
-        block = pl.ds(pl.multiple_of(k * 256, 256), 256)
-        g_down_ref[block, :] = matmul_first(cotangent_ref[:, block], active[...]).astype(
-            jnp.bfloat16
-        )
-        g_feed_ref[block, :] = matmul_first(normed2[:, block], d_feed[...]).astype(jnp.bfloat16)
-        g_gate_ref[block, :] = matmul_first(normed[:, block], d_gate_z_ref[...]).astype(
-            jnp.bfloat16
-        )
+    def mixed_weights(k):
+        block = block_columns(k)
+        store(g_gate_ref, k, matmul_first(normed[:, block], d_gate_z_ref[...]))
         d_mix_now = d_mix[:, block]
-        g_mixed_ref[block, :inner] = matmul_first(d_mix_now, gated[...]).astype(jnp.bfloat16)
-        g_mixed_ref[block, inner:] = matmul_first(d_mix_now, attention_ref[...]).astype(
-            jnp.bfloat16
-        )
-
-    each(width // 256, weight_block)
+        grad = jnp.concatenate(
+            [matmul_first(d_mix_now, gated[...]), matmul_first(d_mix_now, attention_ref[...])],
+            axis=1,
+        )
+        store(g_mixed_ref, k, grad)
+
+    each(blocks, mixed_weights)
+    if merged:
+        for k in range(EARLIER):
+            first.halve_copy(k, 0).wait()
 
 
 def feed_layer(
@@ -625,23 +680,35 @@
     hbm = pl.BlockSpec(memory_space=pl.ANY)
     low, full = jnp.bfloat16, jnp.float32
     shape = jax.ShapeDtypeStruct
-    return pl.pallas_call(
-        feed_kernel,
-        out_shape=[
+    merged = lax.axis_size("seq") == 4
+
+    def grad_shape(columns):
+        if merged:
+            return shape((2,) * (seq_bits() + 2) + (width // 16, columns), low)
+        return shape((width, columns), low)
+
+    out_shape = [
             shape((rows, width), low),
             shape((rows, width), full),
             shape((rows, inner), full),
             shape((rows, inner), low),
             shape((rows, att), full),
-            shape((width, 2 * feed), low),
-            shape((width, inner + att), low),
-            shape((width, feed), low),
-            shape((width, inner), low),
+            grad_shape(2 * feed),
+            grad_shape(inner + att),
+            grad_shape(feed),
+            grad_shape(inner),
             shape((1, width), full),
             shape((1, inner), full),
-        ],
+        ]
+    scratch = []
+    if merged:
+        out_shape += [shape((2,) * 3 + (width // 16, n), low) for n in (feed, MOST)]
+        scratch = [pltpu.SemaphoreType.DMA((2, EARLIER, 1))]
+    return pl.pallas_call(
+        functools.partial(feed_kernel, merged),
+        out_shape=out_shape,
         in_specs=[vmem] * 10 + [hbm] * 3,
-        out_specs=[vmem] * 11,
+        out_specs=[vmem] * len(out_shape),
         scratch_shapes=[
             pltpu.VMEM((width, feed), low),
             pltpu.VMEM((width, feed), low),
@@ -664,7 +731,8 @@
         ]
         + [pltpu.VMEM((rows, width), low)] * 6
         + [pltpu.SemaphoreType.DMA((3,))]
-        + [pltpu.SemaphoreType.DMA((2, tiles))] * 5,
+        + [pltpu.SemaphoreType.DMA((2, tiles))] * 5
+        + scratch,
         compiler_params=pltpu.CompilerParams(
             collective_id=1, has_side_effects=True, vmem_limit_bytes=60 << 20
         ),
@@ -832,7 +900,7 @@
     )
 
     def memory_tile(i):
-        at = tile_rows(i)
+        at = feed_rows(i)
         hidden = tokens_ref[at, :].astype(jnp.float32)
         inverse = lax.rsqrt(jnp.mean(hidden * hidden, axis=1, keepdims=True) + eps_norm)
         low = (hidden * inverse * gain_ref[...]).astype(jnp.bfloat16)
@@ -842,7 +910,8 @@
         turned = value * table_ref[at, :LANES] + turn_half(value) * table_ref[at, LANES:]
         memory_ref[seq, at, :] = jnp.where(lane < HD, turned, value).astype(jnp.bfloat16)
 
-    each(tiles, memory_tile)
+    wide_tiles = rows // FEED_TILE
+    each(wide_tiles, memory_tile)
 
     def memory_start(step, carry):
         @pl.when(seq + step < count)
@@ -854,13 +923,13 @@
     lax.fori_loop(1, count, memory_start, 0)
 
     def pre_tile(i):
-        at = tile_rows(i)
-        to = pl.ds(pl.multiple_of(i * TILE + HALO, HALO), TILE)
+        at = feed_rows(i)
+        to = pl.ds(pl.multiple_of(i * FEED_TILE + HALO, HALO), FEED_TILE)
         low = normed[at, :]
         pre_ref[to, :inner] = matmul(low, input_weight[...])
         pre_ref[to, inner:] = matmul(low, maps_weight[...])
 
-    each(tiles, lambda i: pre_tile(tiles - 1 - i))
+    each(wide_tiles, lambda i: pre_tile(wide_tiles - 1 - i))
 
     @pl.when(seq < count - 1)
     def _():
@@ -869,22 +938,13 @@
     spread_ref[...] = spread_matrix(inner, HD)
     lower = jnp.where(ordered(CHUNK), 1.0, 0.0)
 
-    def project_tile(i):
+    def step_tile(i):
         at = tile_rows(i)
-        low = normed[at, :]
-        gate_z_ref[at, :] = matmul(low, gate_weight[...])
-        raw = matmul(low, step_weight[...]) + bias_ref[...]
+        raw = matmul(normed[at, :], step_weight[...]) + bias_ref[...]
         raw_ref[at, :] = raw
-        cum_ref[at, :] = jnp.dot(
-            lower, rate_ref[...] * soft_plus(raw), precision=highest
-        )
-        value = matmul(low, query_weight[...])
-        for k in range(value.shape[1] // LANES):
-            part = value[:, k * LANES : (k + 1) * LANES]
-            turned = part * table_ref[at, :LANES] + turn_half(part) * table_ref[at, LANES:]
-            query_ref[at, k * LANES : (k + 1) * LANES] = turned.astype(jnp.bfloat16)
-
-    each(tiles, project_tile)
+        cum_ref[at, :] = jnp.dot(lower, rate_ref[...] * soft_plus(raw), precision=highest)
+
+    each(tiles, step_tile)
 
     @pl.when(seq == 0)
     def _():
@@ -981,6 +1041,20 @@
 
     each(tiles, inside_chunk)
 
+    def project_tile(i):
+        at = feed_rows(i)
+        low = normed[at, :]
+        gate_z_ref[at, :] = matmul(low, gate_weight[...])
+        value = matmul(low, query_weight[...])
+        for k in range(value.shape[1] // LANES):
+            part = value[:, k * LANES : (k + 1) * LANES]
+            turned = part * table_ref[at, :LANES] + turn_half(part) * table_ref[at, LANES:]
+            query_ref[at, k * LANES : (k + 1) * LANES] = turned.astype(jnp.bfloat16)
+
+    @pl.when(seq >= 2)
+    def _():
+        each(wide_tiles, project_tile)
+
     @pl.when(seq > 0)
     def _():
         for p in range(pieces):
@@ -995,6 +1069,10 @@
                     came * total[:1, columns] + local[:, columns]
                 ).astype(jnp.bfloat16)
                 chain_copy(p).start()
+
+    @pl.when(seq < 2)
+    def _():
+        each(wide_tiles, project_tile)
 
     def across_chunk(c):
         at = tile_rows(c)
@@ -1110,7 +1188,7 @@
     )
 
 
-KEY_TILE = 256
+KEY_TILE = 512
 
 
 def stacked_heads(values, first, factor):
@@ -1139,12 +1217,11 @@
     return tiles
 
 
-def key_tile(seg_turned, key_seg_ref, first, i, k, heads):
+def key_tile(seg_turned, key_seg_ref, first, i, k):
     at = pl.ds(pl.multiple_of(k * KEY_TILE, KEY_TILE), KEY_TILE)
     place = k * KEY_TILE + lax.broadcasted_iota(jnp.int32, (KEY_TILE, TILE), 0)
     row = first + i * TILE + lax.broadcasted_iota(jnp.int32, (KEY_TILE, TILE), 1)
-    allowed = jnp.where((place <= row) & (key_seg_ref[at, :] == seg_turned), 1.0, 0.0)
-    return at, jnp.concatenate([allowed] * heads, axis=1) > 0.5
+    return at, (place <= row) & (key_seg_ref[at, :] == seg_turned)
 
 
 def query_segments(seg_ref, i):
@@ -1156,32 +1233,32 @@
     heads = queries_in.shape[1] // HD
     turned = stacked_heads(queries_in, True, HD ** (-0.5)).T.astype(jnp.bfloat16)
     segs = query_segments(seg_ref, i)
-    wide = heads * TILE
+    parts = [turned[:, h * TILE : (h + 1) * TILE] for h in range(heads)]
 
     def one(step, carry):
-        most, total, acc = carry
-        k = high - step
-        at, allowed = key_tile(segs, key_seg_ref, first, i, k, heads)
+        at, allowed = key_tile(segs, key_seg_ref, first, i, high - step)
         keys = memory_of(at)
-        scores = jnp.where(allowed, matmul(keys, turned), neg_large)
-        new = jnp.maximum(most, jnp.max(scores, axis=0, keepdims=True))
-        weights = jnp.exp(scores - new)
-        factor = jnp.exp(most - new)
-        total = total * factor + jnp.sum(weights, axis=0, keepdims=True)
-        acc = acc * factor + matmul_first(keys, weights.astype(jnp.bfloat16))
-        return new, total, acc
-
-    most, total, acc = lax.fori_loop(
-        0,
-        high - low + 1,
-        one,
-        (
-            jnp.full((1, wide), neg_large, jnp.float32),
-            jnp.zeros((1, wide), jnp.float32),
-            jnp.zeros((LANES, wide), jnp.float32),
-        ),
+        after = []
+        for part, (most, total, acc) in zip(parts, carry):
+            scores = jnp.where(allowed, matmul(keys, part), neg_large)
+            new = jnp.maximum(most, jnp.max(scores, axis=0, keepdims=True))
+            weights = jnp.exp(scores - new)
+            factor = jnp.exp(most - new)
+            total = total * factor + jnp.sum(weights, axis=0, keepdims=True)
+            acc = acc * factor + matmul_first(keys, weights.astype(jnp.bfloat16))
+            after.append((new, total, acc))
+        return tuple(after)
+
+    zero = (
+        jnp.full((1, TILE), neg_large, jnp.float32),
+        jnp.zeros((1, TILE), jnp.float32),
+        jnp.zeros((LANES, TILE), jnp.float32),
     )
-    return acc / total, most + jnp.log(total)
+    result = lax.fori_loop(0, high - low + 1, one, (zero,) * heads)
+    return (
+        jnp.concatenate([acc / total for _, total, acc in result], axis=1),
+        jnp.concatenate([most + jnp.log(total) for most, total, _ in result], axis=1),
+    )
 
 
 def attend_back_block(
@@ -1198,21 +1275,28 @@
     pick = jnp.where(lane // HD == row, 1.0, 0.0).astype(jnp.bfloat16)
     high_part, low_part = two_parts(d_out * out)
     deltas = matmul_last(pick, high_part) + matmul_last(pick, low_part)
-    delta = jnp.concatenate([deltas[h : h + 1] for h in range(heads)], axis=1)
-
-    def one(step, total):
-        at, allowed = key_tile(segs, key_seg_ref, first, i, high - step, heads)
+    spans = [slice(h * TILE, (h + 1) * TILE) for h in range(heads)]
+
+    def one(step, totals):
+        at, allowed = key_tile(segs, key_seg_ref, first, i, high - step)
         keys = memory_of(at)
-        weights = jnp.exp(matmul(keys, queries_turned) - log)
-        weights = jnp.where(allowed, weights, 0.0)
-        slope = (weights * (matmul(keys, outer_turned) - delta)).astype(jnp.bfloat16)
-        grads[at, :] += matmul(slope, queries) + matmul(weights.astype(jnp.bfloat16), outer)
-        return total + matmul_first(keys, slope)
-
-    total = lax.fori_loop(
-        0, high - low + 1, one, jnp.zeros((LANES, heads * TILE), jnp.float32)
+        slopes, lows, after = [], [], []
+        for h, (part, total) in enumerate(zip(spans, totals)):
+            weights = jnp.exp(matmul(keys, queries_turned[:, part]) - log[:, part])
+            weights = jnp.where(allowed, weights, 0.0)
+            slope = weights * (matmul(keys, outer_turned[:, part]) - deltas[h : h + 1])
+            slopes.append(slope.astype(jnp.bfloat16))
+            lows.append(weights.astype(jnp.bfloat16))
+            after.append(total + matmul_first(keys, slopes[-1]))
+        grads[at, :] += matmul(jnp.concatenate(slopes, axis=1), queries) + matmul(
+            jnp.concatenate(lows, axis=1), outer
+        )
+        return tuple(after)
+
+    totals = lax.fori_loop(
+        0, high - low + 1, one, (jnp.zeros((LANES, TILE), jnp.float32),) * heads
     )
-    return total * HD ** (-0.5)
+    return jnp.concatenate(totals, axis=1) * HD ** (-0.5)
 
 
 def attention_kernel(
@@ -1324,14 +1408,30 @@
     )(*spans, query, memory, segments, key_segments, out, logs, d_out, table)
 
 
+MERGED_INPUTS = 30
+
+
 def mixer_back_kernel(merged, chunks, *refs):
     refs = list(refs)
 
-    def take(names):
+    def take(count):
         nonlocal refs
-        now, refs = refs[: len(names)], refs[len(names) :]
+        now, refs = refs[:count], refs[count:]
         return now
 
+    if merged:
+        given = take(MERGED_INPUTS)
+        early, came = take(4), take(2)
+        d_tokens_ref, *outs, small_out = take(7)
+        copies = take(MERGED_INPUTS)
+        (sem_load,) = take(1)
+        loads = [
+            pltpu.make_async_copy(source, target, sem_load.at[k])
+            for k, (source, target) in enumerate(zip(given, copies))
+        ]
+        for load in loads:
+            load.start()
+        refs = copies + refs
     (
         tokens_ref,
         gain_ref,
@@ -1355,7 +1455,7 @@
         d_second_ref,
         d_y_ref,
         d_gate_z_ref,
-    ) = take(range(22))
+    ) = take(22)
     if merged:
         (
             query_ref,
@@ -1366,12 +1466,10 @@
             d_attention_ref,
             feed_gain_ref,
             mamba_gain_ref,
-        ) = take(range(8))
-        early = take(range(4))
-        d_tokens_ref, *outs, small_out = take(range(7))
+        ) = take(8)
     else:
-        d_query_ref, d_memory_ref = take(range(2))
-        d_tokens_ref, g_side_ref, g_taps_ref, g_gain_ref, g_heads_ref = take(range(5))
+        d_query_ref, d_memory_ref = take(2)
+        d_tokens_ref, g_side_ref, g_taps_ref, g_gain_ref, g_heads_ref = take(5)
     (
         normed,
         spread_ref,
@@ -1398,9 +1496,9 @@
         sem_chain,
         sem_maps,
         sem_norm,
-    ) = take(range(25))
+    ) = take(25)
     if merged:
-        g_side_ref, grads, d_memory_ref, small_in, small_buf, sem_small = take(range(6))
+        g_side_ref, grads, d_memory_ref, small_in, small_buf, sem_small = take(6)
         g_taps_ref = g_gain_ref = g_heads_ref = small_in
     seq, head, batch = lax.axis_index("seq"), lax.axis_index("head"), lax.axis_index("batch")
     count = lax.axis_size("seq")
@@ -1418,9 +1516,11 @@
     memory_at = query_at + query_weight.shape[1]
     if merged:
         greet_all(pltpu.get_barrier_semaphore(), True)
-        reduction = Reduction(chunks, list(early) + [g_side_ref], outs, refs)
+        reduction = Reduction(chunks, list(early) + [g_side_ref], outs, refs, came)
         reduction.allow(sum(1 for c in chunks if c[0] < len(early)))
         advance = reduction.advance
+        for load in loads:
+            load.wait()
     else:
         greet_seq(pltpu.get_barrier_semaphore(), 1)
 
@@ -1533,17 +1633,8 @@
                 columns = pl.ds(query_at + pair * LANES, LANES)
                 side[at, columns] = turned.astype(jnp.bfloat16)
 
-        half = tiles // 2
-        span(0, half, attention_block)
+        span(0, 1, attention_block)
         advance()
-        span(half, tiles, attention_block)
-        advance()
-
-        def low_block(place):
-            at = pl.ds(pl.multiple_of(place * rows, rows), rows)
-            d_memory_ref[place] = grads[at, :].astype(jnp.bfloat16)
-
-        each(count, low_block)
 
     def chain_wait(p):
         columns = pl.ds(p * PIECE, PIECE)
@@ -1561,6 +1652,17 @@
                 jnp.bfloat16
             )
             chain_copy(p).start()
+
+    if merged:
+        for i in range(1, tiles):
+            span(i, i + 1, attention_block)
+            advance()
+
+        def low_block(place):
+            at = pl.ds(pl.multiple_of(place * rows, rows), rows)
+            d_memory_ref[place] = grads[at, :].astype(jnp.bfloat16)
+
+        each(count, low_block)
 
     def memory_start(step, carry):
         @pl.when(seq - step >= 0)
@@ -1774,18 +1876,18 @@
     each(tiles, memory_tile)
 
     def weight_block(k):
-        block = pl.ds(pl.multiple_of(k * 256, 256), 256)
+        size = model // count
+        block = pl.ds(pl.multiple_of(k * size, LANES), size)
         grad = matmul_first(normed[:, block], side[...])
         if merged:
-            _, high, low, own, columns = g_side_ref.shape
-            parts = 256 // (high * low * own)
-            g_side_ref[pl.ds(k * parts, parts)] = grad.reshape(
-                parts, high, low, own, columns
-            ).astype(jnp.bfloat16)
+            bits = seq_bits()
+            g_side_ref[place_bits(k, bits)] = grad.reshape(g_side_ref.shape[bits:]).astype(
+                jnp.bfloat16
+            )
         else:
             g_side_ref[block, :] = grad.astype(jnp.bfloat16)
 
-    each(model // 256, weight_block)
+    each(count, weight_block)
     if merged:
         reduction.allow(len(chunks))
     advance()
@@ -1838,7 +1940,7 @@
             chain_copy(p).wait_send()
 
 
-def mixer_back(common, saved, attention=None, grads=None):
+def mixer_back(common, saved, attention, grads=None, came=()):
     tokens = common[0]
     rows, model = tokens.shape
     gate_weight, query_weight, memory_weight, taps = common[4], common[8], common[9], common[10]
@@ -1887,12 +1989,14 @@
         pltpu.SemaphoreType.DMA((2, tiles)),
     ]
     if merged:
-        blocks = [seq_blocks(g) for g in grads]
-        widths = [g.shape[1] for g in grads] + [side]
+        blocks = list(grads)
+        widths = [g.shape[-1] for g in grads] + [side]
         chunks = column_chunks(widths)
-        operands += blocks
-        in_specs += [hbm] * len(blocks)
-        own = blocks[0].shape[3]
+        loaded = [pltpu.VMEM(x.shape, x.dtype) for x in operands]
+        scratch = loaded + [pltpu.SemaphoreType.DMA((len(loaded),))] + scratch
+        operands += blocks + list(came)
+        in_specs = [hbm] * len(operands)
+        own = blocks[0].shape[-2]
         small = (HALO, model)
         out_shape = (
             [shape((rows, model), full)]
@@ -1900,7 +2004,7 @@
             + [shape(small, full)]
         )
         scratch += [
-            pltpu.VMEM(blocks[0].shape[:4] + (side,), low),
+            pltpu.VMEM(blocks[0].shape[:-1] + (side,), low),
             pltpu.VMEM((count * rows, memory_width), full),
             pltpu.VMEM((count, rows, memory_width), low),
         ]
@@ -2010,7 +2114,7 @@
         out_shape=[jax.ShapeDtypeStruct(s, jnp.float32) for s in shapes],
         in_specs=[vmem] * 6,
         out_specs=[vmem] * len(shapes),
-        compiler_params=pltpu.CompilerParams(vmem_limit_bytes=32 << 20),
+        compiler_params=pltpu.CompilerParams(vmem_limit_bytes=60 << 20),
         name="finish_outputs",
     )(*sums, small)
 
@@ -2113,6 +2217,7 @@
         g_gate,
         g_feed_gain,
         g_mamba_gain,
+        *came,
     ) = feed_layer(
         y,
         gate_z,
@@ -2131,7 +2236,7 @@
     common += [rate, skip]
     saved = [pre, conv, raw, cum, y, states, d_second, d_y, d_gate_z]
     early = [g_down, g_feed, g_mixed, g_gate]
-    if lax.axis_size("seq") <= 4:
+    if lax.axis_size("seq") == 4:
         grad_tokens, *sums, small = mixer_back(
             common,
             saved,
@@ -2146,6 +2251,7 @@
                 g_mamba_gain,
             ],
             early,
+            came,
         )
     else:
         d_query, d_memory = attention_back(

time: 292 us -> 250 us (0.86)
  Pallas kernels: 271 us -> 233 us
  local copies, waits for them, and re-layouts: 15.9 us -> 10.6 us
    pallas_call x1, Pallas kernels: 204 us -> 144 us  [mixer_back(): pl.pallas_call(functools.partial(mixer_back_kernel, merged, chunks), out_...]
    pallas_call x1, Pallas kernels: 30.8 us -> 51.5 us  [feed_layer(): pl.pallas_call(functools.partial(feed_kernel, merged), out_shape=out_shap...]
    unnamed x34 -> x22, local copies, waits for them, and re-layouts: 10.1 us -> 4.87 us
where the time goes in v4:
time: 250 us
  Pallas kernels  233 us (93%)
  local copies, waits for them, and re-layouts  10.6 us (4%)
  other arithmetic  5.05 us (2%)
    pallas_call x1, Pallas kernels, mixer_back(): pl.pallas_call(functools.partial(mixer_back_kernel, merged, chunks), out_...  144 us
    pallas_call x1, Pallas kernels, feed_layer(): pl.pallas_call(functools.partial(feed_kernel, merged), out_shape=out_shap...  51.5 us
    pallas_call x1, Pallas kernels, mixer_forward(): pl.pallas_call(mixer_kernel, out_shape=[shape((rows, inner), full), shape...  26.1 us
    pallas_call x1, Pallas kernels, attention_forward(): pl.pallas_call(attention_kernel, out_shape=[jax.ShapeDtypeStruct((rows, w...  7.09 us

profile of v4, /device:TPU:0, one launch (start us, length us, event | category | flops | bytes accessed | tf_op | source)
XLA Modules:
  0.0 249.8 jit_solution(14566443798440384349)
XLA Ops:
  0.7 0.8 concatenate.9
  1.6 0.8 broadcast_in_dim.54.seg_ref.refs_2_
  2.4 1.0 multiply_cosine_fusion
  3.4 0.8 pad_maximum_fusion.table_ref.refs_3_
  4.3 0.9 copy.45
  5.2 0.8 pad.15.step_weight.refs_7_
  6.0 0.6 select_maximum_fusion.taps_ref.refs_10_
  6.6 0.5 pad_bitcast_fusion
  7.2 0.7 broadcast_in_dim_reshape.3.skip_ref.refs_12_
  7.9 26.1 %mixer_forward.1 = (f32[512,768]{1,0:T(8,128)}, f32[520,1024]{1,0:T(8,128)}, f32[512,1024]{1,0:T(8,128)}, f32[512,128]{1,0:T(8,128)}, f32[512,128]{1,0:T(8,128)}...) custom-call(bf16[512,1024]{1,0:T(8,128)(2,1)} %bitcast.23, ...), custom_call_target="tpu_custom_call" | custom-call | tf_op jit(solution)/shard_map/mixer_forward/pallas_call | solution.py:1138
  34.0 0.1 slice.6
  34.1 0.1 slice.7
  34.2 0.7 convert_reduce_fusion.low_ref
  34.9 0.5 and_select_fusion.high_ref
  35.5 1.3 broadcast_in_dim.61.key_seg_ref.refs_24_
  36.8 7.1 %attention_forward.1 = (f32[512,256]{1,0:T(8,128)}, bf16[512,256]{1,0:T(8,128)(2,1)}, f32[4,8,512]{2,1,0:T(8,128)}) custom-call(s32[1]{0:T(128)} %bitcast.5.first_ref, s32[4]{0:T(128)} %convert_reduce_fusion.low_ref, s32[4]{0:T(128)} %and_select_fusion.high_ref, bf16[512,256]{1,0:T(8,128)(2,1)} %get-tuple-element.74.query_ref.refs_22_, ...), custom_call_target="tpu_custom_call" | custom-call | tf_op jit(solution)/shard_map/attention_forward/pallas_call | solution.py:1339
  43.9 0.6 broadcast_in_dim.62.refs_6_
  44.4 51.5 %feed_layer.1 = (bf16[512,1024]{1,0:T(8,128)(2,1)}, f32[512,1024]{1,0:T(8,128)}, f32[512,768]{1,0:T(8,128)}, bf16[512,768]{1,0:T(8,128)(2,1)}, f32[512,256]{1,0:...) custom-call(f32[512,768]{1,0:T(8,128)} %get-tuple-element.72.refs_0_, ...), custom_call_target="tpu_custom_call" | custom-call | tf_op jit(solution)/shard_map/feed_layer/pallas_call | solution.py:707
  95.9 143.8 %mixer_back.1 = (f32[512,1024]{1,0:T(8,128)}, bf16[2,2,64,1024]{3,2,1,0:T(8,128)(2,1)}, bf16[2,2,64,2048]{3,2,1,0:T(8,128)(2,1)}, bf16[2,2,64,1024]{3,2,1,0:T(8,...) custom-call(bf16[512,1024]{1,0:T(8,128)(2,1)} %bitcast.25, ...), custom_call_target="tpu_custom_call" | custom-call | tf_op jit(solution)/shard_map/mixer_back/pallas_call | solution.py:2020
  239.7 4.9 %finish_outputs.1 = (f32[256,768]{1,0:T(8,128)}, f32[256,768]{1,0:T(8,128)}, f32[256,256]{1,0:T(8,128)}, f32[256,12]{1,0:T(8,128)}, f32[256,768]{1,0:T(8,128)}, ...) custom-call(bf16[256,1024]{1,0:T(8,128)(2,1)} %bitcast.33, ...), custom_call_target="tpu_custom_call" | custom-call | tf_op jit(solution)/shard_map/finish_outputs/pallas_call | solution.py:2112
  244.6 1.6 copy.46
  246.2 1.3 reduce
  247.5 1.0 copy.49
  248.5 1.3 copy.50
  (26 shorter events, 0.2 us)
Async XLA Ops:
  0.7 5.3 %copy-start.4 = (f32[4,256]{1,0:T(4,128)S(1)}, f32[4,256]{1,0:T(4,128)}, u32[]{:S(2)}) copy-start(f32[4,256]{1,0:T(4,128)} %param.30) | copy-start | bytes 12292
  0.7 5.3 %copy-start.3 = (f32[4,768]{1,0:T(4,128)S(1)}, f32[4,768]{1,0:T(4,128)}, u32[]{:S(2)}) copy-start(f32[4,768]{1,0:T(4,128)} %param.29) | copy-start | bytes 36868
  0.7 5.9 %copy-start.8 = (f32[12]{0:T(128)S(1)}, f32[12]{0:T(128)}, u32[]{:S(2)}) copy-start(f32[12]{0:T(128)} %param.31) | copy-start | bytes 148
  0.7 5.9 %copy-start.7 = (f32[12]{0:T(128)S(1)}, f32[12]{0:T(128)}, u32[]{:S(2)}) copy-start(f32[12]{0:T(128)} %param.32) | copy-start | bytes 148
  0.7 6.5 %copy-start.6 = (f32[12]{0:T(128)S(1)}, f32[12]{0:T(128)}, u32[]{:S(2)}) copy-start(f32[12]{0:T(128)} %param.33) | copy-start | bytes 148
  7.9 26.2 %copy-start.2 = (s32[1,2048]{1,0:T(1,128)S(1)}, s32[1,2048]{1,0:T(1,128)}, u32[]{:S(2)}) copy-start(s32[1,2048]{1,0:T(1,128)} %param.23) | copy-start | bytes 24580
  34.0 9.8 %copy-start.5 = (f32[768]{0:T(1024)S(1)}, f32[768]{0:T(1024)}, u32[]{:S(2)}) copy-start(f32[768]{0:T(1024)} %param.34) | copy-start | bytes 9220
  239.7 7.8 %copy-start.1 = (bf16[512,1024]{1,0:T(8,128)(2,1)S(1)}, bf16[512,1024]{1,0:T(8,128)(2,1)}, u32[]{:S(2)}) copy-start(bf16[512,1024]{1,0:T(8,128)(2,1)} %get-tuple-element.77) | copy-start | bytes 3145732
  239.7 8.8 %copy-start = (f32[512,1024]{1,0:T(8,128)S(1)}, f32[512,1024]{1,0:T(8,128)}, u32[]{:S(2)}) copy-start(f32[512,1024]{1,0:T(8,128)} %get-tuple-element.97) | copy-start | bytes 6291460

commit v5 on v4

--- a/solution.py
+++ b/solution.py
@@ -466,6 +466,9 @@
     ) = refs
     rows = y_ref.shape[0]
     tiles = rows // FEED_TILE
+    mamba_gain = jnp.concatenate(
+        [mamba_gain_ref[k : k + 1, :] for k in range(mamba_gain_ref.shape[0])], axis=1
+    )
     inner = y_ref.shape[1]
     width = feed_gain_ref.shape[1]
     feed = down_weight.shape[1]
@@ -519,7 +522,7 @@
         total = square_send[at, :] + square_recv[at, :]
         inverse = lax.rsqrt(total[:, :1] / all_inner + eps_norm)
         inverse_six[at, :] = jnp.broadcast_to(inverse, (FEED_TILE, LANES))
-        low = (g_six[at, :] * inverse * mamba_gain_ref[...]).astype(jnp.bfloat16)
+        low = (g_six[at, :] * inverse * mamba_gain).astype(jnp.bfloat16)
         gated[at, :] = low
         part = matmul_last(low, mamba_output_ref[...]) + matmul_last(
             attention_ref[at, :], attention_out_ref[...]
@@ -609,7 +612,7 @@
             d_gated_now * six * inverse_six[at, :][:, :1], axis=0, keepdims=True
         )
         cross_send[at, :] = jnp.broadcast_to(
-            jnp.sum(d_gated_now * mamba_gain_ref[...] * six, axis=1, keepdims=True), (FEED_TILE, LANES)
+            jnp.sum(d_gated_now * mamba_gain * six, axis=1, keepdims=True), (FEED_TILE, LANES)
         )
         swap(cross_send, cross_recv, sem_cross, i).start()
 
@@ -620,7 +623,7 @@
         swap(cross_send, cross_recv, sem_cross, i).wait()
         cross = (cross_send[at, :] + cross_recv[at, :])[:, :1] / all_inner
         inverse = inverse_six[at, :][:, :1]
-        d_six = inverse * (d_gated[at, :] * mamba_gain_ref[...]) - g_six[at, :] * (
+        d_six = inverse * (d_gated[at, :] * mamba_gain) - g_six[at, :] * (
             inverse * inverse * inverse * cross
         )
         gate_now = gate_z_ref[at, :]
@@ -744,7 +747,7 @@
         tokens,
         cotangent,
         mixer_gain[None],
-        mamba_gain[None],
+        mamba_gain.reshape(inner // LANES, LANES),
         feed_gain[None],
         mamba_output,
         attention_out,
@@ -836,18 +839,19 @@
 def mixer_kernel(
     tokens_ref,
     gain_ref,
-    seg_ref,
+    seg_row_ref,
     table_ref,
     gate_weight,
     input_weight,
     maps_weight,
-    step_weight,
+    step_given,
     query_weight,
     memory_weight,
-    taps_ref,
-    bias_ref,
-    rate_ref,
-    skip_ref,
+    conv_inner_ref,
+    conv_maps_ref,
+    step_bias_ref,
+    log_rate_ref,
+    skip_gain_ref,
     gate_z_ref,
     pre_ref,
     conv_ref,
@@ -857,6 +861,17 @@
     states_ref,
     query_ref,
     memory_ref,
+    attention_ref,
+    attention_low_ref,
+    logs_ref,
+    seg_ref,
+    key_seg_ref,
+    step_weight,
+    taps_ref,
+    rate_ref,
+    skip_ref,
+    step_wide,
+    bias_ref,
     normed,
     spread_ref,
     act,
@@ -881,15 +896,30 @@
     state_width = (width - inner) // 2
     following = (lax.rem(seq + 1, count), head, batch)
     greet_seq(pltpu.get_barrier_semaphore(), 0)
-
-    def memory_copy(step, place, owner):
+    first = seq * rows
+
+    def memory_copy(hop, owner):
         return exchange(
             memory_ref.at[owner],
             memory_ref.at[owner],
-            sem_memory.at[0, step],
-            sem_memory.at[1, step],
-            (place, head, batch),
-        )
+            sem_memory.at[0, hop],
+            sem_memory.at[1, hop],
+            following,
+        )
+
+    def memory_send(hop):
+        @pl.when((seq - hop + 1 >= 0) & (seq < count - 1))
+        def _():
+            memory_copy(hop, lax.rem(seq - hop + 1 + count, count)).start()
+
+    def memory_receive(hop):
+        @pl.when(seq - hop >= 0)
+        def _():
+            memory_copy(hop, lax.rem(seq - hop + count, count)).wait_recv()
+
+    def memory_hop(hop):
+        memory_receive(hop - 1)
+        memory_send(hop)
 
     halo_copy = exchange(
         pre_ref.at[pl.ds(rows, HALO)],
@@ -913,14 +943,7 @@
     wide_tiles = rows // FEED_TILE
     each(wide_tiles, memory_tile)
 
-    def memory_start(step, carry):
-        @pl.when(seq + step < count)
-        def _():
-            memory_copy(step, lax.rem(seq + step, count), seq).start()
-
-        return carry
-
-    lax.fori_loop(1, count, memory_start, 0)
+    memory_send(1)
 
     def pre_tile(i):
         at = feed_rows(i)
@@ -935,12 +958,51 @@
     def _():
         halo_copy.start()
 
+    if count > 2:
+        memory_hop(2)
+
+    def key_block(k):
+        at = pl.ds(pl.multiple_of(k * LANES, LANES), LANES)
+        row = seg_row_ref[:, at].astype(jnp.float32)
+        key_seg_ref[at, :] = jnp.broadcast_to(row, (LANES, LANES)).T
+
+    each(seg_row_ref.shape[1] // LANES, key_block)
+    seg_ref[HALO : HALO + rows, :] = key_seg_ref[pl.ds(pl.multiple_of(first, TILE), rows), :]
+    seg_ref[:HALO, :] = jnp.full((HALO, LANES), -1.0, jnp.float32)
+    seg_ref[HALO + rows :, :] = jnp.full((HALO, LANES), -2.0, jnp.float32)
+
+    @pl.when(seq > 0)
+    def _():
+        seg_ref[:HALO, :] = key_seg_ref[pl.ds(pl.multiple_of(first - HALO, HALO), HALO), :]
+
+    @pl.when(seq < count - 1)
+    def _():
+        seg_ref[HALO + rows :, :] = key_seg_ref[pl.ds(pl.multiple_of(first + rows, TILE), HALO), :]
+
+    heads = step_given.shape[0]
+    lane = lax.broadcasted_iota(jnp.int32, (1, LANES), 1)
+    wide_lane = lax.broadcasted_iota(jnp.int32, (1, inner), 1)
+    bias_row = log_row = jnp.zeros((1, LANES), jnp.float32)
+    skip_row = jnp.zeros((1, inner), jnp.float32)
+    for h in range(heads):
+        bias_row = jnp.where(lane == h, step_bias_ref[h], bias_row)
+        log_row = jnp.where(lane == h, log_rate_ref[h], log_row)
+        skip_row = jnp.where(wide_lane // HD == h, skip_gain_ref[h], skip_row)
+    bias_ref[...] = bias_row
+    rate_ref[...] = jnp.where(lane < heads, -jnp.exp(log_row), 0.0)
+    skip_ref[...] = skip_row
+    step_wide[...] = jnp.zeros_like(step_wide)
+    step_wide[:heads, :] = step_given[...].astype(jnp.float32)
+    step_weight[...] = step_wide[...].astype(jnp.bfloat16)
+    taps_ref[...] = jnp.zeros_like(taps_ref)
+    taps_ref[: conv_inner_ref.shape[0], :inner] = conv_inner_ref[...]
+    taps_ref[: conv_inner_ref.shape[0], inner:] = conv_maps_ref[...]
     spread_ref[...] = spread_matrix(inner, HD)
     lower = jnp.where(ordered(CHUNK), 1.0, 0.0)
 
     def step_tile(i):
         at = tile_rows(i)
-        raw = matmul(normed[at, :], step_weight[...]) + bias_ref[...]
+        raw = matmul_last(normed[at, :], step_weight[...]) + bias_ref[...]
         raw_ref[at, :] = raw
         cum_ref[at, :] = jnp.dot(lower, rate_ref[...] * soft_plus(raw), precision=highest)
 
@@ -1021,6 +1083,9 @@
             for p in range(pieces):
                 chain_copy(p).start()
 
+    if count > 3:
+        memory_hop(3)
+
     def inside_chunk(c):
         at = tile_rows(c)
         own, _, _ = chunk_flags(seg_ref, c)
@@ -1051,28 +1116,68 @@
             turned = part * table_ref[at, :LANES] + turn_half(part) * table_ref[at, LANES:]
             query_ref[at, k * LANES : (k + 1) * LANES] = turned.astype(jnp.bfloat16)
 
+    def chain_wait(p):
+        columns = pl.ds(p * PIECE, PIECE)
+        chain_copy(p).wait_recv()
+        came = chain_in[:, columns].astype(jnp.float32)
+        state[:, columns] = came
+        return came
+
     @pl.when(seq >= 2)
     def _():
         each(wide_tiles, project_tile)
 
-    @pl.when(seq > 0)
+    @pl.when((seq > 0) & (seq < count - 1))
     def _():
         for p in range(pieces):
             columns = pl.ds(p * PIECE, PIECE)
-            chain_copy(p).wait_recv()
-            came = chain_in[:, columns].astype(jnp.float32)
-            state[:, columns] = came
-
-            @pl.when(seq < count - 1)
-            def _():
-                chain_out[:, columns] = (
-                    came * total[:1, columns] + local[:, columns]
-                ).astype(jnp.bfloat16)
-                chain_copy(p).start()
+            chain_out[:, columns] = (
+                chain_wait(p) * total[:1, columns] + local[:, columns]
+            ).astype(jnp.bfloat16)
+            chain_copy(p).start()
 
     @pl.when(seq < 2)
     def _():
         each(wide_tiles, project_tile)
+
+    span(4, count, memory_hop)
+    if count > 1:
+        memory_receive(count - 1)
+
+    def memory_rest(hop):
+        @pl.when((seq - hop + 1 >= 0) & (seq < count - 1))
+        def _():
+            memory_copy(hop, lax.rem(seq - hop + 1 + count, count)).wait_send()
+
+        @pl.when(seq + hop < count)
+        def _():
+            memory_ref[lax.rem(seq + hop, count)] = jnp.zeros(memory_ref.shape[1:], jnp.bfloat16)
+
+    span(1, count, memory_rest)
+    def attention_block(i):
+        at = tile_rows(i)
+        turned, log = attend_block(
+            first,
+            0,
+            (first + i * TILE + TILE - 1) // KEY_TILE,
+            i,
+            query_ref[at, :],
+            lambda k: memory_ref[k],
+            seg_ref,
+            key_seg_ref,
+        )
+        for pair, tile in enumerate(unstacked_heads(turned, False)):
+            columns = slice(pair * LANES, (pair + 1) * LANES)
+            attention_ref[at, columns] = tile
+            attention_low_ref[at, columns] = tile.astype(jnp.bfloat16)
+        logs_ref[i] = jnp.broadcast_to(log, logs_ref.shape[1:])
+
+    each(tiles, attention_block)
+
+    @pl.when((seq > 0) & (seq == count - 1))
+    def _():
+        for p in range(pieces):
+            chain_wait(p)
 
     def across_chunk(c):
         at = tile_rows(c)
@@ -1087,20 +1192,6 @@
     each(tiles, across_chunk)
     states_ref[tiles] = state[...].astype(jnp.bfloat16)
 
-    def memory_wait(step, carry):
-        @pl.when(seq + step < count)
-        def _():
-            memory_copy(step, lax.rem(seq + step, count), seq).wait_send()
-            memory_ref[lax.rem(seq + step, count)] = jnp.zeros(memory_ref.shape[1:], jnp.bfloat16)
-
-        @pl.when(seq - step >= 0)
-        def _():
-            memory_copy(step, seq, lax.rem(seq - step + count, count)).wait_recv()
-
-        return carry
-
-    lax.fori_loop(1, count, memory_wait, 0)
-
     @pl.when(seq < count - 1)
     def _():
         halo_copy.wait_send()
@@ -1108,30 +1199,24 @@
             chain_copy(p).wait_send()
 
 
-def mixer_forward(
-    tokens,
-    mixer_gain,
-    segments,
-    table,
-    mamba_gate,
-    mamba_input,
-    mamba_maps,
-    step_weight,
-    query_weight,
-    memory_weight,
-    taps,
-    bias,
-    rate,
-    skip,
-):
+def mixer_forward(*operands):
+    tokens, seg_row, table = operands[0], operands[2], operands[3]
+    mamba_gate, step_given, query_weight, memory_weight = (
+        operands[4],
+        operands[7],
+        operands[8],
+        operands[9],
+    )
     rows, width = tokens.shape
+    total = seg_row.shape[1]
     count = lax.axis_size("seq")
     inner = mamba_gate.shape[1]
-    conv_width = taps.shape[1]
+    conv_width = inner + operands[6].shape[1]
     state_width = (conv_width - inner) // 2
     query = query_weight.shape[1]
     chunks = rows // CHUNK
     pieces = inner // PIECE
+    smem = pl.BlockSpec(memory_space=pltpu.SMEM)
     vmem = pl.BlockSpec(memory_space=pltpu.VMEM)
     low, full = jnp.bfloat16, jnp.float32
     shape = jax.ShapeDtypeStruct
@@ -1147,10 +1232,21 @@
             shape((chunks + 1, state_width, inner), low),
             shape((rows, query), low),
             shape((count, rows, memory_weight.shape[1]), low),
+            shape((rows, query), full),
+            shape((rows, query), low),
+            shape((chunks, HALO, query // HD * TILE), full),
+            shape((rows + 2 * HALO, LANES), full),
+            shape((total, LANES), full),
+            shape((LANES, width), low),
+            shape((HALO, conv_width), full),
+            shape((1, LANES), full),
+            shape((1, inner), full),
         ],
-        in_specs=[vmem] * 14,
-        out_specs=[vmem] * 9,
+        in_specs=[vmem] * 12 + [smem] * 3,
+        out_specs=[vmem] * 18,
         scratch_shapes=[
+            pltpu.VMEM((LANES, width), full),
+            pltpu.VMEM((1, LANES), full),
             pltpu.VMEM((rows, width), low),
             pltpu.VMEM((LANES, inner), low),
             pltpu.VMEM((rows, conv_width), full),
@@ -1170,22 +1266,7 @@
             collective_id=2, has_side_effects=True, vmem_limit_bytes=60 << 20
         ),
         name="mixer_forward",
-    )(
-        tokens,
-        mixer_gain,
-        segments,
-        table,
-        mamba_gate,
-        mamba_input,
-        mamba_maps,
-        step_weight,
-        query_weight,
-        memory_weight,
-        taps,
-        bias,
-        rate,
-        skip,
-    )
+    )(*operands)
 
 
 KEY_TILE = 512
@@ -1237,7 +1318,7 @@
 
     def one(step, carry):
         at, allowed = key_tile(segs, key_seg_ref, first, i, high - step)
-        keys = memory_of(at)
+        keys = memory_of(high - step)
         after = []
         for part, (most, total, acc) in zip(parts, carry):
             scores = jnp.where(allowed, matmul(keys, part), neg_large)
@@ -1279,7 +1360,7 @@
 
     def one(step, totals):
         at, allowed = key_tile(segs, key_seg_ref, first, i, high - step)
-        keys = memory_of(at)
+        keys = memory_of(high - step)
         slopes, lows, after = [], [], []
         for h, (part, total) in enumerate(zip(spans, totals)):
             weights = jnp.exp(matmul(keys, queries_turned[:, part]) - log[:, part])
@@ -1297,57 +1378,6 @@
         0, high - low + 1, one, (jnp.zeros((LANES, TILE), jnp.float32),) * heads
     )
     return jnp.concatenate(totals, axis=1) * HD ** (-0.5)
-
-
-def attention_kernel(
-    first_ref,
-    low_ref,
-    high_ref,
-    query_ref,
-    memory_ref,
-    seg_ref,
-    key_seg_ref,
-    out_ref,
-    low_out_ref,
-    log_ref,
-):
-    def block(i):
-        at_rows = tile_rows(i)
-        turned, log = attend_block(
-            first_ref[0],
-            low_ref[i],
-            high_ref[i],
-            i,
-            query_ref[at_rows, :],
-            lambda at: memory_ref[at, :],
-            seg_ref,
-            key_seg_ref,
-        )
-        for pair, tile in enumerate(unstacked_heads(turned, False)):
-            columns = slice(pair * LANES, (pair + 1) * LANES)
-            out_ref[at_rows, columns] = tile
-            low_out_ref[at_rows, columns] = tile.astype(jnp.bfloat16)
-        log_ref[i] = jnp.broadcast_to(log, log_ref.shape[1:])
-
-    each(query_ref.shape[0] // TILE, block)
-
-
-def attention_forward(spans, query, memory, segments, key_segments):
-    rows, width = query.shape
-    full = jnp.float32
-    vmem = pl.BlockSpec(memory_space=pltpu.VMEM)
-    return pl.pallas_call(
-        attention_kernel,
-        out_shape=[
-            jax.ShapeDtypeStruct((rows, width), full),
-            jax.ShapeDtypeStruct((rows, width), jnp.bfloat16),
-            jax.ShapeDtypeStruct((rows // TILE, HALO, width // HD * TILE), full),
-        ],
-        in_specs=[pl.BlockSpec(memory_space=pltpu.SMEM)] * 3 + [vmem] * 4,
-        out_specs=[vmem] * 3,
-        compiler_params=pltpu.CompilerParams(vmem_limit_bytes=56 << 20),
-        name="attention_forward",
-    )(*spans, query, memory, segments, key_segments)
 
 
 def attention_back_kernel(
@@ -1379,7 +1409,7 @@
             d_out_ref[at, :],
             out_ref[at, :],
             log_ref[i][:1],
-            lambda key_at: memory_ref[key_at, :],
+            lambda k: memory_ref[pl.ds(pl.multiple_of(k * KEY_TILE, KEY_TILE), KEY_TILE), :],
             seg_ref,
             key_seg_ref,
             grads,
@@ -1623,7 +1653,7 @@
                 d_attention_ref[at, :],
                 attention_ref[at, :],
                 logs_ref[i][:1],
-                lambda key_at: memory_ref[key_at, :],
+                lambda k: memory_ref[pl.ds(pl.multiple_of(k * KEY_TILE, KEY_TILE), KEY_TILE), :],
                 seg_ref,
                 key_seg_ref,
                 grads,
@@ -1898,7 +1928,7 @@
             matmul_last(d_gate_z_ref[at, :], gate_weight[...])
             + matmul_last(side[at, :inner], input_weight[...])
             + matmul_last(side[at, inner:step_at], maps_weight[...]) / lax.axis_size("head")
-            + matmul_last(side[at, step_at:query_at], step_weight[...])
+            + matmul(side[at, step_at:query_at], step_weight[...])
             + matmul_last(side[at, query_at:memory_at], query_weight[...])
             + matmul_last(side[at, memory_at:], memory_weight[...])
         )
@@ -2030,93 +2060,113 @@
     )(*operands)
 
 
-def finish_kernel(sizes, down, feed, mixed, gate, side, small, *outs):
+def finish_kernel(sizes, count, *refs):
     inner, maps, heads, query, own = sizes
     full = jnp.float32
+    refs = list(refs)
+
+    def take(number):
+        nonlocal refs
+        now, refs = refs[:number], refs[number:]
+        return now
+
+    sums, (small,), passed = take(5), take(1), take(2)
+    outs, small_outs, passed_outs = take(count), take(9), take(2)
+    loaded, held, wide = take(5), take(2), take(count)
+    sem_in, sem_out = refs
+    loads = [
+        pltpu.make_async_copy(a, b, sem_in.at[k])
+        for k, (a, b) in enumerate(zip([*sums, *passed], loaded + held))
+    ]
+    for copy in loads:
+        copy.start()
+    down, feed, mixed, gate, side = loaded
+    half = feed.shape[1] // 2
+    step_at = inner + maps
+    query_at = step_at + LANES
+    memory_at = query_at + query
+    parts = (
+        (0, lambda: down[...]),
+        (1, lambda: feed[:, :half]),
+        (1, lambda: feed[:, half:]),
+        (2, lambda: mixed[:, :inner]),
+        (2, lambda: mixed[:, inner:]),
+        (3, lambda: gate[...]),
+        (4, lambda: side[:, :inner]),
+        (4, lambda: side[:, inner:step_at]),
+        (4, lambda: side[:, query_at:memory_at]),
+        (4, lambda: side[:, memory_at:]),
+    )
+    stores = []
+    for k, (group, value) in enumerate(parts):
+        if k == 0 or parts[k - 1][0] != group:
+            loads[group].wait()
+        wide[k][...] = value().astype(full)
+        stores.append(pltpu.make_async_copy(wide[k], outs[k], sem_out.at[k]))
+        stores[-1].start()
+    o_step, o_conv_inner, o_conv_maps, o_mixer_gain, o_rate, o_bias, o_skip, o_mamba, o_feed = (
+        small_outs
+    )
+    o_step[...] = side[:, step_at:query_at].astype(full).T[:heads]
     seq = lax.axis_index("seq")
-    wide = small.shape[1]
-    columns = [0, inner, inner + maps, inner + maps + heads]
-    query_at = inner + maps + LANES
-    (
-        o_gate_z,
-        o_inner,
-        o_maps,
-        o_step,
-        o_output,
-        o_query,
-        o_memory,
-        o_attention,
-        o_gate,
-        o_lift,
-        o_down,
-        o_conv_inner,
-        o_conv_maps,
-        o_mixer_gain,
-        o_rate,
-        o_bias,
-        o_skip,
-        o_mamba_gain,
-        o_feed_gain,
-    ) = outs
-    o_gate_z[...] = gate[...].astype(full)
-    o_inner[...] = side[:, : columns[1]].astype(full)
-    o_maps[...] = side[:, columns[1] : columns[2]].astype(full)
-    o_step[...] = side[:, columns[2] : columns[2] + LANES].astype(full)[:, :heads]
-    o_query[...] = side[:, query_at : query_at + query].astype(full)
-    o_memory[...] = side[:, query_at + query :].astype(full)
-    o_output[...] = mixed[:, :inner].astype(full)
-    o_attention[...] = mixed[:, inner:].astype(full)
-    o_gate[...] = feed[:, : o_gate.shape[1]].astype(full)
-    o_lift[...] = feed[:, o_gate.shape[1] :].astype(full)
-    o_down[...] = down[...].astype(full)
     value = small[...]
+    width = value.shape[1]
     o_conv_inner[...] = value[:4, :inner]
     o_conv_maps[...] = value[:4, inner:]
-    turned = pltpu.roll(value, lax.rem(wide - seq * own, wide), 1)
+    turned = pltpu.roll(value, lax.rem(width - seq * own, width), 1)
     o_mixer_gain[...] = turned[5:6, :own]
-    o_feed_gain[...] = turned[6:7, :own]
+    o_feed[...] = turned[6:7, :own]
     for k, out in enumerate((o_rate, o_bias, o_skip)):
         out[...] = value[7:8, k * LANES : (k + 1) * LANES][:, :heads]
-    o_mamba_gain[...] = value[4:5, :inner]
-
-
-def finish_outputs(sums, small, sizes):
+    for k in range(inner // LANES):
+        o_mamba[k : k + 1, :] = value[4:5, k * LANES : (k + 1) * LANES]
+    for k, (a, b) in enumerate(zip(held, passed_outs)):
+        loads[5 + k].wait()
+        stores.append(pltpu.make_async_copy(a, b, sem_out.at[count + k]))
+        stores[-1].start()
+    for copy in stores:
+        copy.wait()
+
+
+def finish_outputs(sums, small, passed, sizes):
     inner, maps, heads, query, own = sizes
-    rows = own
-    sums = [s.reshape(rows, s.shape[-1]) for s in sums]
-    down, feed, mixed, gate, side = sums
-    half = feed.shape[1] // 2
-    memory = side.shape[1] - inner - maps - LANES - query
-    shapes = [
-        (rows, inner),
-        (rows, inner),
-        (rows, maps),
-        (rows, heads),
-        (rows, inner),
-        (rows, query),
-        (rows, memory),
-        (rows, mixed.shape[1] - inner),
-        (rows, half),
-        (rows, half),
-        (rows, half),
-        (4, inner),
-        (4, maps),
-        (1, own),
-        (1, heads),
-        (1, heads),
-        (1, heads),
-        (1, inner),
-        (1, own),
+    sums = [s.reshape(own, s.shape[-1]) for s in sums]
+    half = sums[1].shape[1] // 2
+    attention = sums[2].shape[1] - inner
+    memory = sums[4].shape[1] - inner - maps - LANES - query
+    full = jnp.float32
+    widths = (sums[0].shape[1], half, half, inner, attention, inner, inner, maps, query, memory)
+    big = [jax.ShapeDtypeStruct((own, w), full) for w in widths]
+    little = [
+        jax.ShapeDtypeStruct(s, full)
+        for s in (
+            (heads, own),
+            (4, inner),
+            (4, maps),
+            (1, own),
+            (1, heads),
+            (1, heads),
+            (1, heads),
+            (inner // LANES, LANES),
+            (1, own),
+        )
     ]
     vmem = pl.BlockSpec(memory_space=pltpu.VMEM)
+    hbm = pl.BlockSpec(memory_space=pl.ANY)
     return pl.pallas_call(
-        functools.partial(finish_kernel, sizes),
-        out_shape=[jax.ShapeDtypeStruct(s, jnp.float32) for s in shapes],
-        in_specs=[vmem] * 6,
-        out_specs=[vmem] * len(shapes),
+        functools.partial(finish_kernel, sizes, len(big)),
+        out_shape=big + little + [jax.ShapeDtypeStruct(p.shape, p.dtype) for p in passed],
+        in_specs=[hbm] * 5 + [vmem] + [hbm] * 2,
+        out_specs=[hbm] * len(big) + [vmem] * len(little) + [hbm] * 2,
+        scratch_shapes=[pltpu.VMEM(s.shape, s.dtype) for s in [*sums, *passed]]
+        + [pltpu.VMEM(s.shape, full) for s in big]
+        + [
+            pltpu.SemaphoreType.DMA((7,)),
+            pltpu.SemaphoreType.DMA((len(big) + 2,)),
+        ],
         compiler_params=pltpu.CompilerParams(vmem_limit_bytes=60 << 20),
         name="finish_outputs",
-    )(*sums, small)
+    )(*sums, small, *passed)
 
 
 def rotation_table(position):
@@ -2156,55 +2206,45 @@
     rows, wide = tokens.shape
     tap_count, inner = conv_inner.shape
     head_count = log_rate.shape[0]
-    segments = seg_ids[0]
     offset = lax.axis_index("seq") * rows
-    padded = jnp.concatenate(
-        [jnp.full((HALO,), -1, jnp.int32), segments, jnp.full((HALO,), -2, jnp.int32)]
-    )
-    window = lax.dynamic_slice_in_dim(padded, offset, rows + 2 * HALO)
-    window_wide = jnp.broadcast_to(
-        window.astype(jnp.float32)[:, None], (rows + 2 * HALO, LANES)
-    )
-    key_segments = jnp.broadcast_to(
-        segments.astype(jnp.float32)[:, None], (segments.shape[0], LANES)
-    )
     table = rotation_table(offset + jnp.arange(rows, dtype=jnp.int32))
-    starts = offset + jnp.arange(rows // TILE, dtype=jnp.int32) * TILE
-    reach = segments[KEY_TILE - 1 :: KEY_TILE]
-    low = jnp.sum(
-        (reach[None, :] < window[HALO : HALO + rows : TILE][:, None]).astype(jnp.int32), axis=1
-    )
-    spans = (offset[None], low, (starts + TILE - 1) // KEY_TILE)
-
-    def lanes_of(values):
-        return jnp.pad(values, (0, LANES - head_count))[None]
-
-    step_weight = jnp.pad(mamba_step, ((0, 0), (0, LANES - head_count)))
-    taps = jnp.pad(
-        jnp.concatenate([conv_inner, conv_maps], axis=1), ((0, HALO - tap_count), (0, 0))
-    )
-    bias, rate = lanes_of(step_bias), lanes_of(-jnp.exp(log_rate))
-    skip = jnp.repeat(skip_gain, inner // head_count)[None]
-    common = [
+    (
+        gate_z,
+        pre,
+        conv,
+        raw,
+        cum,
+        y,
+        states,
+        query,
+        memory,
+        attention,
+        attention_low,
+        logs,
+        window,
+        key_segments,
+        step_weight,
+        taps,
+        rate,
+        skip,
+    ) = mixer_forward(
         tokens,
         mixer_gain[None],
-        window_wide,
+        seg_ids,
         table,
         mamba_gate,
         mamba_input,
         mamba_maps,
-        step_weight,
+        mamba_step.T,
         query_weight,
         memory_weight,
-        taps,
-    ]
-    gate_z, pre, conv, raw, cum, y, states, query, memory = mixer_forward(
-        *common, bias, rate, skip
+        conv_inner,
+        conv_maps,
+        step_bias,
+        log_rate,
+        skip_gain,
     )
     all_memory = memory.reshape(memory.shape[0] * rows, memory.shape[2])
-    attention, attention_low, logs = attention_forward(
-        spans, query, all_memory, window_wide, key_segments
-    )
     (
         layer_out,
         d_second,
@@ -2233,7 +2273,21 @@
         lift_weight,
         down_weight,
     )
-    common += [rate, skip]
+    common = [
+        tokens,
+        mixer_gain[None],
+        window,
+        table,
+        mamba_gate,
+        mamba_input,
+        mamba_maps,
+        step_weight,
+        query_weight,
+        memory_weight,
+        taps,
+        rate,
+        skip,
+    ]
     saved = [pre, conv, raw, cum, y, states, d_second, d_y, d_gate_z]
     early = [g_down, g_feed, g_mixed, g_gate]
     if lax.axis_size("seq") == 4:
@@ -2254,8 +2308,13 @@
             came,
         )
     else:
+        starts = offset + jnp.arange(rows // TILE, dtype=jnp.int32) * TILE
+        reach = seg_ids[0, KEY_TILE - 1 :: KEY_TILE]
+        own = lax.dynamic_slice_in_dim(seg_ids[0], offset, rows)[::TILE]
+        low = jnp.sum((reach[None, :] < own[:, None]).astype(jnp.int32), axis=1)
+        spans = (offset[None], low, (starts + TILE - 1) // KEY_TILE)
         d_query, d_memory = attention_back(
-            spans, query, all_memory, window_wide, key_segments, attention, logs, d_attention, table
+            spans, query, all_memory, window, key_segments, attention, logs, d_attention, table
         )
         grad_tokens, g_side, g_taps, g_mixer_gain, g_heads = mixer_back(
             common, saved, [d_query, d_memory.reshape(memory.shape)]
@@ -2281,17 +2340,17 @@
         wide // lax.axis_size("seq"),
     )
     (
+        o_down,
+        o_gate,
+        o_lift,
+        o_output,
+        o_attention,
         o_gate_z,
         o_inner,
         o_maps,
-        o_step,
-        o_output,
         o_query,
         o_memory,
-        o_attention,
-        o_gate,
-        o_lift,
-        o_down,
+        o_step,
         o_conv_inner,
         o_conv_maps,
         o_mixer_gain,
@@ -2300,7 +2359,9 @@
         o_skip,
         o_mamba_gain,
         o_feed_gain,
-    ) = finish_outputs(sums, small, sizes)
+        layer_out,
+        grad_tokens,
+    ) = finish_outputs(sums, small, (layer_out, grad_tokens), sizes)
     return (
         layer_out[None],
         grad_tokens[None],
@@ -2308,13 +2369,13 @@
         o_gate_z,
         o_inner,
         o_maps,
-        o_step,
+        o_step.T,
         o_conv_inner,
         o_conv_maps,
         o_rate[0],
         o_bias[0],
         o_skip[0],
-        o_mamba_gain[0],
+        o_mamba_gain.reshape(inner),
         o_output,
         o_query,
         o_memory,

time: 250 us -> 232 us (0.928)
  local copies, waits for them, and re-layouts: 10.6 us -> 0 us
  Pallas kernels: 233 us -> 229 us
  other arithmetic: 5.05 us -> 1.83 us
    pallas_call x1, Pallas kernels: 26.1 us -> 33 us  [mixer_forward(): pl.pallas_call(mixer_kernel, out_shape=[shape((rows, inner), full), shape...]
    unnamed x22 -> x0, local copies, waits for them, and re-layouts: 4.87 us -> none
    pallas_call x1, Pallas kernels: 51.5 us -> 47 us  [feed_layer(): pl.pallas_call(functools.partial(feed_kernel, merged), out_shape=out_shap...]
    pallas_call x2 -> x1, Pallas kernels: 12 us -> 7.72 us  [finish_outputs(): pl.pallas_call(functools.partial(finish_kernel, sizes, len(big)), out_sha...]
    broadcast_in_dim x5 -> x0, local copies, waits for them, and re-layouts: 3.32 us -> none  [the longest x1 1.31 us: body(): jnp.broadcast_to(segments.astype(jnp.float32)[:, None], (segments.shape[0...]
    pallas_call x1, Pallas kernels: 144 us -> 141 us  [mixer_back(): pl.pallas_call(functools.partial(mixer_back_kernel, merged, chunks), out_...]
where the time goes in v5:
time: 232 us
  Pallas kernels  229 us (99%)
    pallas_call x1, Pallas kernels, mixer_back(): pl.pallas_call(functools.partial(mixer_back_kernel, merged, chunks), out_...  141 us
    pallas_call x1, Pallas kernels, feed_layer(): pl.pallas_call(functools.partial(feed_kernel, merged), out_shape=out_shap...  47 us
    pallas_call x1, Pallas kernels, mixer_forward(): pl.pallas_call(mixer_kernel, out_shape=[shape((rows, inner), full), shape...  33 us
    pallas_call x1, Pallas kernels, finish_outputs(): pl.pallas_call(functools.partial(finish_kernel, sizes, len(big)), out_sha...  7.72 us

profile of v5, /device:TPU:0, one launch (start us, length us, event | category | flops | bytes accessed | tf_op | source)
XLA Modules:
  0.0 231.7 jit_solution(6807233283452052857)
XLA Ops:
  0.7 1.0 multiply_cosine_fusion
  1.7 0.8 pad_maximum_fusion.table_ref.refs_3_
  2.5 33.0 %mixer_forward.1 = (f32[512,768]{1,0:T(8,128)}, f32[520,1024]{1,0:T(8,128)}, f32[512,1024]{1,0:T(8,128)}, f32[512,128]{1,0:T(8,128)}, f32[512,128]{1,0:T(8,128)}...) custom-call(bf16[512,1024]{1,0:T(8,128)(2,1)} %bitcast.21, ...), custom_call_target="tpu_custom_call" | custom-call | tf_op jit(solution)/shard_map/mixer_forward/pallas_call | solution.py:1223
  35.5 47.0 %feed_layer.1 = (bf16[512,1024]{1,0:T(8,128)(2,1)}, f32[512,1024]{1,0:T(8,128)}, f32[512,768]{1,0:T(8,128)}, bf16[512,768]{1,0:T(8,128)(2,1)}, f32[512,256]{1,0:...) custom-call(f32[512,768]{1,0:T(8,128)} %get-tuple-element.89.refs_0_, ...), custom_call_target="tpu_custom_call" | custom-call | tf_op jit(solution)/shard_map/feed_layer/pallas_call | solution.py:710
  82.5 141.2 %mixer_back.1 = (f32[512,1024]{1,0:T(8,128)}, bf16[2,2,64,1024]{3,2,1,0:T(8,128)(2,1)}, bf16[2,2,64,2048]{3,2,1,0:T(8,128)(2,1)}, bf16[2,2,64,1024]{3,2,1,0:T(8,...) custom-call(bf16[512,1024]{1,0:T(8,128)(2,1)} %bitcast.23, ...), custom_call_target="tpu_custom_call" | custom-call | tf_op jit(solution)/shard_map/mixer_back/pallas_call | solution.py:2050
  223.7 7.7 %finish_outputs.1 = (f32[256,1024]{1,0:T(8,128)}, f32[256,1024]{1,0:T(8,128)}, f32[256,1024]{1,0:T(8,128)}, f32[256,768]{1,0:T(8,128)}, f32[256,256]{1,0:T(8,128...) custom-call(bf16[256,1024]{1,0:T(8,128)(2,1)} %bitcast.28, ...), custom_call_target="tpu_custom_call" | custom-call | tf_op jit(solution)/shard_map/finish_outputs/pallas_call | solution.py:2156
  (2 shorter events, 0.0 us)

commit v6 on v5

--- a/solution.py
+++ b/solution.py
@@ -33,6 +33,39 @@
         device_id=device,
         device_id_type=MESH,
     )
+
+
+def moving(kernel, inputs, loaded, outputs, *refs):
+    given, refs = refs[:inputs], refs[inputs:]
+    targets, refs = refs[:outputs], refs[outputs:]
+    taken, refs = refs[:loaded], refs[loaded:]
+    held, refs = refs[:outputs], refs[outputs:]
+    sem_in, sem_out, refs = refs[0], refs[1], refs[2:]
+    loads = [
+        pltpu.make_async_copy(source, target, sem_in.at[k])
+        for k, (source, target) in enumerate(zip(given[:loaded], taken))
+    ]
+    for load in loads:
+        load.start()
+    stores = [
+        pltpu.make_async_copy(source, target, sem_out.at[k])
+        for k, (source, target) in enumerate(zip(held, targets))
+    ]
+    kernel(loads, stores, *taken, *given[loaded:], *held, *refs)
+    for store in stores:
+        store.wait()
+
+
+def moving_scratch(operands, results):
+    return [pltpu.VMEM(x.shape, x.dtype) for x in [*operands, *results]] + [
+        pltpu.SemaphoreType.DMA((len(operands),)),
+        pltpu.SemaphoreType.DMA((len(results),)),
+    ]
+
+
+def start_all(stores, *which):
+    for k in which:
+        stores[k].start()
 
 
 def each(count, action):
@@ -401,7 +434,7 @@
     return pl.ds(pl.multiple_of(i * FEED_TILE, FEED_TILE), FEED_TILE)
 
 
-def feed_kernel(merged, *refs):
+def feed_kernel(merged, loads, stores, *refs):
     (
         y_ref,
         gate_z_ref,
@@ -466,15 +499,12 @@
     ) = refs
     rows = y_ref.shape[0]
     tiles = rows // FEED_TILE
-    mamba_gain = jnp.concatenate(
-        [mamba_gain_ref[k : k + 1, :] for k in range(mamba_gain_ref.shape[0])], axis=1
-    )
     inner = y_ref.shape[1]
     width = feed_gain_ref.shape[1]
     feed = down_weight.shape[1]
     all_inner = inner * lax.axis_size("head")
     peer = peer_device()
-    loads = [
+    weight_loads = [
         pltpu.make_async_copy(source, target, weight_sem.at[k])
         for k, (source, target) in enumerate(
             (
@@ -484,7 +514,7 @@
             )
         )
     ]
-    for load in loads:
+    for load in weight_loads:
         load.start()
     devices = [peer]
     if merged:
@@ -496,6 +526,11 @@
         )
         devices += [first.peer(bit) for bit in range(first.bits - 3, first.bits)]
     greet(pltpu.get_barrier_semaphore(), devices)
+    for load in loads:
+        load.wait()
+    mamba_gain = jnp.concatenate(
+        [mamba_gain_ref[k : k + 1, :] for k in range(mamba_gain_ref.shape[0])], axis=1
+    )
 
     def swap(send, recv, sems, i):
         rows_now = feed_rows(i)
@@ -531,7 +566,7 @@
         swap(mixed_send, mixed_recv, sem_mixed, i).start()
 
     each(tiles, mixed_tile)
-    for load in loads:
+    for load in weight_loads:
         load.wait()
 
     def feed_tile(i):
@@ -584,6 +619,7 @@
     if merged:
         for k in range(EARLIER):
             first.halve_copy(k, 0).start()
+    start_all(stores, 5, 7)
     g_feed_gain_ref[...] = jnp.zeros_like(g_feed_gain_ref)
     g_mamba_gain_ref[...] = jnp.zeros_like(g_mamba_gain_ref)
 
@@ -634,6 +670,7 @@
         ).astype(jnp.bfloat16)
 
     each(tiles, gate_back)
+    start_all(stores, 1, 2, 3, 4)
 
     def out_tile(i):
         at = feed_rows(i)
@@ -642,6 +679,7 @@
         out_ref[at, :] = (second[at, :] + total).astype(jnp.bfloat16)
 
     each(tiles, out_tile)
+    start_all(stores, 0)
 
     def mixed_weights(k):
         block = block_columns(k)
@@ -654,9 +692,11 @@
         store(g_mixed_ref, k, grad)
 
     each(blocks, mixed_weights)
+    start_all(stores, 6, 8, 9, 10)
     if merged:
         for k in range(EARLIER):
             first.halve_copy(k, 0).wait()
+        start_all(stores, 11, 12)
 
 
 def feed_layer(
@@ -707,12 +747,28 @@
     if merged:
         out_shape += [shape((2,) * 3 + (width // 16, n), low) for n in (feed, MOST)]
         scratch = [pltpu.SemaphoreType.DMA((2, EARLIER, 1))]
+    operands = [
+        y,
+        gate_z,
+        attention_low,
+        tokens,
+        cotangent,
+        mixer_gain[None],
+        mamba_gain.reshape(inner // LANES, LANES),
+        feed_gain[None],
+        mamba_output,
+        attention_out,
+        gate_weight,
+        lift_weight,
+        down_weight,
+    ]
     return pl.pallas_call(
-        functools.partial(feed_kernel, merged),
+        functools.partial(moving, functools.partial(feed_kernel, merged), 13, 10, len(out_shape)),
         out_shape=out_shape,
-        in_specs=[vmem] * 10 + [hbm] * 3,
-        out_specs=[vmem] * len(out_shape),
-        scratch_shapes=[
+        in_specs=[hbm] * 13,
+        out_specs=[hbm] * len(out_shape),
+        scratch_shapes=moving_scratch(operands[:10], out_shape)
+        + [
             pltpu.VMEM((width, feed), low),
             pltpu.VMEM((width, feed), low),
             pltpu.VMEM((width, feed), low),
@@ -740,21 +796,7 @@
             collective_id=1, has_side_effects=True, vmem_limit_bytes=60 << 20
         ),
         name="feed_layer",
-    )(
-        y,
-        gate_z,
-        attention_low,
-        tokens,
-        cotangent,
-        mixer_gain[None],
-        mamba_gain.reshape(inner // LANES, LANES),
-        feed_gain[None],
-        mamba_output,
-        attention_out,
-        gate_weight,
-        lift_weight,
-        down_weight,
-    )
+    )(*operands)
 
 
 CHUNK = 128
@@ -837,6 +879,8 @@
 
 
 def mixer_kernel(
+    loads,
+    stores,
     tokens_ref,
     gain_ref,
     seg_row_ref,
@@ -883,6 +927,7 @@
     state,
     chain_out,
     chain_in,
+    memory_turned,
     sem_memory,
     sem_halo,
     sem_chain,
@@ -896,6 +941,8 @@
     state_width = (width - inner) // 2
     following = (lax.rem(seq + 1, count), head, batch)
     greet_seq(pltpu.get_barrier_semaphore(), 0)
+    for load in loads:
+        load.wait()
     first = seq * rows
 
     def memory_copy(hop, owner):
@@ -1036,6 +1083,7 @@
             act[at, columns] = summed * sigmoid(summed)
 
     each(tiles, conv_tile)
+    start_all(stores, 1, 2, 3, 4, 12, 13, 14, 15, 16, 17)
     local[...] = jnp.zeros_like(local)
     total[...] = jnp.ones_like(total)
 
@@ -1154,6 +1202,11 @@
             memory_ref[lax.rem(seq + hop, count)] = jnp.zeros(memory_ref.shape[1:], jnp.bfloat16)
 
     span(1, count, memory_rest)
+    def turn_block(k):
+        memory_turned[k] = memory_ref[k].astype(jnp.float32).T.astype(jnp.bfloat16)
+
+    each(seq + 1, turn_block)
+
     def attention_block(i):
         at = tile_rows(i)
         turned, log = attend_block(
@@ -1162,7 +1215,7 @@
             (first + i * TILE + TILE - 1) // KEY_TILE,
             i,
             query_ref[at, :],
-            lambda k: memory_ref[k],
+            lambda k: (memory_ref[k], memory_turned[k]),
             seg_ref,
             key_seg_ref,
         )
@@ -1172,7 +1225,9 @@
             attention_low_ref[at, columns] = tile.astype(jnp.bfloat16)
         logs_ref[i] = jnp.broadcast_to(log, logs_ref.shape[1:])
 
+    start_all(stores, 0, 7, 8)
     each(tiles, attention_block)
+    start_all(stores, 9, 10, 11)
 
     @pl.when((seq > 0) & (seq == count - 1))
     def _():
@@ -1191,6 +1246,7 @@
 
     each(tiles, across_chunk)
     states_ref[tiles] = state[...].astype(jnp.bfloat16)
+    start_all(stores, 5, 6)
 
     @pl.when(seq < count - 1)
     def _():
@@ -1220,9 +1276,8 @@
     vmem = pl.BlockSpec(memory_space=pltpu.VMEM)
     low, full = jnp.bfloat16, jnp.float32
     shape = jax.ShapeDtypeStruct
-    return pl.pallas_call(
-        mixer_kernel,
-        out_shape=[
+    hbm = pl.BlockSpec(memory_space=pl.ANY)
+    out_shape = [
             shape((rows, inner), full),
             shape((rows + HALO, conv_width), full),
             shape((rows, conv_width), full),
@@ -1241,10 +1296,14 @@
             shape((HALO, conv_width), full),
             shape((1, LANES), full),
             shape((1, inner), full),
-        ],
-        in_specs=[vmem] * 12 + [smem] * 3,
-        out_specs=[vmem] * 18,
-        scratch_shapes=[
+        ]
+    return pl.pallas_call(
+        functools.partial(moving, mixer_kernel, 15, 12, len(out_shape)),
+        out_shape=out_shape,
+        in_specs=[hbm] * 12 + [smem] * 3,
+        out_specs=[hbm] * len(out_shape),
+        scratch_shapes=moving_scratch(operands[:12], out_shape)
+        + [
             pltpu.VMEM((LANES, width), full),
             pltpu.VMEM((1, LANES), full),
             pltpu.VMEM((rows, width), low),
@@ -1258,6 +1317,7 @@
             pltpu.VMEM((state_width, inner), full),
             pltpu.VMEM((state_width, inner), low),
             pltpu.VMEM((state_width, inner), low),
+            pltpu.VMEM((count, memory_weight.shape[1], rows), low),
             pltpu.SemaphoreType.DMA((2, count)),
             pltpu.SemaphoreType.DMA((2,)),
             pltpu.SemaphoreType.DMA((2, pieces)),
@@ -1318,7 +1378,7 @@
 
     def one(step, carry):
         at, allowed = key_tile(segs, key_seg_ref, first, i, high - step)
-        keys = memory_of(high - step)
+        keys, keys_turned = memory_of(high - step)
         after = []
         for part, (most, total, acc) in zip(parts, carry):
             scores = jnp.where(allowed, matmul(keys, part), neg_large)
@@ -1326,7 +1386,7 @@
             weights = jnp.exp(scores - new)
             factor = jnp.exp(most - new)
             total = total * factor + jnp.sum(weights, axis=0, keepdims=True)
-            acc = acc * factor + matmul_first(keys, weights.astype(jnp.bfloat16))
+            acc = acc * factor + matmul(keys_turned, weights.astype(jnp.bfloat16))
             after.append((new, total, acc))
         return tuple(after)
 

time: 232 us -> 224 us (0.966)
  Pallas kernels: 229 us -> 221 us
    pallas_call x2, Pallas kernels: 80 us -> 71.2 us  [the longest x1 42.7 us: feed_layer(): pl.pallas_call(functools.partial(moving, functools.partial(feed_kernel, m...]
where the time goes in v6:
time: 224 us
  Pallas kernels  221 us (99%)
    pallas_call x1, Pallas kernels, mixer_back(): pl.pallas_call(functools.partial(mixer_back_kernel, merged, chunks), out_...  142 us
    pallas_call x1, Pallas kernels, feed_layer(): pl.pallas_call(functools.partial(moving, functools.partial(feed_kernel, m...  42.7 us
    pallas_call x1, Pallas kernels, mixer_forward(): pl.pallas_call(functools.partial(moving, mixer_kernel, 15, 12, len(out_sh...  28.5 us
    pallas_call x1, Pallas kernels, finish_outputs(): pl.pallas_call(functools.partial(finish_kernel, sizes, len(big)), out_sha...  7.72 us

profile of v6, /device:TPU:0, one launch (start us, length us, event | category | flops | bytes accessed | tf_op | source)
XLA Modules:
  0.0 223.9 jit_solution(2340581982623753562)
XLA Ops:
  0.7 1.0 multiply_cosine_fusion
  1.7 0.8 pad_maximum_fusion.refs_3_
  2.5 28.5 %mixer_forward.1 = (f32[512,768]{1,0:T(8,128)}, f32[520,1024]{1,0:T(8,128)}, f32[512,1024]{1,0:T(8,128)}, f32[512,128]{1,0:T(8,128)}, f32[512,128]{1,0:T(8,128)}...) custom-call(bf16[512,1024]{1,0:T(8,128)(2,1)} %bitcast.21, ...), custom_call_target="tpu_custom_call" | custom-call | tf_op jit(solution)/shard_map/mixer_forward/pallas_call | solution.py:1300
  31.0 42.7 %feed_layer.1 = (bf16[512,1024]{1,0:T(8,128)(2,1)}, f32[512,1024]{1,0:T(8,128)}, f32[512,768]{1,0:T(8,128)}, bf16[512,768]{1,0:T(8,128)(2,1)}, f32[512,256]{1,0:...) custom-call(f32[512,768]{1,0:T(8,128)} %get-tuple-element.89.refs_0_, ...), custom_call_target="tpu_custom_call" | custom-call | tf_op jit(solution)/shard_map/feed_layer/pallas_call | solution.py:765
  73.7 142.3 %mixer_back.1 = (f32[512,1024]{1,0:T(8,128)}, bf16[2,2,64,1024]{3,2,1,0:T(8,128)(2,1)}, bf16[2,2,64,2048]{3,2,1,0:T(8,128)(2,1)}, bf16[2,2,64,1024]{3,2,1,0:T(8,...) custom-call(bf16[512,1024]{1,0:T(8,128)(2,1)} %bitcast.23, ...), custom_call_target="tpu_custom_call" | custom-call | tf_op jit(solution)/shard_map/mixer_back/pallas_call | solution.py:2110
  216.0 7.7 %finish_outputs.1 = (f32[256,1024]{1,0:T(8,128)}, f32[256,1024]{1,0:T(8,128)}, f32[256,1024]{1,0:T(8,128)}, f32[256,768]{1,0:T(8,128)}, f32[256,256]{1,0:T(8,128...) custom-call(bf16[256,1024]{1,0:T(8,128)(2,1)} %bitcast.28, ...), custom_call_target="tpu_custom_call" | custom-call | tf_op jit(solution)/shard_map/finish_outputs/pallas_call | solution.py:2216
  (2 shorter events, 0.0 us)

commit v7 on v6

--- a/solution.py
+++ b/solution.py
@@ -16,8 +16,8 @@
 
 LANES = 128
 MOST = 512
-TAIL = (512, 384, 256, 128, 128, 128)
-AHEAD = 7
+TAIL = (512, 512, 384, 128)
+AHEAD = 8
 EARLIER = 3
 LAG = 3
 PATTERN = (0, 1, 2, 0, 1, 3, 0, 1, 0, 1, 2, 0, 1, 3, 0, 1)
@@ -2138,7 +2138,7 @@
         pltpu.make_async_copy(a, b, sem_in.at[k])
         for k, (a, b) in enumerate(zip([*sums, *passed], loaded + held))
     ]
-    for copy in loads:
+    for copy in loads[5:] + loads[:5]:
         copy.start()
     down, feed, mixed, gate, side = loaded
     half = feed.shape[1] // 2
@@ -2158,6 +2158,10 @@
         (4, lambda: side[:, memory_at:]),
     )
     stores = []
+    for k, (a, b) in enumerate(zip(held, passed_outs)):
+        loads[5 + k].wait()
+        stores.append(pltpu.make_async_copy(a, b, sem_out.at[count + k]))
+        stores[-1].start()
     for k, (group, value) in enumerate(parts):
         if k == 0 or parts[k - 1][0] != group:
             loads[group].wait()
@@ -2180,10 +2184,6 @@
         out[...] = value[7:8, k * LANES : (k + 1) * LANES][:, :heads]
     for k in range(inner // LANES):
         o_mamba[k : k + 1, :] = value[4:5, k * LANES : (k + 1) * LANES]
-    for k, (a, b) in enumerate(zip(held, passed_outs)):
-        loads[5 + k].wait()
-        stores.append(pltpu.make_async_copy(a, b, sem_out.at[count + k]))
-        stores[-1].start()
     for copy in stores:
         copy.wait()
 

time: 224 us -> 223 us (level)
  no operation moved by 1% of the time
where the time goes in v7:
time: 223 us
  Pallas kernels  220 us (99%)
    pallas_call x1, Pallas kernels, mixer_back(): pl.pallas_call(functools.partial(mixer_back_kernel, merged, chunks), out_...  142 us
    pallas_call x1, Pallas kernels, feed_layer(): pl.pallas_call(functools.partial(moving, functools.partial(feed_kernel, m...  42.7 us
    pallas_call x1, Pallas kernels, mixer_forward(): pl.pallas_call(functools.partial(moving, mixer_kernel, 15, 12, len(out_sh...  28.5 us
    pallas_call x1, Pallas kernels, finish_outputs(): pl.pallas_call(functools.partial(finish_kernel, sizes, len(big)), out_sha...  6.78 us

profile of v7, /device:TPU:0, one launch (start us, length us, event | category | flops | bytes accessed | tf_op | source)
XLA Modules:
  0.0 222.8 jit_solution(889803055339554147)
XLA Ops:
  0.7 1.0 multiply_cosine_fusion
  1.7 0.8 pad_maximum_fusion.refs_3_
  2.5 28.5 %mixer_forward.1 = (f32[512,768]{1,0:T(8,128)}, f32[520,1024]{1,0:T(8,128)}, f32[512,1024]{1,0:T(8,128)}, f32[512,128]{1,0:T(8,128)}, f32[512,128]{1,0:T(8,128)}...) custom-call(bf16[512,1024]{1,0:T(8,128)(2,1)} %bitcast.21, ...), custom_call_target="tpu_custom_call" | custom-call | tf_op jit(solution)/shard_map/mixer_forward/pallas_call | solution.py:1300
  31.0 42.7 %feed_layer.1 = (bf16[512,1024]{1,0:T(8,128)(2,1)}, f32[512,1024]{1,0:T(8,128)}, f32[512,768]{1,0:T(8,128)}, bf16[512,768]{1,0:T(8,128)(2,1)}, f32[512,256]{1,0:...) custom-call(f32[512,768]{1,0:T(8,128)} %get-tuple-element.89.refs_0_, ...), custom_call_target="tpu_custom_call" | custom-call | tf_op jit(solution)/shard_map/feed_layer/pallas_call | solution.py:765
  73.7 142.1 %mixer_back.1 = (f32[512,1024]{1,0:T(8,128)}, bf16[2,2,64,1024]{3,2,1,0:T(8,128)(2,1)}, bf16[2,2,64,2048]{3,2,1,0:T(8,128)(2,1)}, bf16[2,2,64,1024]{3,2,1,0:T(8,...) custom-call(bf16[512,1024]{1,0:T(8,128)(2,1)} %bitcast.23, ...), custom_call_target="tpu_custom_call" | custom-call | tf_op jit(solution)/shard_map/mixer_back/pallas_call | solution.py:2110
  215.8 6.8 %finish_outputs.1 = (f32[256,1024]{1,0:T(8,128)}, f32[256,1024]{1,0:T(8,128)}, f32[256,1024]{1,0:T(8,128)}, f32[256,768]{1,0:T(8,128)}, f32[256,256]{1,0:T(8,128...) custom-call(bf16[256,1024]{1,0:T(8,128)(2,1)} %bitcast.28, ...), custom_call_target="tpu_custom_call" | custom-call | tf_op jit(solution)/shard_map/finish_outputs/pallas_call | solution.py:2216
  (2 shorter events, 0.0 us)
